TPU v7x, 32 devices: a whole 2x2x4 slice. The times are simulated.
32 devices in a mesh: row: 4 (over z), col: 8 (over y, x, core).
Axes of the slice: x: 2, y: 2, z: 4, core: 2. Of those that a mesh axis runs over, the one named last changes fastest.
Arguments:
- lam_tiles: bfloat16 [32, 64, 16, 128], P(('row', 'col')), may hold values from -6 to 6
- lam_ids: int32 [32, 64], P(('row', 'col')), may hold values from 0 to 255, as said below
- integrals: bfloat16 [4096, 32768], P('row', 'col'), may hold values from -0.125 to 0.125
Outputs:
- ladder: float32 [512, 4096], P('col', 'row')
Inputs may be any that keep to these rules, and one draw needn't show every extreme that they name: `lam_ids`: within a group the 64 ids are distinct; at most 16 of them lie in one block of 32 consecutive ids, and every group has exactly 16 in one block, the same block for all groups.
All inputs are finite; a program needn't handle non-finite values.
Results may differ from a plain program's by a relative error of at most 0.0003.
Values may be sent and summed in bfloat16 or wider, within the bound.
No kernel may reach another device: no remote copies, remote signals or barrier semaphores. Data moves between devices by JAX's collectives and lax.ppermute only.
A program may use at most 128 MiB of HBM per device.

v0:
```python
import jax
import jax.numpy as jnp
from jax import lax
from jax.sharding import PartitionSpec as P

CAP = 16


def bucket_tiles(tiles, labels, target, n_dest, slots):
    onehot = (target[:, None] == jnp.arange(n_dest, dtype=jnp.int32)[None, :]).astype(jnp.int32)
    before = jnp.cumsum(onehot, axis=0) - onehot
    place = jnp.sum(before * onehot, axis=1)
    buffer = jnp.zeros((n_dest, slots) + tiles.shape[1:], tiles.dtype)
    buffer = buffer.at[target, place].set(tiles)
    marks = jnp.full((n_dest, slots), -1, jnp.int32).at[target, place].set(labels)
    return (buffer, marks)


def place_tiles(tiles, index, width):
    selector = (index[:, :, None] == jnp.arange(width, dtype=jnp.int32)[None, None, :]).astype(
        tiles.dtype
    )
    return jnp.einsum("nsw,nspt->nwpt", selector, tiles, preferred_element_type=jnp.bfloat16)


def shards(lam_tiles, lam_ids, integrals):
    n_row = lax.axis_size("row")
    n_col = lax.axis_size("col")
    g_dev, s_count, pairs, tile = lam_tiles.shape
    ab_dev = integrals.shape[0]
    kt_dev = integrals.shape[1] // tile
    groups = g_dev * n_row * n_col
    first = (lax.axis_index("row") * n_col + lax.axis_index("col")) * g_dev
    owned = first + lax.broadcasted_iota(jnp.int32, (g_dev, s_count), 0)
    labels = owned * kt_dev + lam_ids % kt_dev
    target = lam_ids // kt_dev
    buffer, marks = bucket_tiles(
        lam_tiles.reshape(-1, pairs, tile),
        labels.reshape(-1),
        target.reshape(-1),
        n_col,
        g_dev * CAP,
    )
    got_tiles, got_marks = (
        lax.all_to_all(buffer, "col", split_axis=0, concat_axis=0, tiled=True),
        lax.all_to_all(marks, "col", split_axis=0, concat_axis=0, tiled=True),
    )
    piece_tiles = lax.all_gather(got_tiles[None], "row", axis=0, tiled=True)
    piece_marks = lax.all_gather(got_marks[None], "row", axis=0, tiled=True)
    sources = piece_marks.shape[0] * piece_marks.shape[1]
    flat_marks = piece_marks.reshape(sources, piece_marks.shape[2])
    flat_tiles = piece_tiles.reshape((sources,) + piece_tiles.shape[2:])
    source = lax.broadcasted_iota(jnp.int32, flat_marks.shape, 0)
    index = jnp.where(flat_marks >= 0, flat_marks - source * (g_dev * kt_dev), -1)
    built = place_tiles(flat_tiles, index, g_dev * kt_dev)
    columns = integrals.reshape(ab_dev, kt_dev, tile)
    product = jnp.einsum("gkpt,akt->gpa", built, columns, preferred_element_type=jnp.float32)
    return lax.psum_scatter(
        0.5 * product.reshape(groups * pairs // n_col * lax.axis_size("col"), ab_dev),
        "col",
        scatter_dimension=0,
        tiled=True,
    )


def solution(mesh):
    return jax.shard_map(
        shards,
        mesh=mesh,
        in_specs=(P(("row", "col"), None, None, None), P(("row", "col"), None), P("row", "col")),
        out_specs=P("col", "row"),
        check_vma=False,
    )
```

profile of v0, /device:TPU:0, one launch (start us, length us, event | category | flops | bytes accessed | tf_op | source)
XLA Modules:
  0.0 132.9 jit_solution(9944941024033586606)
XLA Ops:
  6.5 0.0 all-gather.4.cloned.1.call-start
  6.5 0.7 fusion.16
  7.2 0.1 fusion.13
  7.3 0.1 reduce_window_sum.11
  7.4 0.2 select_reduce_fusion
  7.6 0.1 broadcast_in_dim.26
  7.7 4.7 %scatter_fusion.1 = bf16[8,16,16,128]{3,2,1,0:T(8,128)(2,1)S(1)} fusion(bf16[8,16,16,128]{3,2,1,0:T(8,128)(2,1)S(1)} %broadcast_in_dim.26, s32[64]{0:T(128)S(1)} %fusion.17, bf16[64,16,128]{2,1,0:T(8,128)(2,1)} %bitcast.40), kind=kCustom, calls=%fused_computation.1 | custom fusion | bytes 786944 | tf_op jit(solution)/shard_map/scatter | solution.py:14
  12.3 14.8 %all_to_all.14 = bf16[8,16,16,128]{3,2,1,0:T(8,128)(2,1)} all-to-all(bf16[8,16,16,128]{3,2,1,0:T(8,128)(2,1)S(1)} %scatter_fusion.1), channel_id=1, replica_groups=mesh['row'=4,'col'=8] {'col'}, dimensions={0} | all-to-all | bytes 1048576 | tf_op jit(solution)/shard_map/all_to_all | solution.py:45
  27.1 0.0 all-gather.4.cloned.1.call-update
  27.2 0.6 broadcast_in_dim.12
  27.8 10.2 %scatter_fusion = s32[8,16]{1,0:T(8,128)} fusion(s32[8,16]{1,0:T(8,128)} %broadcast_in_dim.12, s32[64]{0:T(128)S(1)} %fusion.17, s32[64]{0:T(128)S(1)} %get-tuple-element.5), kind=kCustom, calls=%fused_computation | custom fusion | bytes 1280 | tf_op jit(solution)/shard_map/scatter | solution.py:15
  38.0 3.3 %all-to-all-start = ((s32[8,1,16]{2,1,0:T(1,128)}), s32[8,1,16]{2,1,0:T(1,128)S(1)}, u32[]{:S(2)}, u32[]{:S(2)}) async-start(s32[8,1,16]{2,1,0:T(1,128)} %bitcast.6), calls=%async_computation | async-start | bytes 8192 | tf_op jit(solution)/shard_map/all_to_all | solution.py:46
  41.3 0.0 reduce-scatter.2.cloned.1.call-start
  41.3 4.5 %all-to-all-done = s32[8,1,16]{2,1,0:T(1,128)S(1)} async-done(((s32[8,1,16]{2,1,0:T(1,128)}), s32[8,1,16]{2,1,0:T(1,128)S(1)}, u32[]{:S(2)}, u32[]{:S(2)}) %all-to-all-start) | async-done | bytes 544 | tf_op jit(solution)/shard_map/all_to_all | solution.py:46
  45.8 13.4 %all-gather = s32[32,1,16]{2,1,0:T(1,128)S(1)} all-gather(s32[8,1,16]{2,1,0:T(1,128)S(1)} %all-to-all-done), channel_id=2, replica_groups=mesh['row'=4,'col'=8] {'row'}, dimensions={0}, use_global_device_ids=true | all-gather | bytes 2560 | tf_op jit(solution)/shard_map/all_gather | solution.py:49
  59.2 0.1 subtract_select_fusion
  59.3 13.6 %all-gather.4.cloned.1.call-done = bf16[32,16,16,128]{3,2,1,0:T(8,128)(2,1)} async-done(((bf16[8,16,16,128]{3,2,1,0:T(8,128)(2,1)}), bf16[32,16,16,128]{3,2,1,0:T(8,128)(2,1)}) %all-gather.4.cloned.1.call-update) | async-done | bytes 2097168 | tf_op jit(solution)/shard_map/all_gather | solution.py:48
  72.9 3.6 %fusion.4 = bf16[32,32,16,128]{3,1,2,0:T(8,128)(2,1)S(1)} fusion(bf16[32,16,16,128]{3,2,1,0:T(8,128)(2,1)} %all-gather.4.cloned.1.call-done, s32[32,16]{1,0:T(8,128)S(1)} %subtract_select_fusion), kind=kOutput, calls=%fused_computation.7 | convolution fusion | flops 67125248 | bytes 6293504 | tf_op jit(solution)/shard_map/nsw,nspt->nwpt/dot_general | solution.py:23
  76.4 9.5 %bitcast_multiply_fusion = f32[512,1024]{1,0:T(8,128)} fusion(bf16[512,32,128]{2,1,0:T(8,128)(2,1)S(1)} %bitcast.39, bf16[1024,4096]{1,0:T(8,128)(2,1)} %param.5), kind=kOutput, calls=%fused_computation.6 | convolution fusion | flops 4295491584 | bytes 14680064 | tf_op jit(solution)/shard_map/gkpt,akt->gpa/dot_general | solution.py:57
  85.9 0.0 reduce-scatter.2.cloned.1.call-update
  85.9 40.1 %reduce-scatter.2.cloned.1.call-done = f32[64,1024]{1,0:T(8,128)} async-done(((f32[512,1024]{1,0:T(8,128)}), f32[64,1024]{1,0:T(8,128)}) %reduce-scatter.2.cloned.1.call-update) | async-done | bytes 262160 | tf_op jit(solution)/shard_map/reduce_scatter | solution.py:58
  (2 shorter events, 0.0 us)
Async XLA Ops:
  6.5 66.3 %all-gather.4.cloned.1.call-start = ((), (), s32[]{:S(2)}) async-start(), calls=%async_computation.4 | async-start | bytes 2621440 | tf_op jit(solution)/shard_map/all_gather | solution.py:48
  38.0 7.8 %all-to-all-start = ((s32[8,1,16]{2,1,0:T(1,128)}), s32[8,1,16]{2,1,0:T(1,128)S(1)}, u32[]{:S(2)}, u32[]{:S(2)}) async-start(s32[8,1,16]{2,1,0:T(1,128)} %bitcast.6), calls=%async_computation | async-start | bytes 8192 | tf_op jit(solution)/shard_map/all_to_all | solution.py:46
  41.3 84.8 %reduce-scatter.2.cloned.1.call-start = ((), (), s32[]{:S(2)}) async-start(), calls=%async_computation.3 | async-start | bytes 2359296 | tf_op jit(solution)/shard_map/reduce_scatter | solution.py:58
Sparse Core Ops, SparseCore 0:
  27.3 45.5 all-gather.3
  86.1 39.9 reduce-scatter.1
where the time goes:
time: 134 us; the launch traced here: 133 us
  waiting for transfers between devices  58.1 us (43%)
  blocking collectives  28.2 us (21%)
  local copies, waits for them, and re-layouts  15.5 us (12%)
  between operations  13.5 us (10%)
  matrix products  13 us (10%)
  starting transfers between devices  3.35 us (2%)
    reduce_scatter x1, waiting for transfers between devices, shards(): lax.psum_scatter(0.5 * product.reshape(groups * pairs // n_col * lax.axis...  40.1 us
    all_to_all x1, blocking collectives, shards(): lax.all_to_all(buffer, 'col', split_axis=0, concat_axis=0, tiled=True)  14.8 us
    all_gather x1, waiting for transfers between devices, shards(): piece_tiles = lax.all_gather(got_tiles[None], 'row', axis=0, tiled=True)  13.6 us
    all_gather x1, blocking collectives, shards(): piece_marks = lax.all_gather(got_marks[None], 'row', axis=0, tiled=True)  13.4 us
    scatter x1, local copies, waits for them, and re-layouts, bucket_tiles(): jnp.full((n_dest, slots), -1, jnp.int32).at[target, place].set(labels)  10.2 us
    dot_general x1, matrix products, shards(): jnp.einsum('gkpt,akt->gpa', built, columns, preferred_element_type=jnp.fl...  9.48 us
    scatter x1, local copies, waits for them, and re-layouts, bucket_tiles(): buffer = buffer.at[target, place].set(tiles)  4.66 us
    all_to_all x1, waiting for transfers between devices, shards(): lax.all_to_all(marks, 'col', split_axis=0, concat_axis=0, tiled=True)  4.45 us
  transfers between devices with their start and end apart: 3, of which 3 were waited for; matrix products, arithmetic and copies ran while one was open for 8% of the time, Pallas kernels for 0%

commit v1 on v0

v1 whole, which is shorter than its diff:
```python
import functools

import jax
import jax.numpy as jnp
from jax import lax
from jax.experimental import pallas as pl
from jax.experimental.pallas import tpu as pltpu
from jax.sharding import PartitionSpec as P

CAP = 16

VMEM = pl.BlockSpec(memory_space=pltpu.VMEM)
SMEM = pl.BlockSpec(memory_space=pltpu.SMEM)
ANY = pl.BlockSpec(memory_space=pl.ANY)


def shift_of(size):
    assert size & (size - 1) == 0
    return size.bit_length() - 1


class Plan:
    def __init__(self, lam_tiles, integrals):
        self.n_row = lax.axis_size("row")
        self.n_col = lax.axis_size("col")
        g_dev, self.slots, self.pairs, self.tile = lam_tiles.shape
        assert g_dev == 1 and self.pairs == 16 and self.slots <= self.tile
        self.ab, self.cd = integrals.shape
        self.kt = self.cd // self.tile
        self.n_pair = self.n_col // 2
        self.per_row = self.n_col // self.n_row
        assert self.per_row % 2 == 0
        self.owned = self.n_col * self.pairs // self.per_row
        self.bucket = (CAP + 1) * self.pairs
        self.head = -(-(self.n_col + 1) // 16) * 16
        self.packed = self.slots * self.pairs + self.head


def pack_kernel(plan, ids, me, tiles, packed, *rest):
    outs, (buf, head, count, sem) = rest[: plan.n_pair], rest[plan.n_pair :]
    rows = plan.pairs
    body = pltpu.make_async_copy(tiles, packed.at[pl.ds(0, plan.slots * rows)], sem.at[0])
    body.start()
    head[...] = jnp.full(head.shape, plan.kt, jnp.int32)
    for m in range(plan.n_col):
        count[m] = 0
    lane = lax.broadcasted_iota(jnp.int32, (1, plan.tile), 1)
    col = me[1]

    def step(s, slot_row):
        tile_id = ids[0, s]
        m = (tile_id >> shift_of(plan.kt)) ^ col
        place = count[m]
        count[m] = place + 1
        at = pl.multiple_of(m * plan.bucket + place * rows, rows)
        buf[pl.ds(at, rows), :] = tiles[pl.ds(pl.multiple_of(s * rows, rows), rows), :]
        line = head[pl.ds(m, 1), :]
        head[pl.ds(m, 1), :] = jnp.where(lane == place, tile_id & (plan.kt - 1), line)
        return jnp.where(lane == s, m * CAP + place, slot_row)

    slot_row = lax.fori_loop(0, plan.slots, step, jnp.zeros((1, plan.tile), jnp.int32), unroll=8)
    head[plan.n_col : plan.n_col + 1, :] = slot_row
    heads = head[...].astype(jnp.float32)
    spread_heads(plan, heads, buf)
    copies = [body]
    top = buf.at[pl.ds(plan.n_col * plan.bucket, plan.head)]
    top[...] = heads.astype(jnp.bfloat16)
    copies.append(pltpu.make_async_copy(top, packed.at[pl.ds(plan.slots * rows, plan.head)], sem.at[1]))
    copies[-1].start()
    for i, out in enumerate(outs):
        part = buf.at[pl.ds(i * 2 * plan.bucket, 2 * plan.bucket)]
        copies.append(pltpu.make_async_copy(part, out, sem.at[2 + i]))
        copies[-1].start()
    for copy in copies:
        copy.wait()


def spread_heads(plan, heads, buf):
    for m in range(plan.n_col):
        line = jnp.broadcast_to(heads[m : m + 1, :], (plan.pairs, plan.tile))
        at = m * plan.bucket + CAP * plan.pairs
        buf[at : at + plan.pairs, :] = line.astype(jnp.bfloat16)


def pack(plan, ids, me, tiles):
    bf16 = jnp.bfloat16
    return pl.pallas_call(
        functools.partial(pack_kernel, plan),
        out_shape=[jax.ShapeDtypeStruct((plan.packed, plan.tile), bf16)]
        + [jax.ShapeDtypeStruct((2 * plan.bucket, plan.tile), bf16)] * plan.n_pair,
        in_specs=[SMEM, SMEM, VMEM],
        out_specs=[ANY] * (1 + plan.n_pair),
        scratch_shapes=[
            pltpu.VMEM((plan.n_col * plan.bucket + plan.head, plan.tile), bf16),
            pltpu.VMEM((plan.head, plan.tile), jnp.int32),
            pltpu.SMEM((plan.n_col,), jnp.int32),
            pltpu.SemaphoreType.DMA((2 + plan.n_pair,)),
        ],
        name="pack_tiles",
    )(ids, me, tiles)


def bucket_kernel(plan, packed, *rest):
    outs, (buf, line, places, sem) = rest[: plan.n_pair], rest[plan.n_pair :]
    rows = plan.pairs
    heads = packed[plan.slots * rows :, :].astype(jnp.float32)
    line[...] = jnp.broadcast_to(heads[plan.n_col : plan.n_col + 1, :], line.shape).astype(jnp.int32)
    copy = pltpu.make_async_copy(line, places, sem.at[0])
    copy.start()
    spread_heads(plan, heads, buf)
    copy.wait()

    def step(s, _):
        place = places[0, s]
        at = pl.multiple_of((place + (place >> shift_of(CAP))) * rows, rows)
        buf[pl.ds(at, rows), :] = packed[pl.ds(pl.multiple_of(s * rows, rows), rows), :]
        return 0

    lax.fori_loop(0, plan.slots, step, 0, unroll=8)
    copies = []
    for i, out in enumerate(outs):
        part = buf.at[pl.ds(i * 2 * plan.bucket, 2 * plan.bucket)]
        copies.append(pltpu.make_async_copy(part, out, sem.at[1 + i]))
        copies[-1].start()
    for copy in copies:
        copy.wait()


def bucket(plan, packed):
    bf16 = jnp.bfloat16
    return pl.pallas_call(
        functools.partial(bucket_kernel, plan),
        out_shape=[jax.ShapeDtypeStruct((2 * plan.bucket, plan.tile), bf16)] * plan.n_pair,
        in_specs=[VMEM],
        out_specs=[ANY] * plan.n_pair,
        scratch_shapes=[
            pltpu.VMEM((plan.n_col * plan.bucket, plan.tile), bf16),
            pltpu.VMEM((8, plan.tile), jnp.int32),
            pltpu.SMEM((8, plan.tile), jnp.int32),
            pltpu.SemaphoreType.DMA((1 + plan.n_pair,)),
        ],
        name="bucket_tiles",
    )(packed)


def build_kernel(plan, me, *rest):
    near, far, out, line, places, sem = rest[: plan.n_pair], *rest[plan.n_pair :]
    rows = plan.pairs
    sources = [(ref, 0, 2 * i) for i, ref in enumerate(near)]
    sources += [(far, i * plan.bucket, 2 * i + 1) for i in range(plan.n_pair)]
    for i, (ref, base, _) in enumerate(sources):
        at = base + CAP * rows
        line[i : i + 1, :] = ref[at : at + rows, :].astype(jnp.float32)[0:1, :].astype(jnp.int32)
    copy = pltpu.make_async_copy(line, places, sem)
    copy.start()
    out[...] = jnp.zeros(out.shape, out.dtype)
    copy.wait()
    col = me[1]
    for i, (ref, base, m) in enumerate(sources):
        to = pl.multiple_of((col ^ m) * rows, rows)
        for s in range(CAP):
            at = pl.multiple_of(places[i, s] * plan.tile, plan.tile)
            tile = ref[base + s * rows : base + (s + 1) * rows, :]
            out[pl.ds(to, rows), pl.ds(at, plan.tile)] = tile


def build(plan, me, near, far):
    first = pl.BlockSpec((plan.bucket, plan.tile), lambda i: (0, 0))
    whole = pl.BlockSpec(far.shape, lambda i: (0, 0))
    shape = (plan.n_col * plan.pairs, plan.cd + plan.tile)
    return pl.pallas_call(
        functools.partial(build_kernel, plan),
        out_shape=jax.ShapeDtypeStruct(shape, jnp.bfloat16),
        grid=(1,),
        in_specs=[SMEM] + [first] * plan.n_pair + [whole],
        out_specs=pl.BlockSpec(shape, lambda i: (0, 0)),
        scratch_shapes=[
            pltpu.VMEM((plan.n_col, plan.tile), jnp.int32),
            pltpu.SMEM((plan.n_col, plan.tile), jnp.int32),
            pltpu.SemaphoreType.DMA,
        ],
        name="build_rows",
    )(me, *near, far)


def product_kernel(plan, me, *rest):
    planes, (cols, keep, send, lam, total) = rest[: plan.n_row], rest[plan.n_row :]
    height = plan.n_col * plan.pairs

    @pl.when(pl.program_id(0) == 0)
    def _():
        for d, plane in enumerate(planes):
            lam[d * height : (d + 1) * height, :] = plane[...]

    total[...] = lax.dot_general(
        lam[...], cols[...], (((1,), (1,)), ((), ())), preferred_element_type=jnp.float32
    )
    row, col = me[0], me[1]
    core = col & 1
    for d in range(plan.n_row):
        for h in range(0, plan.per_row, 2):
            to = ((((row ^ d) * plan.per_row + h) ^ col) >> 1) * plan.owned
            to = pl.multiple_of(to, plan.owned)
            for out, side in ((keep, core), (send, 1 - core)):
                at = pl.multiple_of(d * height + (h + side) * plan.owned, plan.owned)
                out[pl.ds(to, plan.owned), :] = total[pl.ds(at, plan.owned), :]


def product(plan, me, planes, integrals, block=256):
    height = plan.n_col * plan.pairs
    half = plan.n_pair * plan.owned
    return pl.pallas_call(
        functools.partial(product_kernel, plan),
        out_shape=[jax.ShapeDtypeStruct((half, plan.ab), jnp.float32)] * 2,
        grid=(plan.ab // block,),
        in_specs=[SMEM]
        + [pl.BlockSpec((height, plan.cd), lambda i: (0, 0))] * plan.n_row
        + [pl.BlockSpec((block, plan.cd), lambda i: (i, 0))],
        out_specs=[pl.BlockSpec((half, block), lambda i: (0, i))] * 2,
        scratch_shapes=[
            pltpu.VMEM((plan.n_row * height, plan.cd), jnp.bfloat16),
            pltpu.VMEM((plan.n_row * height, block), jnp.float32),
        ],
        compiler_params=pltpu.CompilerParams(vmem_limit_bytes=56 * 1024 * 1024),
        name="product",
    )(me, *planes, integrals)


def swap(x, axis, m):
    return lax.ppermute(x, axis, [(i, i ^ m) for i in range(lax.axis_size(axis))])


def shards(lam_tiles, lam_ids, integrals):
    plan = Plan(lam_tiles, integrals)
    me = jnp.stack([lax.axis_index("row"), lax.axis_index("col")]).astype(jnp.int32)
    tiles = lam_tiles.reshape(plan.slots * plan.pairs, plan.tile)
    packed, *own = pack(plan, lam_ids, me, tiles)
    arrived = [swap(packed, "row", d) for d in range(1, plan.n_row)]
    planes = []
    for d in range(plan.n_row):
        parts = own if d == 0 else bucket(plan, arrived[d - 1])
        near = [parts[0]] + [swap(parts[m], "col", 2 * m) for m in range(1, plan.n_pair)]
        far = jnp.concatenate([part[plan.bucket :] for part in near], axis=0)
        planes.append(build(plan, me, near, swap(far, "col", 1)))
    keep, send = product(plan, me, planes, integrals)
    got = swap(send, "col", 1)
    both = [
        keep[m * plan.owned : (m + 1) * plan.owned] + got[m * plan.owned : (m + 1) * plan.owned]
        for m in range(plan.n_pair)
    ]
    out = both[0]
    for m in range(1, plan.n_pair):
        out = out + swap(both[m], "col", 2 * m)
    return 0.5 * out


def solution(mesh):
    return jax.shard_map(
        shards,
        mesh=mesh,
        in_specs=(P(("row", "col"), None, None, None), P(("row", "col"), None), P("row", "col")),
        out_specs=P("col", "row"),
        check_vma=False,
    )
```

time: 134 us -> 101 us (0.75)
  Pallas kernels: 0 us -> 32.2 us
  blocking collectives: 28.2 us -> 0 us
  waiting for transfers between devices: 58.1 us -> 31.2 us
  starting transfers between devices: 3.35 us -> 24.6 us
  between operations: 13.5 us -> 0.42 us
  matrix products: 13 us -> 0 us
  local copies, waits for them, and re-layouts: 15.5 us -> 7.91 us
  other arithmetic: 1.1 us -> 3.7 us
    reduce_scatter x1 -> x0, waiting for transfers between devices: 40.1 us -> none  [shards(): lax.psum_scatter(0.5 * product.reshape(groups * pairs // n_col * lax.axis...]
    pallas_call x0 -> x9, Pallas kernels: none -> 32.2 us  [the longest x4 12.1 us: build(): pl.pallas_call(functools.partial(build_kernel, plan), out_shape=jax.Shape...]
    ppermute x0 -> x23, waiting for transfers between devices: none -> 31.2 us  [swap(): lax.ppermute(x, axis, [(i, i ^ m) for i in range(lax.axis_size(axis))])]
    ppermute x0 -> x23, starting transfers between devices: none -> 24.6 us  [swap(): lax.ppermute(x, axis, [(i, i ^ m) for i in range(lax.axis_size(axis))])]
    scatter x2 -> x0, local copies, waits for them, and re-layouts: 14.9 us -> none  [the longest x1 10.2 us: bucket_tiles(): jnp.full((n_dest, slots), -1, jnp.int32).at[target, place].set(labels)]
    all_to_all x1 -> x0, blocking collectives: 14.8 us -> none  [shards(): lax.all_to_all(buffer, 'col', split_axis=0, concat_axis=0, tiled=True)]
    all_gather x1 -> x0, waiting for transfers between devices: 13.6 us -> none  [shards(): piece_tiles = lax.all_gather(got_tiles[None], 'row', axis=0, tiled=True)]
    all_gather x1 -> x0, blocking collectives: 13.4 us -> none  [shards(): piece_marks = lax.all_gather(got_marks[None], 'row', axis=0, tiled=True)]
  transfers between devices with their start and end apart: 3 -> 23, of which waited for: 3 -> 11; matrix products, arithmetic and copies ran while one was open for 8% -> 4% of each run, Pallas kernels for 0% -> 17%
where the time goes in v1:
time: 101 us; the launch traced here: 100 us
  Pallas kernels  32.2 us (32%)
  waiting for transfers between devices  31.2 us (31%)
  starting transfers between devices  24.6 us (24%)
  local copies, waits for them, and re-layouts  7.91 us (8%)
  other arithmetic  3.7 us (4%)
    ppermute x23, waiting for transfers between devices, swap(): lax.ppermute(x, axis, [(i, i ^ m) for i in range(lax.axis_size(axis))])  31.2 us
    ppermute x23, starting transfers between devices, swap(): lax.ppermute(x, axis, [(i, i ^ m) for i in range(lax.axis_size(axis))])  24.6 us
    pallas_call x4, Pallas kernels, build(): pl.pallas_call(functools.partial(build_kernel, plan), out_shape=jax.Shape...  12.1 us
    pallas_call x1, Pallas kernels, product(): pl.pallas_call(functools.partial(product_kernel, plan), out_shape=[jax.Sh...  9.85 us
    pallas_call x3, Pallas kernels, bucket(): pl.pallas_call(functools.partial(bucket_kernel, plan), out_shape=[jax.Sha...  7.99 us
    unnamed x40, local copies, waits for them, and re-layouts  4.28 us
    slice x16, local copies, waits for them, and re-layouts, shards(): far = jnp.concatenate([part[plan.bucket:] for part in near], axis=0)  3.63 us
    pallas_call x1, Pallas kernels, pack(): pl.pallas_call(functools.partial(pack_kernel, plan), out_shape=[jax.Shape...  2.23 us
  transfers between devices with their start and end apart: 23, of which 11 were waited for; matrix products, arithmetic and copies ran while one was open for 4% of the time, Pallas kernels for 17%

profile of v1, /device:TPU:0, one launch (start us, length us, event | category | flops | bytes accessed | tf_op | source)
XLA Modules:
  0.0 100.1 jit_solution(17405527518604193750)
XLA Ops:
  0.0 0.6 pad_add_fusion.me
  0.6 2.2 %pack_tiles.1 = (bf16[1040,128]{1,0:T(8,128)(2,1)}, bf16[544,128]{1,0:T(8,128)(2,1)}, bf16[544,128]{1,0:T(8,128)(2,1)}, bf16[544,128]{1,0:T(8,128)(2,1)}, bf16[544,128]{1,0:T(8,128)(2,1)}) custom-call(s32[1,64]{1,0:T(1,128)} %ids.1, s32[2]{0:T(128)} %pad_add_fusion.me, bf16[1024,128]{1,0:T(8,128)(2,1)} %bitcast.3), custom_call_target="tpu_custom_call" | custom-call | tf_op jit(solution)/shard_map/pack_tiles/pallas_call | solution.py:87
  2.9 3.0 %collective-permute-start = (bf16[544,128]{1,0:T(8,128)(2,1)}, bf16[544,128]{1,0:T(8,128)(2,1)S(1)}, u32[]{:S(2)}, u32[]{:S(2)}) collective-permute-start(bf16[544,128]{1,0:T(8,128)(2,1)} %get-tuple-element.25), channel_id=1, source_target_pairs={{0,2},{1,3},{2,0},{3,1},{4,6},{5,7},{6,4},{7,5},{8,10},{9,11},{10,... | collective-permute-start | bytes 417800 | tf_op jit(solution)/shard_map/ppermute | solution.py:230
  5.9 1.6 %collective-permute-start.4 = (bf16[1040,128]{1,0:T(8,128)(2,1)}, bf16[1040,128]{1,0:T(8,128)(2,1)S(1)}, u32[]{:S(2)}, u32[]{:S(2)}) collective-permute-start(bf16[1040,128]{1,0:T(8,128)(2,1)} %get-tuple-element.28), channel_id=1, source_target_pairs={{0,8},{8,0},{16,24},{24,16},{1,9},{9,1},{17,25},{25,17},{2,10},{10... | collective-permute-start | bytes 798728 | tf_op jit(solution)/shard_map/ppermute | solution.py:230
  7.5 2.6 %collective-permute-start.9 = (bf16[1040,128]{1,0:T(8,128)(2,1)}, bf16[1040,128]{1,0:T(8,128)(2,1)S(1)}, u32[]{:S(2)}, u32[]{:S(2)}) collective-permute-start(bf16[1040,128]{1,0:T(8,128)(2,1)} %get-tuple-element.28), channel_id=1, source_target_pairs={{0,16},{8,24},{16,0},{24,8},{1,17},{9,25},{17,1},{25,9},{2,18},{10... | collective-permute-start | bytes 798728 | tf_op jit(solution)/shard_map/ppermute | solution.py:230
  10.1 0.2 collective-permute-start.14
  10.3 1.5 %collective-permute-start.1 = (bf16[544,128]{1,0:T(8,128)(2,1)}, bf16[544,128]{1,0:T(8,128)(2,1)S(1)}, u32[]{:S(2)}, u32[]{:S(2)}) collective-permute-start(bf16[544,128]{1,0:T(8,128)(2,1)} %get-tuple-element.26), channel_id=1, source_target_pairs={{0,4},{1,5},{2,6},{3,7},{4,0},{5,1},{6,2},{7,3},{8,12},{9,13},{10,... | collective-permute-start | bytes 417800 | tf_op jit(solution)/shard_map/ppermute | solution.py:230
  11.8 0.0 collective-permute-done.rest_1_
  11.8 0.7 collective-permute-start.2
  12.5 0.9 slice.72
  13.4 5.1 %collective-permute-done.1.rest_2_ = bf16[544,128]{1,0:T(8,128)(2,1)S(1)} collective-permute-done((bf16[544,128]{1,0:T(8,128)(2,1)}, bf16[544,128]{1,0:T(8,128)(2,1)S(1)}, u32[]{:S(2)}, u32[]{:S(2)}) %collective-permute-start.1) | collective-permute-done | bytes 139296 | tf_op jit(solution)/shard_map/ppermute | solution.py:230
  18.5 0.0 collective-permute-done.2.rest_3_
  18.5 0.2 collective-permute-done.4.packed
  18.8 0.7 copy-done.18
  19.5 2.7 %bucket_tiles.3 = (bf16[544,128]{1,0:T(8,128)(2,1)}, bf16[544,128]{1,0:T(8,128)(2,1)}, bf16[544,128]{1,0:T(8,128)(2,1)}, bf16[544,128]{1,0:T(8,128)(2,1)}) custom-call(bf16[1040,128]{1,0:T(8,128)(2,1)} %copy-done.18), custom_call_target="tpu_custom_call" | custom-call | tf_op jit(solution)/shard_map/bucket_tiles/pallas_call | solution.py:131
  22.1 0.4 collective-permute-start.5
  22.6 1.7 %collective-permute-start.6 = (bf16[544,128]{1,0:T(8,128)(2,1)}, bf16[544,128]{1,0:T(8,128)(2,1)S(1)}, u32[]{:S(2)}, u32[]{:S(2)}) collective-permute-start(bf16[544,128]{1,0:T(8,128)(2,1)} %get-tuple-element.31), channel_id=1, source_target_pairs={{0,4},{1,5},{2,6},{3,7},{4,0},{5,1},{6,2},{7,3},{8,12},{9,13},{10,... | collective-permute-start | bytes 417800 | tf_op jit(solution)/shard_map/ppermute | solution.py:230
  24.3 1.4 %collective-permute-start.7 = (bf16[544,128]{1,0:T(8,128)(2,1)}, bf16[544,128]{1,0:T(8,128)(2,1)S(1)}, u32[]{:S(2)}, u32[]{:S(2)}) collective-permute-start(bf16[544,128]{1,0:T(8,128)(2,1)} %get-tuple-element.32), channel_id=1, source_target_pairs={{0,6},{1,7},{2,4},{3,5},{4,2},{5,3},{6,0},{7,1},{8,14},{9,15},{10,... | collective-permute-start | bytes 417800 | tf_op jit(solution)/shard_map/ppermute | solution.py:230
  25.7 3.6 %collective-permute-done.9.packed = bf16[1040,128]{1,0:T(8,128)(2,1)S(1)} collective-permute-done((bf16[1040,128]{1,0:T(8,128)(2,1)}, bf16[1040,128]{1,0:T(8,128)(2,1)S(1)}, u32[]{:S(2)}, u32[]{:S(2)}) %collective-permute-start.9) | collective-permute-done | bytes 266272 | tf_op jit(solution)/shard_map/ppermute | solution.py:230
  29.3 0.7 copy-done.17
  30.0 2.7 %bucket_tiles.4 = (bf16[544,128]{1,0:T(8,128)(2,1)}, bf16[544,128]{1,0:T(8,128)(2,1)}, bf16[544,128]{1,0:T(8,128)(2,1)}, bf16[544,128]{1,0:T(8,128)(2,1)}) custom-call(bf16[1040,128]{1,0:T(8,128)(2,1)} %copy-done.17), custom_call_target="tpu_custom_call" | custom-call | tf_op jit(solution)/shard_map/bucket_tiles/pallas_call | solution.py:131
  32.7 0.6 collective-permute-start.10
  33.3 0.0 collective-permute-done.14.packed
  33.3 1.5 %collective-permute-start.11 = (bf16[544,128]{1,0:T(8,128)(2,1)}, bf16[544,128]{1,0:T(8,128)(2,1)S(1)}, u32[]{:S(2)}, u32[]{:S(2)}) collective-permute-start(bf16[544,128]{1,0:T(8,128)(2,1)} %get-tuple-element.35), channel_id=1, source_target_pairs={{0,4},{1,5},{2,6},{3,7},{4,0},{5,1},{6,2},{7,3},{8,12},{9,13},{10,... | collective-permute-start | bytes 417800 | tf_op jit(solution)/shard_map/ppermute | solution.py:230
  34.9 0.9 slice.76
  35.8 0.9 slice.80
  36.7 2.7 %bucket_tiles.5 = (bf16[544,128]{1,0:T(8,128)(2,1)}, bf16[544,128]{1,0:T(8,128)(2,1)}, bf16[544,128]{1,0:T(8,128)(2,1)}, bf16[544,128]{1,0:T(8,128)(2,1)}) custom-call(bf16[1040,128]{1,0:T(8,128)(2,1)} %copy-done.16), custom_call_target="tpu_custom_call" | custom-call | tf_op jit(solution)/shard_map/bucket_tiles/pallas_call | solution.py:131
  39.3 0.9 slice.84
  40.2 0.1 collective-permute-start.3
  40.3 0.0 collective-permute-done.6.rest_2_
  40.4 1.5 %collective-permute-start.12 = (bf16[544,128]{1,0:T(8,128)(2,1)S(1)}, bf16[544,128]{1,0:T(8,128)(2,1)S(1)}, u32[]{:S(2)}, u32[]{:S(2)}) collective-permute-start(bf16[544,128]{1,0:T(8,128)(2,1)S(1)} %copy-done.19), channel_id=1, source_target_pairs={{0,6},{1,7},{2,4},{3,5},{4,2},{5,3},{6,0},{7,1},{8,14},{9,15},{10,... | collective-permute-start | bytes 417800 | tf_op jit(solution)/shard_map/ppermute | solution.py:230
  41.9 0.6 collective-permute-start.15
  42.5 1.6 %collective-permute-start.16 = (bf16[544,128]{1,0:T(8,128)(2,1)}, bf16[544,128]{1,0:T(8,128)(2,1)S(1)}, u32[]{:S(2)}, u32[]{:S(2)}) collective-permute-start(bf16[544,128]{1,0:T(8,128)(2,1)} %get-tuple-element.39), channel_id=1, source_target_pairs={{0,4},{1,5},{2,6},{3,7},{4,0},{5,1},{6,2},{7,3},{8,12},{9,13},{10,... | collective-permute-start | bytes 417800 | tf_op jit(solution)/shard_map/ppermute | solution.py:230
  44.1 0.0 collective-permute-done.11.rest_2_
  44.1 1.5 %collective-permute-start.17 = (bf16[544,128]{1,0:T(8,128)(2,1)}, bf16[544,128]{1,0:T(8,128)(2,1)S(1)}, u32[]{:S(2)}, u32[]{:S(2)}) collective-permute-start(bf16[544,128]{1,0:T(8,128)(2,1)} %get-tuple-element.40), channel_id=1, source_target_pairs={{0,6},{1,7},{2,4},{3,5},{4,2},{5,3},{6,0},{7,1},{8,14},{9,15},{10,... | collective-permute-start | bytes 417800 | tf_op jit(solution)/shard_map/ppermute | solution.py:230
  45.7 2.2 %collective-permute-done.12.rest_3_ = bf16[544,128]{1,0:T(8,128)(2,1)S(1)} collective-permute-done((bf16[544,128]{1,0:T(8,128)(2,1)S(1)}, bf16[544,128]{1,0:T(8,128)(2,1)S(1)}, u32[]{:S(2)}, u32[]{:S(2)}) %collective-permute-start.12) | collective-permute-done | bytes 139296 | tf_op jit(solution)/shard_map/ppermute | solution.py:230
  47.8 0.0 collective-permute-start.8
  47.9 2.0 %collective-permute-done.15.rest_1_ = bf16[544,128]{1,0:T(8,128)(2,1)S(1)} collective-permute-done((bf16[544,128]{1,0:T(8,128)(2,1)}, bf16[544,128]{1,0:T(8,128)(2,1)S(1)}, u32[]{:S(2)}, u32[]{:S(2)}) %collective-permute-start.15) | collective-permute-done | bytes 139296 | tf_op jit(solution)/shard_map/ppermute | solution.py:230
  49.8 0.0 collective-permute-start.13
  49.9 0.9 collective-permute-done.16.rest_2_
  50.8 2.6 %collective-permute-done.17.rest_3_ = bf16[544,128]{1,0:T(8,128)(2,1)S(1)} collective-permute-done((bf16[544,128]{1,0:T(8,128)(2,1)}, bf16[544,128]{1,0:T(8,128)(2,1)S(1)}, u32[]{:S(2)}, u32[]{:S(2)}) %collective-permute-start.17) | collective-permute-done | bytes 139296 | tf_op jit(solution)/shard_map/ppermute | solution.py:230
  53.5 0.1 collective-permute-start.18
  53.6 0.0 collective-permute-done.3.rest_4_
  53.6 0.7 copy-done.12
  54.3 3.0 %build_rows.4.rest_0_ = bf16[128,4224]{1,0:T(8,128)(2,1)} custom-call(s32[2]{0:T(128)} %pad_add_fusion.me, bf16[544,128]{1,0:T(8,128)(2,1)} %get-tuple-element.24.rest_0_, bf16[544,128]{1,0:T(8,128)(2,1)} %copy-done, bf16[544,128]{1,0:T(8,128)(2,1)} %copy-done.1, bf16[544,128]{1,0:T(8,128)(2,1)} %copy-done.2, bf16[1088,128]{1,0:T(8,128)(2,1)} %copy-done.12), custom_call_target="tpu_custom_call" | custom-call | tf_op jit(solution)/shard_map/build_rows/pallas_call | solution.py:171
  57.4 0.0 collective-permute-done.8.rest_4_
  57.4 0.7 copy-done.13
  58.1 3.0 %build_rows.5.rest_1_ = bf16[128,4224]{1,0:T(8,128)(2,1)} custom-call(s32[2]{0:T(128)} %pad_add_fusion.me, bf16[544,128]{1,0:T(8,128)(2,1)} %get-tuple-element.29.rest_0_, bf16[544,128]{1,0:T(8,128)(2,1)} %copy-done.3, bf16[544,128]{1,0:T(8,128)(2,1)} %copy-done.4, bf16[544,128]{1,0:T(8,128)(2,1)} %copy-done.5, bf16[1088,128]{1,0:T(8,128)(2,1)} %copy-done.13), custom_call_target="tpu_custom_call" | custom-call | tf_op jit(solution)/shard_map/build_rows/pallas_call | solution.py:171
  61.1 0.0 collective-permute-done.13.rest_4_
  61.2 0.7 copy-done.14
  61.8 3.0 %build_rows.6.rest_2_ = bf16[128,4224]{1,0:T(8,128)(2,1)} custom-call(s32[2]{0:T(128)} %pad_add_fusion.me, bf16[544,128]{1,0:T(8,128)(2,1)} %get-tuple-element.33.rest_0_, bf16[544,128]{1,0:T(8,128)(2,1)} %copy-done.6, bf16[544,128]{1,0:T(8,128)(2,1)} %copy-done.7, bf16[544,128]{1,0:T(8,128)(2,1)} %copy-done.8, bf16[1088,128]{1,0:T(8,128)(2,1)} %copy-done.14), custom_call_target="tpu_custom_call" | custom-call | tf_op jit(solution)/shard_map/build_rows/pallas_call | solution.py:171
  64.9 0.7 copy-done.15
  65.6 3.0 %build_rows.7.rest_3_ = bf16[128,4224]{1,0:T(8,128)(2,1)} custom-call(s32[2]{0:T(128)} %pad_add_fusion.me, bf16[544,128]{1,0:T(8,128)(2,1)} %get-tuple-element.37.rest_0_, bf16[544,128]{1,0:T(8,128)(2,1)} %copy-done.9, bf16[544,128]{1,0:T(8,128)(2,1)} %copy-done.10, bf16[544,128]{1,0:T(8,128)(2,1)} %copy-done.11, bf16[1088,128]{1,0:T(8,128)(2,1)} %copy-done.15), custom_call_target="tpu_custom_call" | custom-call | tf_op jit(solution)/shard_map/build_rows/pallas_call | solution.py:171
  68.6 9.8 %product.1 = (f32[256,1024]{1,0:T(8,128)}, f32[256,1024]{1,0:T(8,128)}) custom-call(s32[2]{0:T(128)} %pad_add_fusion.me, bf16[128,4224]{1,0:T(8,128)(2,1)} %build_rows.4.rest_0_, bf16[128,4224]{1,0:T(8,128)(2,1)} %build_rows.5.rest_1_, bf16[128,4224]{1,0:T(8,128)(2,1)} %build_rows.6.rest_2_, bf16[128,4224]{1,0:T(8,128)(2,1)} %build_rows.7.rest_3_, ...), custom_call_target="tpu_custom_call" | custom-call | tf_op jit(solution)/shard_map/product/pallas_call | solution.py:212
  78.5 0.5 collective-permute-start.19
  79.0 2.5 %collective-permute-done.19 = f32[256,1024]{1,0:T(8,128)S(1)} collective-permute-done((f32[256,1024]{1,0:T(8,128)}, f32[256,1024]{1,0:T(8,128)S(1)}, u32[]{:S(2)}, u32[]{:S(2)}) %collective-permute-start.19) | collective-permute-done | bytes 1048608 | tf_op jit(solution)/shard_map/ppermute | solution.py:230
  81.5 1.2 %slice_add_fusion.2 = (f32[64,1024]{1,0:T(8,128)S(1)}, f32[64,1024]{1,0:T(8,128)S(1)}, f32[64,1024]{1,0:T(8,128)S(1)}) fusion(f32[256,1024]{1,0:T(8,128)S(1)} %collective-permute-done.19, f32[256,1024]{1,0:T(8,128)} %get-tuple-element.41), kind=kLoop, calls=%fused_computation.6 | loop fusion | flops 196608 | bytes 2359296 | tf_op jit(solution)/shard_map/add | solution.py:248
  82.7 1.6 %collective-permute-start.20 = (f32[64,1024]{1,0:T(8,128)S(1)}, f32[64,1024]{1,0:T(8,128)S(1)}, u32[]{:S(2)}, u32[]{:S(2)}) collective-permute-start(f32[64,1024]{1,0:T(8,128)S(1)} %get-tuple-element.43), channel_id=1, source_target_pairs={{0,2},{1,3},{2,0},{3,1},{4,6},{5,7},{6,4},{7,5},{8,10},{9,11},{10,... | collective-permute-start | bytes 786440 | tf_op jit(solution)/shard_map/ppermute | solution.py:230
  84.3 0.5 collective-permute-start.22
  84.7 1.5 %collective-permute-start.21 = (f32[64,1024]{1,0:T(8,128)S(1)}, f32[64,1024]{1,0:T(8,128)S(1)}, u32[]{:S(2)}, u32[]{:S(2)}) collective-permute-start(f32[64,1024]{1,0:T(8,128)S(1)} %get-tuple-element.45), channel_id=1, source_target_pairs={{0,4},{1,5},{2,6},{3,7},{4,0},{5,1},{6,2},{7,3},{8,12},{9,13},{10,... | collective-permute-start | bytes 786440 | tf_op jit(solution)/shard_map/ppermute | solution.py:230
  86.3 5.6 %collective-permute-done.20 = f32[64,1024]{1,0:T(8,128)S(1)} collective-permute-done((f32[64,1024]{1,0:T(8,128)S(1)}, f32[64,1024]{1,0:T(8,128)S(1)}, u32[]{:S(2)}, u32[]{:S(2)}) %collective-permute-start.20) | collective-permute-done | bytes 262176 | tf_op jit(solution)/shard_map/ppermute | solution.py:230
  91.9 5.1 %collective-permute-done.22 = f32[64,1024]{1,0:T(8,128)S(1)} collective-permute-done((f32[64,1024]{1,0:T(8,128)S(1)}, f32[64,1024]{1,0:T(8,128)S(1)}, u32[]{:S(2)}, u32[]{:S(2)}) %collective-permute-start.22) | collective-permute-done | bytes 262176 | tf_op jit(solution)/shard_map/ppermute | solution.py:230
  97.0 1.4 %collective-permute-done.21 = f32[64,1024]{1,0:T(8,128)S(1)} collective-permute-done((f32[64,1024]{1,0:T(8,128)S(1)}, f32[64,1024]{1,0:T(8,128)S(1)}, u32[]{:S(2)}, u32[]{:S(2)}) %collective-permute-start.21) | collective-permute-done | bytes 262176 | tf_op jit(solution)/shard_map/ppermute | solution.py:230
  98.3 1.8 %fusion.3 = f32[64,1024]{1,0:T(8,128)} fusion(f32[64,1024]{1,0:T(8,128)S(1)} %collective-permute-done.22, f32[64,1024]{1,0:T(8,128)S(1)} %collective-permute-done.21, f32[64,1024]{1,0:T(8,128)S(1)} %collective-permute-done.20, f32[256,1024]{1,0:T(8,128)S(1)} %collective-permute-done.19, f32[256,1024]{1,0:T(8,128)} %get-tuple-element.41), kind=kLoop, calls=%fused_computation.11 | loop fusion | flops 327680 | bytes 1572864 | tf_op jit(solution)/shard_map/mul | solution.py:254
  (54 shorter events, 0.2 us)
Async XLA Ops:
  2.9 8.9 %collective-permute-start = (bf16[544,128]{1,0:T(8,128)(2,1)}, bf16[544,128]{1,0:T(8,128)(2,1)S(1)}, u32[]{:S(2)}, u32[]{:S(2)}) collective-permute-start(bf16[544,128]{1,0:T(8,128)(2,1)} %get-tuple-element.25), channel_id=1, source_target_pairs={{0,2},{1,3},{2,0},{3,1},{4,6},{5,7},{6,4},{7,5},{8,10},{9,11},{10,... | collective-permute-start | bytes 417800 | tf_op jit(solution)/shard_map/ppermute | solution.py:230
  5.9 12.9 %collective-permute-start.4 = (bf16[1040,128]{1,0:T(8,128)(2,1)}, bf16[1040,128]{1,0:T(8,128)(2,1)S(1)}, u32[]{:S(2)}, u32[]{:S(2)}) collective-permute-start(bf16[1040,128]{1,0:T(8,128)(2,1)} %get-tuple-element.28), channel_id=1, source_target_pairs={{0,8},{8,0},{16,24},{24,16},{1,9},{9,1},{17,25},{25,17},{2,10},{10... | collective-permute-start | bytes 798728 | tf_op jit(solution)/shard_map/ppermute | solution.py:230
  7.5 21.9 %collective-permute-start.9 = (bf16[1040,128]{1,0:T(8,128)(2,1)}, bf16[1040,128]{1,0:T(8,128)(2,1)S(1)}, u32[]{:S(2)}, u32[]{:S(2)}) collective-permute-start(bf16[1040,128]{1,0:T(8,128)(2,1)} %get-tuple-element.28), channel_id=1, source_target_pairs={{0,16},{8,24},{16,0},{24,8},{1,17},{9,25},{17,1},{25,9},{2,18},{10... | collective-permute-start | bytes 798728 | tf_op jit(solution)/shard_map/ppermute | solution.py:230
  10.1 23.3 %collective-permute-start.14 = (bf16[1040,128]{1,0:T(8,128)(2,1)}, bf16[1040,128]{1,0:T(8,128)(2,1)S(1)}, u32[]{:S(2)}, u32[]{:S(2)}) collective-permute-start(bf16[1040,128]{1,0:T(8,128)(2,1)} %get-tuple-element.28), channel_id=1, source_target_pairs={{0,24},{8,16},{16,8},{24,0},{1,25},{9,17},{17,9},{25,1},{2,26},{10... | collective-permute-start | bytes 798728 | tf_op jit(solution)/shard_map/ppermute | solution.py:230
  10.3 8.2 %collective-permute-start.1 = (bf16[544,128]{1,0:T(8,128)(2,1)}, bf16[544,128]{1,0:T(8,128)(2,1)S(1)}, u32[]{:S(2)}, u32[]{:S(2)}) collective-permute-start(bf16[544,128]{1,0:T(8,128)(2,1)} %get-tuple-element.26), channel_id=1, source_target_pairs={{0,4},{1,5},{2,6},{3,7},{4,0},{5,1},{6,2},{7,3},{8,12},{9,13},{10,... | collective-permute-start | bytes 417800 | tf_op jit(solution)/shard_map/ppermute | solution.py:230
  11.8 27.5 %copy-start = (bf16[544,128]{1,0:T(8,128)(2,1)}, bf16[544,128]{1,0:T(8,128)(2,1)S(1)}, u32[]{:S(2)}) copy-start(bf16[544,128]{1,0:T(8,128)(2,1)S(1)} %collective-permute-done.rest_1_) | copy-start | bytes 417796
  11.8 6.7 %collective-permute-start.2 = (bf16[544,128]{1,0:T(8,128)(2,1)}, bf16[544,128]{1,0:T(8,128)(2,1)S(1)}, u32[]{:S(2)}, u32[]{:S(2)}) collective-permute-start(bf16[544,128]{1,0:T(8,128)(2,1)} %get-tuple-element.27), channel_id=1, source_target_pairs={{0,6},{1,7},{2,4},{3,5},{4,2},{5,3},{6,0},{7,1},{8,14},{9,15},{10,... | collective-permute-start | bytes 417800 | tf_op jit(solution)/shard_map/ppermute | solution.py:230
  18.5 21.9 %copy-start.1 = (bf16[544,128]{1,0:T(8,128)(2,1)}, bf16[544,128]{1,0:T(8,128)(2,1)S(1)}, u32[]{:S(2)}) copy-start(bf16[544,128]{1,0:T(8,128)(2,1)S(1)} %collective-permute-done.1.rest_2_) | copy-start | bytes 417796
  18.5 23.4 %copy-start.2 = (bf16[544,128]{1,0:T(8,128)(2,1)}, bf16[544,128]{1,0:T(8,128)(2,1)S(1)}, u32[]{:S(2)}) copy-start(bf16[544,128]{1,0:T(8,128)(2,1)S(1)} %collective-permute-done.2.rest_3_) | copy-start | bytes 417796
  18.8 0.7 copy-start.18
  22.1 18.1 %collective-permute-start.5 = (bf16[544,128]{1,0:T(8,128)(2,1)}, bf16[544,128]{1,0:T(8,128)(2,1)S(1)}, u32[]{:S(2)}, u32[]{:S(2)}) collective-permute-start(bf16[544,128]{1,0:T(8,128)(2,1)} %get-tuple-element.30), channel_id=1, source_target_pairs={{0,2},{1,3},{2,0},{3,1},{4,6},{5,7},{6,4},{7,5},{8,10},{9,11},{10,... | collective-permute-start | bytes 417800 | tf_op jit(solution)/shard_map/ppermute | solution.py:230
  22.6 17.8 %collective-permute-start.6 = (bf16[544,128]{1,0:T(8,128)(2,1)}, bf16[544,128]{1,0:T(8,128)(2,1)S(1)}, u32[]{:S(2)}, u32[]{:S(2)}) collective-permute-start(bf16[544,128]{1,0:T(8,128)(2,1)} %get-tuple-element.31), channel_id=1, source_target_pairs={{0,4},{1,5},{2,6},{3,7},{4,0},{5,1},{6,2},{7,3},{8,12},{9,13},{10,... | collective-permute-start | bytes 417800 | tf_op jit(solution)/shard_map/ppermute | solution.py:230
  24.3 17.6 %collective-permute-start.7 = (bf16[544,128]{1,0:T(8,128)(2,1)}, bf16[544,128]{1,0:T(8,128)(2,1)S(1)}, u32[]{:S(2)}, u32[]{:S(2)}) collective-permute-start(bf16[544,128]{1,0:T(8,128)(2,1)} %get-tuple-element.32), channel_id=1, source_target_pairs={{0,6},{1,7},{2,4},{3,5},{4,2},{5,3},{6,0},{7,1},{8,14},{9,15},{10,... | collective-permute-start | bytes 417800 | tf_op jit(solution)/shard_map/ppermute | solution.py:230
  29.3 0.7 copy-start.17
  32.7 7.6 %copy-start.19 = (bf16[544,128]{1,0:T(8,128)(2,1)S(1)}, bf16[544,128]{1,0:T(8,128)(2,1)}, u32[]{:S(2)}) copy-start(bf16[544,128]{1,0:T(8,128)(2,1)} %get-tuple-element.36) | copy-start | bytes 417796
  32.7 9.8 %collective-permute-start.10 = (bf16[544,128]{1,0:T(8,128)(2,1)}, bf16[544,128]{1,0:T(8,128)(2,1)S(1)}, u32[]{:S(2)}, u32[]{:S(2)}) collective-permute-start(bf16[544,128]{1,0:T(8,128)(2,1)} %get-tuple-element.34), channel_id=1, source_target_pairs={{0,2},{1,3},{2,0},{3,1},{4,6},{5,7},{6,4},{7,5},{8,10},{9,11},{10,... | collective-permute-start | bytes 417800 | tf_op jit(solution)/shard_map/ppermute | solution.py:230
  33.3 3.3 %copy-start.16 = (bf16[1040,128]{1,0:T(8,128)(2,1)}, bf16[1040,128]{1,0:T(8,128)(2,1)S(1)}, u32[]{:S(2)}) copy-start(bf16[1040,128]{1,0:T(8,128)(2,1)S(1)} %collective-permute-done.14.packed) | copy-start | bytes 798724
  33.3 10.8 %collective-permute-start.11 = (bf16[544,128]{1,0:T(8,128)(2,1)}, bf16[544,128]{1,0:T(8,128)(2,1)S(1)}, u32[]{:S(2)}, u32[]{:S(2)}) collective-permute-start(bf16[544,128]{1,0:T(8,128)(2,1)} %get-tuple-element.35), channel_id=1, source_target_pairs={{0,4},{1,5},{2,6},{3,7},{4,0},{5,1},{6,2},{7,3},{8,12},{9,13},{10,... | collective-permute-start | bytes 417800 | tf_op jit(solution)/shard_map/ppermute | solution.py:230
  40.2 10.5 %copy-start.3 = (bf16[544,128]{1,0:T(8,128)(2,1)}, bf16[544,128]{1,0:T(8,128)(2,1)S(1)}, u32[]{:S(2)}) copy-start(bf16[544,128]{1,0:T(8,128)(2,1)S(1)} %collective-permute-done.5.rest_1_) | copy-start | bytes 417796
  40.2 13.3 %collective-permute-start.3 = (bf16[1088,128]{1,0:T(8,128)(2,1)S(1)}, bf16[1088,128]{1,0:T(8,128)(2,1)S(1)}, u32[]{:S(2)}, u32[]{:S(2)}) collective-permute-start(bf16[1088,128]{1,0:T(8,128)(2,1)S(1)} %pad_maximum_fusion), channel_id=1, source_target_pairs={{0,1},{1,0},{2,3},{3,2},{4,5},{5,4},{6,7},{7,6},{8,9},{9,8},{10,11... | collective-permute-start | bytes 835592 | tf_op jit(solution)/shard_map/ppermute | solution.py:230
  40.4 13.0 %copy-start.4 = (bf16[544,128]{1,0:T(8,128)(2,1)}, bf16[544,128]{1,0:T(8,128)(2,1)S(1)}, u32[]{:S(2)}) copy-start(bf16[544,128]{1,0:T(8,128)(2,1)S(1)} %collective-permute-done.6.rest_2_) | copy-start | bytes 417796
  40.4 7.5 %collective-permute-start.12 = (bf16[544,128]{1,0:T(8,128)(2,1)S(1)}, bf16[544,128]{1,0:T(8,128)(2,1)S(1)}, u32[]{:S(2)}, u32[]{:S(2)}) collective-permute-start(bf16[544,128]{1,0:T(8,128)(2,1)S(1)} %copy-done.19), channel_id=1, source_target_pairs={{0,6},{1,7},{2,4},{3,5},{4,2},{5,3},{6,0},{7,1},{8,14},{9,15},{10,... | collective-permute-start | bytes 417800 | tf_op jit(solution)/shard_map/ppermute | solution.py:230
  41.9 11.5 %copy-start.5 = (bf16[544,128]{1,0:T(8,128)(2,1)}, bf16[544,128]{1,0:T(8,128)(2,1)S(1)}, u32[]{:S(2)}) copy-start(bf16[544,128]{1,0:T(8,128)(2,1)S(1)} %collective-permute-done.7.rest_3_) | copy-start | bytes 417796
  41.9 7.9 %collective-permute-start.15 = (bf16[544,128]{1,0:T(8,128)(2,1)}, bf16[544,128]{1,0:T(8,128)(2,1)S(1)}, u32[]{:S(2)}, u32[]{:S(2)}) collective-permute-start(bf16[544,128]{1,0:T(8,128)(2,1)} %get-tuple-element.38), channel_id=1, source_target_pairs={{0,2},{1,3},{2,0},{3,1},{4,6},{5,7},{6,4},{7,5},{8,10},{9,11},{10,... | collective-permute-start | bytes 417800 | tf_op jit(solution)/shard_map/ppermute | solution.py:230
  42.5 10.9 %copy-start.6 = (bf16[544,128]{1,0:T(8,128)(2,1)}, bf16[544,128]{1,0:T(8,128)(2,1)S(1)}, u32[]{:S(2)}) copy-start(bf16[544,128]{1,0:T(8,128)(2,1)S(1)} %collective-permute-done.10.rest_1_) | copy-start | bytes 417796
  42.5 8.2 %collective-permute-start.16 = (bf16[544,128]{1,0:T(8,128)(2,1)}, bf16[544,128]{1,0:T(8,128)(2,1)S(1)}, u32[]{:S(2)}, u32[]{:S(2)}) collective-permute-start(bf16[544,128]{1,0:T(8,128)(2,1)} %get-tuple-element.39), channel_id=1, source_target_pairs={{0,4},{1,5},{2,6},{3,7},{4,0},{5,1},{6,2},{7,3},{8,12},{9,13},{10,... | collective-permute-start | bytes 417800 | tf_op jit(solution)/shard_map/ppermute | solution.py:230
  44.1 9.3 %copy-start.7 = (bf16[544,128]{1,0:T(8,128)(2,1)}, bf16[544,128]{1,0:T(8,128)(2,1)S(1)}, u32[]{:S(2)}) copy-start(bf16[544,128]{1,0:T(8,128)(2,1)S(1)} %collective-permute-done.11.rest_2_) | copy-start | bytes 417796
  44.1 9.3 %collective-permute-start.17 = (bf16[544,128]{1,0:T(8,128)(2,1)}, bf16[544,128]{1,0:T(8,128)(2,1)S(1)}, u32[]{:S(2)}, u32[]{:S(2)}) collective-permute-start(bf16[544,128]{1,0:T(8,128)(2,1)} %get-tuple-element.40), channel_id=1, source_target_pairs={{0,6},{1,7},{2,4},{3,5},{4,2},{5,3},{6,0},{7,1},{8,14},{9,15},{10,... | collective-permute-start | bytes 417800 | tf_op jit(solution)/shard_map/ppermute | solution.py:230
  47.8 9.5 %copy-start.8 = (bf16[544,128]{1,0:T(8,128)(2,1)}, bf16[544,128]{1,0:T(8,128)(2,1)S(1)}, u32[]{:S(2)}) copy-start(bf16[544,128]{1,0:T(8,128)(2,1)S(1)} %collective-permute-done.12.rest_3_) | copy-start | bytes 417796
  47.8 9.5 %collective-permute-start.8 = (bf16[1088,128]{1,0:T(8,128)(2,1)S(1)}, bf16[1088,128]{1,0:T(8,128)(2,1)S(1)}, u32[]{:S(2)}, u32[]{:S(2)}) collective-permute-start(bf16[1088,128]{1,0:T(8,128)(2,1)S(1)} %pad_maximum_fusion.1), channel_id=1, source_target_pairs={{0,1},{1,0},{2,3},{3,2},{4,5},{5,4},{6,7},{7,6},{8,9},{9,8},{10,11... | collective-permute-start | bytes 835592 | tf_op jit(solution)/shard_map/ppermute | solution.py:230
  49.8 7.5 %copy-start.9 = (bf16[544,128]{1,0:T(8,128)(2,1)}, bf16[544,128]{1,0:T(8,128)(2,1)S(1)}, u32[]{:S(2)}) copy-start(bf16[544,128]{1,0:T(8,128)(2,1)S(1)} %collective-permute-done.15.rest_1_) | copy-start | bytes 417796
  49.8 11.3 %collective-permute-start.13 = (bf16[1088,128]{1,0:T(8,128)(2,1)S(1)}, bf16[1088,128]{1,0:T(8,128)(2,1)S(1)}, u32[]{:S(2)}, u32[]{:S(2)}) collective-permute-start(bf16[1088,128]{1,0:T(8,128)(2,1)S(1)} %pad_maximum_fusion.2), channel_id=1, source_target_pairs={{0,1},{1,0},{2,3},{3,2},{4,5},{5,4},{6,7},{7,6},{8,9},{9,8},{10,11... | collective-permute-start | bytes 835592 | tf_op jit(solution)/shard_map/ppermute | solution.py:230
  50.8 6.6 %copy-start.10 = (bf16[544,128]{1,0:T(8,128)(2,1)}, bf16[544,128]{1,0:T(8,128)(2,1)S(1)}, u32[]{:S(2)}) copy-start(bf16[544,128]{1,0:T(8,128)(2,1)S(1)} %collective-permute-done.16.rest_2_) | copy-start | bytes 417796
  53.4 4.0 %copy-start.11 = (bf16[544,128]{1,0:T(8,128)(2,1)}, bf16[544,128]{1,0:T(8,128)(2,1)S(1)}, u32[]{:S(2)}) copy-start(bf16[544,128]{1,0:T(8,128)(2,1)S(1)} %collective-permute-done.17.rest_3_) | copy-start | bytes 417796
  53.5 11.4 %collective-permute-start.18 = (bf16[1088,128]{1,0:T(8,128)(2,1)S(1)}, bf16[1088,128]{1,0:T(8,128)(2,1)S(1)}, u32[]{:S(2)}, u32[]{:S(2)}) collective-permute-start(bf16[1088,128]{1,0:T(8,128)(2,1)S(1)} %pad_maximum_fusion.3), channel_id=1, source_target_pairs={{0,1},{1,0},{2,3},{3,2},{4,5},{5,4},{6,7},{7,6},{8,9},{9,8},{10,11... | collective-permute-start | bytes 835592 | tf_op jit(solution)/shard_map/ppermute | solution.py:230
  53.6 0.7 copy-start.12
  57.4 0.7 copy-start.13
  61.2 0.7 copy-start.14
  64.9 0.7 copy-start.15
  78.5 3.0 %collective-permute-start.19 = (f32[256,1024]{1,0:T(8,128)}, f32[256,1024]{1,0:T(8,128)S(1)}, u32[]{:S(2)}, u32[]{:S(2)}) collective-permute-start(f32[256,1024]{1,0:T(8,128)} %get-tuple-element.42), channel_id=1, source_target_pairs={{0,1},{1,0},{2,3},{3,2},{4,5},{5,4},{6,7},{7,6},{8,9},{9,8},{10,11... | collective-permute-start | bytes 3145736 | tf_op jit(solution)/shard_map/ppermute | solution.py:230
  82.7 9.2 %collective-permute-start.20 = (f32[64,1024]{1,0:T(8,128)S(1)}, f32[64,1024]{1,0:T(8,128)S(1)}, u32[]{:S(2)}, u32[]{:S(2)}) collective-permute-start(f32[64,1024]{1,0:T(8,128)S(1)} %get-tuple-element.43), channel_id=1, source_target_pairs={{0,2},{1,3},{2,0},{3,1},{4,6},{5,7},{6,4},{7,5},{8,10},{9,11},{10,... | collective-permute-start | bytes 786440 | tf_op jit(solution)/shard_map/ppermute | solution.py:230
  84.3 12.7 %collective-permute-start.22 = (f32[64,1024]{1,0:T(8,128)S(1)}, f32[64,1024]{1,0:T(8,128)S(1)}, u32[]{:S(2)}, u32[]{:S(2)}) collective-permute-start(f32[64,1024]{1,0:T(8,128)S(1)} %get-tuple-element.44), channel_id=1, source_target_pairs={{0,6},{1,7},{2,4},{3,5},{4,2},{5,3},{6,0},{7,1},{8,14},{9,15},{10,... | collective-permute-start | bytes 786440 | tf_op jit(solution)/shard_map/ppermute | solution.py:230
  84.7 13.6 %collective-permute-start.21 = (f32[64,1024]{1,0:T(8,128)S(1)}, f32[64,1024]{1,0:T(8,128)S(1)}, u32[]{:S(2)}, u32[]{:S(2)}) collective-permute-start(f32[64,1024]{1,0:T(8,128)S(1)} %get-tuple-element.45), channel_id=1, source_target_pairs={{0,4},{1,5},{2,6},{3,7},{4,0},{5,1},{6,2},{7,3},{8,12},{9,13},{10,... | collective-permute-start | bytes 786440 | tf_op jit(solution)/shard_map/ppermute | solution.py:230

commit v2 on v0

v2 whole, which is shorter than its diff:
```python
import functools

import jax
import jax.numpy as jnp
from jax import lax
from jax.experimental import pallas as pl
from jax.experimental.pallas import tpu as pltpu
from jax.sharding import PartitionSpec as P

CAP = 16

VMEM = pl.BlockSpec(memory_space=pltpu.VMEM)
HBM = pl.BlockSpec(memory_space=pltpu.HBM)


def shift_of(size):
    assert size & (size - 1) == 0
    return size.bit_length() - 1


class Plan:
    def __init__(self, lam_tiles, integrals):
        self.n_row = lax.axis_size("row")
        self.n_col = lax.axis_size("col")
        g_dev, self.slots, self.pairs, self.tile = lam_tiles.shape
        assert g_dev == 1 and self.pairs == 16 and self.slots <= self.tile
        self.ab, self.cd = integrals.shape
        self.kt = self.cd // self.tile
        self.n_pair = self.n_col // 2
        self.per_row = self.n_col // self.n_row
        assert self.per_row % 2 == 0
        self.owned = self.n_col * self.pairs // self.per_row
        self.height = self.n_col * self.pairs
        self.bucket = (CAP + 1) * self.pairs
        self.head = -(-(self.n_col + 1) // 16) * 16
        self.body = self.slots * self.pairs
        self.packed = self.body + self.head


def pack_kernel(plan, ids, tiles, packed, ids_row, buf, sem):
    load = pltpu.make_async_copy(tiles, buf.at[pl.ds(0, plan.body)], sem.at[0])
    load_ids = pltpu.make_async_copy(ids, ids_row, sem.at[1])
    load_ids.start()
    load.start()
    load_ids.wait()
    n = plan.slots
    row = jnp.broadcast_to(ids_row[...], (n, n))
    col = row.astype(jnp.float32).T.astype(jnp.int32)
    here, there = (lax.broadcasted_iota(jnp.int32, (n, n), i) for i in range(2))
    same = (row >> shift_of(plan.kt)) == (col >> shift_of(plan.kt))
    place_row = jnp.sum(jnp.where(same & (here < there), 1, 0), axis=0, keepdims=True)
    place_col = jnp.sum(jnp.where(same & (there < here), 1, 0), axis=1, keepdims=True)
    line = lax.broadcasted_iota(jnp.int32, (plan.head, n), 0)
    ids_line = jnp.broadcast_to(ids_row[...], (plan.head, n))
    block = ids_line >> shift_of(plan.kt)
    lane = lax.broadcasted_iota(jnp.int32, (n, plan.tile), 1)
    tile_at = lax.broadcasted_iota(jnp.int32, (n, plan.tile), 0)

    def spread(values, where):
        return lax.dot_general(
            values.astype(jnp.float32).astype(jnp.bfloat16),
            jnp.where(where, 1.0, 0.0).astype(jnp.bfloat16),
            (((1,), (0,)), ((), ())),
            preferred_element_type=jnp.float32,
        )

    missing = jnp.where(block == line, (ids_line & (plan.kt - 1)) - plan.kt, 0)
    places = spread(missing, place_col == lane) + plan.kt
    slot = jnp.where(line == plan.n_col, block * CAP + place_row, 0)
    slots = spread(slot, tile_at == lane)
    top = lax.broadcasted_iota(jnp.int32, (plan.head, plan.tile), 0)
    head = jnp.where(top == plan.n_col, slots, places)
    buf[plan.body :, :] = head.astype(jnp.bfloat16)
    load.wait()
    store = pltpu.make_async_copy(buf, packed, sem.at[0])
    store.start()
    store.wait()


def pack(plan, ids, tiles):
    return pl.pallas_call(
        functools.partial(pack_kernel, plan),
        out_shape=jax.ShapeDtypeStruct((plan.packed, plan.tile), jnp.bfloat16),
        in_specs=[HBM, HBM],
        out_specs=HBM,
        scratch_shapes=[
            pltpu.VMEM(ids.shape, jnp.int32),
            pltpu.VMEM((plan.packed, plan.tile), jnp.bfloat16),
            pltpu.SemaphoreType.DMA((2,)),
        ],
        compiler_params=pltpu.CompilerParams(vmem_limit_bytes=8 * 1024 * 1024),
        cost_estimate=cost(plan, 2 * plan.packed * plan.tile * 2),
        name="pack_tiles",
    )(ids, tiles)


def cost(plan, moved, flops=0):
    return pl.CostEstimate(flops=flops, bytes_accessed=moved, transcendentals=0)


def bucket_kernel(plan, count, *rest):
    packed, outs = rest[:count], rest[count : count + plan.n_pair]
    bodies, tops, buf, heads, line, places, sem = rest[count + plan.n_pair :]
    rows, piece = plan.pairs, count * plan.bucket
    loads = []
    for i, ref in enumerate(packed):
        top = tops.at[pl.ds(i * plan.head, plan.head)]
        loads.append(pltpu.make_async_copy(ref.at[pl.ds(plan.body, plan.head)], top, sem.at[2 * i]))
        loads[-1].start()
    for i, ref in enumerate(packed):
        body = bodies.at[pl.ds(i * plan.body, plan.body)]
        loads.append(pltpu.make_async_copy(ref.at[pl.ds(0, plan.body)], body, sem.at[2 * i + 1]))
        loads[-1].start()
    col = lax.axis_index("col")
    for i in range(count):
        loads[i].wait()
        head = tops[i * plan.head : (i + 1) * plan.head, :].astype(jnp.float32)
        heads[i * plan.head : (i + 1) * plan.head, :] = head
        slot = head[plan.n_col : plan.n_col + 1, :].astype(jnp.int32)
        m = (slot >> shift_of(CAP)) ^ col
        at = (m >> 1) * piece + i * plan.bucket + (slot & (CAP - 1)) * rows
        line[i : i + 1, :] = jnp.where((m & 1) == 0, at, plan.n_pair * piece)
    copy = pltpu.make_async_copy(line, places, sem.at[2 * count])
    copy.start()
    for i in range(count):
        for chip in range(plan.n_pair):
            ids = heads[pl.ds(i * plan.head + (col ^ (2 * chip)), 1), :]
            at = chip * piece + i * plan.bucket + CAP * rows
            buf[at : at + rows, :] = jnp.broadcast_to(ids, (rows, plan.tile)).astype(jnp.bfloat16)
    copy.wait()
    for i in range(count):
        loads[count + i].wait()

        def step(s, _, i=i):
            at = pl.multiple_of(places[i, s], rows)
            tile = bodies[pl.ds(pl.multiple_of(i * plan.body + s * rows, rows), rows), :]
            buf[pl.ds(at, rows), :] = tile
            return 0

        lax.fori_loop(0, plan.slots, step, 0, unroll=16)
    copies = []
    for i, out in enumerate(outs):
        part = buf.at[pl.ds(i * piece, piece)]
        copies.append(pltpu.make_async_copy(part, out, sem.at[2 * count + 1 + i]))
        copies[-1].start()
    for copy in copies:
        copy.wait()


def bucket(plan, packed):
    count = len(packed)
    piece = count * plan.bucket
    lines = -(-count // 8) * 8
    bf16 = jnp.bfloat16
    return pl.pallas_call(
        functools.partial(bucket_kernel, plan, count),
        out_shape=[jax.ShapeDtypeStruct((piece, plan.tile), bf16)] * plan.n_pair,
        in_specs=[HBM] * count,
        out_specs=[HBM] * plan.n_pair,
        scratch_shapes=[
            pltpu.VMEM((count * plan.body, plan.tile), bf16),
            pltpu.VMEM((count * plan.head, plan.tile), bf16),
            pltpu.VMEM((plan.n_pair * piece + plan.pairs, plan.tile), bf16),
            pltpu.VMEM((count * plan.head, plan.tile), jnp.float32),
            pltpu.VMEM((lines, plan.tile), jnp.int32),
            pltpu.SMEM((lines, plan.tile), jnp.int32),
            pltpu.SemaphoreType.DMA((2 * count + 1 + plan.n_pair,)),
        ],
        compiler_params=pltpu.CompilerParams(vmem_limit_bytes=20 * 1024 * 1024),
        cost_estimate=cost(plan, 4 * plan.n_pair * piece * plan.tile * 2),
        name="bucket_tiles",
    )(*packed)


def stage_kernel(steps, block, source, out, sem):
    copies = []
    for i in range(steps):
        here = pl.ds(i * block, block)
        copies.append(pltpu.make_async_copy(source.at[here], out.at[here], sem.at[i]))
        copies[-1].start()
    for copy in copies:
        copy.wait()


def stage(plan, integrals, block=256):
    steps = plan.ab // block
    return pl.pallas_call(
        functools.partial(stage_kernel, steps, block),
        out_shape=pltpu.VMEM(integrals.shape, integrals.dtype),
        in_specs=[HBM],
        out_specs=VMEM,
        scratch_shapes=[pltpu.SemaphoreType.DMA((steps,))],
        compiler_params=pltpu.CompilerParams(vmem_limit_bytes=2 * 1024 * 1024),
        cost_estimate=cost(plan, 2 * plan.ab * plan.cd * 2),
        name="stage_integrals",
    )(integrals)


def send_kernel(plan, groups, block, *rest):
    n_in = len(groups) * plan.n_pair
    parts, rest = rest[:n_in], rest[n_in:]
    cols, lam, send, tiles, line, places, sem, part_sem = rest
    rows = plan.pairs
    half = plan.n_pair * plan.owned
    sources, loads, at = [], [], 0
    for g, planes in enumerate(groups):
        for chip in range(plan.n_pair):
            ref = parts[g * plan.n_pair + chip]
            to = tiles.at[pl.ds(at, ref.shape[0])]
            loads.append(pltpu.make_async_copy(ref, to, part_sem.at[len(loads)]))
            loads[-1].start()
            for d in planes:
                for side in range(2):
                    sources.append((at, d, 2 * chip + side))
                    at += plan.bucket
    lam[...] = jnp.zeros(lam.shape, lam.dtype)
    for load in loads:
        load.wait()
    for i, (base, _, _) in enumerate(sources):
        head = tiles[base + CAP * rows : base + plan.bucket, :].astype(jnp.float32)
        line[i : i + 1, :] = head[0:1, :].astype(jnp.int32)
    copy = pltpu.make_async_copy(line, places, sem)
    copy.start()
    copy.wait()
    row, col = lax.axis_index("row"), lax.axis_index("col")
    per_owner = plan.owned // rows
    for i, (base, d, m) in enumerate(sources):
        group = (row ^ d) * plan.n_col + (col ^ m)
        rel = (group >> shift_of(per_owner)) ^ col
        to = (rel & 1) * half + (rel >> 1) * plan.owned + (group & (per_owner - 1)) * rows
        for s in range(CAP):
            at = places[i, s]
            line_at = pl.multiple_of(jnp.where(at < plan.kt, to, 2 * half), rows)
            at = pl.multiple_of((at & (plan.kt - 1)) * plan.tile, plan.tile)
            tile = tiles[base + s * rows : base + (s + 1) * rows, :]
            lam[pl.ds(line_at, rows), pl.ds(at, plan.tile)] = tile
    multiply(plan, block, lam, half, cols, send)


def multiply(plan, block, lam, first, cols, out):
    for i in range(0, plan.ab, block):
        out[:, i : i + block] = lax.dot_general(
            lam[first : first + out.shape[0], :],
            cols[i : i + block, :],
            (((1,), (1,)), ((), ())),
            preferred_element_type=jnp.float32,
        )


def send_product(plan, groups, parts, integrals, block=256):
    half = plan.n_pair * plan.owned
    n_src = plan.n_row * plan.n_col
    flat = [part for group in parts for part in group]
    bf16 = jnp.bfloat16
    return pl.pallas_call(
        functools.partial(send_kernel, plan, groups, block),
        out_shape=[
            pltpu.VMEM((2 * half + plan.pairs, plan.cd), bf16),
            pltpu.VMEM((half, plan.ab), jnp.float32),
        ],
        in_specs=[HBM] * len(flat) + [VMEM],
        out_specs=[VMEM, VMEM],
        scratch_shapes=[
            pltpu.VMEM((n_src * plan.bucket, plan.tile), bf16),
            pltpu.VMEM((n_src, plan.tile), jnp.int32),
            pltpu.SMEM((n_src, plan.tile), jnp.int32),
            pltpu.SemaphoreType.DMA,
            pltpu.SemaphoreType.DMA((len(flat),)),
        ],
        compiler_params=pltpu.CompilerParams(vmem_limit_bytes=28 * 1024 * 1024),
        cost_estimate=cost(plan, plan.ab * plan.cd * 4, 4 * half * plan.ab * plan.cd),
        name="place_and_multiply",
    )(*flat, integrals)


def keep_kernel(plan, block, lam, cols, out):
    multiply(plan, block, lam, 0, cols, out)


def keep_product(plan, lam, integrals, block=256):
    half = plan.n_pair * plan.owned
    return pl.pallas_call(
        functools.partial(keep_kernel, plan, block),
        out_shape=pltpu.VMEM((half, plan.ab), jnp.float32),
        in_specs=[VMEM, VMEM],
        out_specs=VMEM,
        compiler_params=pltpu.CompilerParams(vmem_limit_bytes=20 * 1024 * 1024),
        cost_estimate=cost(plan, (plan.ab + half) * plan.cd * 2, 2 * half * plan.ab * plan.cd),
        name="multiply_kept",
    )(lam, integrals)


def swap(x, axis, m):
    return lax.ppermute(x, axis, [(i, i ^ m) for i in range(lax.axis_size(axis))])


def shards(lam_tiles, lam_ids, integrals):
    plan = Plan(lam_tiles, integrals)
    packed = pack(plan, lam_ids, lam_tiles.reshape(plan.body, plan.tile))
    groups = [[0], list(range(1, plan.n_row - 1)), [plan.n_row - 1]]
    parts = []

    def spread(planes):
        raws = [raw for d in planes for raw in (arrived[d], swap(arrived[d], "col", 1))]
        if len(parts) == 1:
            *raws, parts[0] = lax.optimization_barrier((*raws, parts[0]))
        elif parts:
            *raws, parts[-1][0] = lax.optimization_barrier((*raws, parts[-1][0]))
        out = bucket(plan, raws)
        parts.append([out[0]] + [swap(out[m], "col", 2 * m) for m in range(1, plan.n_pair)])

    arrived = {0: packed}
    bit = plan.n_row // 2
    arrived[bit] = swap(packed, "row", bit)
    spread(groups[0])
    staged = stage(plan, integrals)
    arrived[bit], parts[0][1], staged = lax.optimization_barrier((arrived[bit], parts[0][1], staged))
    while bit > 1:
        bit //= 2
        arrived.update({d | bit: swap(raw, "row", bit) for d, raw in arrived.items()})
    for group in groups[1:]:
        spread(group)
    lam, send = send_product(plan, groups, parts, staged)
    got = swap(send, "col", 1)
    keep = keep_product(plan, lam, staged)
    both = [
        keep[m * plan.owned : (m + 1) * plan.owned] + got[m * plan.owned : (m + 1) * plan.owned]
        for m in range(plan.n_pair)
    ]
    others = [swap(both[m], "col", 2 * m) for m in range(1, plan.n_pair)]
    return 0.5 * functools.reduce(jnp.add, others, both[0])


def solution(mesh):
    return jax.shard_map(
        shards,
        mesh=mesh,
        in_specs=(P(("row", "col"), None, None, None), P(("row", "col"), None), P("row", "col")),
        out_specs=P("col", "row"),
        check_vma=False,
    )
```

time: 134 us -> 81.3 us (0.61)
  blocking collectives: 28.2 us -> 0 us
  waiting for transfers between devices: 58.1 us -> 35.4 us
  starting transfers between devices: 3.35 us -> 23.4 us
  Pallas kernels: 0 us -> 16.3 us
  between operations: 13.5 us -> 0.1 us
  matrix products: 13 us -> 0 us
  local copies, waits for them, and re-layouts: 15.5 us -> 4.99 us
    reduce_scatter x1 -> x0, waiting for transfers between devices: 40.1 us -> none  [shards(): lax.psum_scatter(0.5 * product.reshape(groups * pairs // n_col * lax.axis...]
    ppermute x0 -> x20, waiting for transfers between devices: none -> 35.4 us  [swap(): lax.ppermute(x, axis, [(i, i ^ m) for i in range(lax.axis_size(axis))])]
    ppermute x0 -> x20, starting transfers between devices: none -> 23.4 us  [swap(): lax.ppermute(x, axis, [(i, i ^ m) for i in range(lax.axis_size(axis))])]
    pallas_call x0 -> x7, Pallas kernels: none -> 16.3 us  [the longest x1 6.82 us: send_product(): pl.pallas_call(functools.partial(send_kernel, plan, groups, block), out_s...]
    scatter x2 -> x0, local copies, waits for them, and re-layouts: 14.9 us -> none  [the longest x1 10.2 us: bucket_tiles(): jnp.full((n_dest, slots), -1, jnp.int32).at[target, place].set(labels)]
    all_to_all x1 -> x0, blocking collectives: 14.8 us -> none  [shards(): lax.all_to_all(buffer, 'col', split_axis=0, concat_axis=0, tiled=True)]
    all_gather x1 -> x0, waiting for transfers between devices: 13.6 us -> none  [shards(): piece_tiles = lax.all_gather(got_tiles[None], 'row', axis=0, tiled=True)]
    all_gather x1 -> x0, blocking collectives: 13.4 us -> none  [shards(): piece_marks = lax.all_gather(got_marks[None], 'row', axis=0, tiled=True)]
  transfers between devices with their start and end apart: 3 -> 20, of which waited for: 3 -> 11; matrix products, arithmetic and copies ran while one was open for 8% -> 0% of each run, Pallas kernels for 0% -> 11%
where the time goes in v2:
time: 81.3 us; the launch traced here: 81.2 us
  waiting for transfers between devices  35.4 us (44%)
  starting transfers between devices  23.4 us (29%)
  Pallas kernels  16.3 us (20%)
  local copies, waits for them, and re-layouts  4.99 us (6%)
  other arithmetic  0.92 us (1%)
    ppermute x20, waiting for transfers between devices, swap(): lax.ppermute(x, axis, [(i, i ^ m) for i in range(lax.axis_size(axis))])  35.4 us
    ppermute x20, starting transfers between devices, swap(): lax.ppermute(x, axis, [(i, i ^ m) for i in range(lax.axis_size(axis))])  23.4 us
    pallas_call x1, Pallas kernels, send_product(): pl.pallas_call(functools.partial(send_kernel, plan, groups, block), out_s...  6.82 us
    pallas_call x3, Pallas kernels, bucket(): pl.pallas_call(functools.partial(bucket_kernel, plan, count), out_shape=[...  6.14 us
    unnamed x6, local copies, waits for them, and re-layouts  4.99 us
    pallas_call x1, Pallas kernels, keep_product(): pl.pallas_call(functools.partial(keep_kernel, plan, block), out_shape=plt...  2.35 us
  transfers between devices with their start and end apart: 20, of which 11 were waited for; matrix products, arithmetic and copies ran while one was open for 0% of the time, Pallas kernels for 11%

profile of v2, /device:TPU:0, one launch (start us, length us, event | category | flops | bytes accessed | tf_op | source)
XLA Modules:
  0.0 81.2 jit_solution(10006935944183609034)
XLA Ops:
  0.0 0.0 copy-start.1
  0.0 0.9 %copy-done.1 = bf16[1,64,16,128]{3,2,1,0:T(8,128)(2,1)S(1)} copy-done((bf16[1,64,16,128]{3,2,1,0:T(8,128)(2,1)S(1)}, bf16[1,64,16,128]{3,2,1,0:T(8,128)(2,1)}, u32[]{:S(2)}) %copy-start.1) | copy-done | bytes 262168
  1.0 0.0 copy-start.2
  1.0 0.7 copy-done.2
  1.6 0.4 pack_tiles.1.rest_0_
  2.0 0.5 collective-permute-start.3
  2.5 2.6 %collective-permute-start = (bf16[1040,128]{1,0:T(8,128)(2,1)S(1)}, bf16[1040,128]{1,0:T(8,128)(2,1)S(1)}, u32[]{:S(2)}, u32[]{:S(2)}) collective-permute-start(bf16[1040,128]{1,0:T(8,128)(2,1)S(1)} %pack_tiles.1.rest_0_), channel_id=1, source_target_pairs={{0,8},{8,0},{16,24},{24,16},{1,9},{9,1},{17,25},{25,17},{2,10},{10... | collective-permute-start | bytes 798728 | tf_op jit(solution)/shard_map/ppermute | solution.py:294
  5.1 2.6 %collective-permute-start.2 = (bf16[1040,128]{1,0:T(8,128)(2,1)S(1)}, bf16[1040,128]{1,0:T(8,128)(2,1)S(1)}, u32[]{:S(2)}, u32[]{:S(2)}) collective-permute-start(bf16[1040,128]{1,0:T(8,128)(2,1)S(1)} %pack_tiles.1.rest_0_), channel_id=1, source_target_pairs={{0,16},{8,24},{16,0},{24,8},{1,17},{9,25},{17,1},{25,9},{2,18},{10... | collective-permute-start | bytes 798728 | tf_op jit(solution)/shard_map/ppermute | solution.py:294
  7.7 0.0 collective-permute-done.3.rest_1_
  7.7 2.1 %bucket_tiles.3 = (bf16[544,128]{1,0:T(8,128)(2,1)S(1)}, bf16[544,128]{1,0:T(8,128)(2,1)S(1)}, bf16[544,128]{1,0:T(8,128)(2,1)S(1)}, bf16[544,128]{1,0:T(8,128)(2,1)S(1)}) custom-call(bf16[1040,128]{1,0:T(8,128)(2,1)S(1)} %pack_tiles.1.rest_0_, bf16[1040,128]{1,0:T(8,128)(2,1)S(1)} %collective-permute-done.3.rest_1_), custom_call_target="tpu_custom_call" | custom-call | bytes 2228224 | tf_op jit(solution)/shard_map/bucket_tiles/pallas_call | solution.py:155
  9.8 1.6 %collective-permute-start.4 = (bf16[544,128]{1,0:T(8,128)(2,1)S(1)}, bf16[544,128]{1,0:T(8,128)(2,1)S(1)}, u32[]{:S(2)}, u32[]{:S(2)}) collective-permute-start(bf16[544,128]{1,0:T(8,128)(2,1)S(1)} %get-tuple-element.33), channel_id=1, source_target_pairs={{0,2},{1,3},{2,0},{3,1},{4,6},{5,7},{6,4},{7,5},{8,10},{9,11},{10,... | collective-permute-start | bytes 417800 | tf_op jit(solution)/shard_map/ppermute | solution.py:294
  11.4 0.0 copy-start
  11.4 3.4 %copy-done = bf16[1024,4096]{1,0:T(8,128)(2,1)S(1)} copy-done((bf16[1024,4096]{1,0:T(8,128)(2,1)S(1)}, bf16[1024,4096]{1,0:T(8,128)(2,1)}, u32[]{:S(2)}) %copy-start) | copy-done | bytes 8388632
  14.7 0.6 stage_integrals.1.rest_12_.cols
  15.4 2.4 %collective-permute-done.rest_0_ = bf16[1040,128]{1,0:T(8,128)(2,1)S(1)} collective-permute-done((bf16[1040,128]{1,0:T(8,128)(2,1)S(1)}, bf16[1040,128]{1,0:T(8,128)(2,1)S(1)}, u32[]{:S(2)}, u32[]{:S(2)}) %collective-permute-start) | collective-permute-done | bytes 266272 | tf_op jit(solution)/shard_map/ppermute | solution.py:294
  17.7 0.0 collective-permute-start.1
  17.7 2.5 %collective-permute-done.2.rest_2_ = bf16[1040,128]{1,0:T(8,128)(2,1)S(1)} collective-permute-done((bf16[1040,128]{1,0:T(8,128)(2,1)S(1)}, bf16[1040,128]{1,0:T(8,128)(2,1)S(1)}, u32[]{:S(2)}, u32[]{:S(2)}) %collective-permute-start.2) | collective-permute-done | bytes 266272 | tf_op jit(solution)/shard_map/ppermute | solution.py:294
  20.3 0.0 collective-permute-done.4.rest_1_
  20.3 0.0 collective-permute-start.5
  20.3 0.5 collective-permute-start.8
  20.7 1.5 %collective-permute-start.6 = (bf16[544,128]{1,0:T(8,128)(2,1)S(1)}, bf16[544,128]{1,0:T(8,128)(2,1)S(1)}, u32[]{:S(2)}, u32[]{:S(2)}) collective-permute-start(bf16[544,128]{1,0:T(8,128)(2,1)S(1)} %get-tuple-element.37), channel_id=1, source_target_pairs={{0,4},{1,5},{2,6},{3,7},{4,0},{5,1},{6,2},{7,3},{8,12},{9,13},{10,... | collective-permute-start | bytes 417800 | tf_op jit(solution)/shard_map/ppermute | solution.py:294
  22.2 1.4 %collective-permute-start.7 = (bf16[544,128]{1,0:T(8,128)(2,1)S(1)}, bf16[544,128]{1,0:T(8,128)(2,1)S(1)}, u32[]{:S(2)}, u32[]{:S(2)}) collective-permute-start(bf16[544,128]{1,0:T(8,128)(2,1)S(1)} %get-tuple-element.38), channel_id=1, source_target_pairs={{0,6},{1,7},{2,4},{3,5},{4,2},{5,3},{6,0},{7,1},{8,14},{9,15},{10,... | collective-permute-start | bytes 417800 | tf_op jit(solution)/shard_map/ppermute | solution.py:294
  23.7 5.8 %collective-permute-done.6.rest_2_ = bf16[544,128]{1,0:T(8,128)(2,1)S(1)} collective-permute-done((bf16[544,128]{1,0:T(8,128)(2,1)S(1)}, bf16[544,128]{1,0:T(8,128)(2,1)S(1)}, u32[]{:S(2)}, u32[]{:S(2)}) %collective-permute-start.6) | collective-permute-done | bytes 139296 | tf_op jit(solution)/shard_map/ppermute | solution.py:294
  29.5 0.0 collective-permute-done.7.rest_3_
  29.5 0.0 collective-permute-done.1.rest_1_
  29.5 0.0 collective-permute-done.5.rest_3_
  29.5 2.0 %bucket_tiles.4 = (bf16[1088,128]{1,0:T(8,128)(2,1)S(1)}, bf16[1088,128]{1,0:T(8,128)(2,1)S(1)}, bf16[1088,128]{1,0:T(8,128)(2,1)S(1)}, bf16[1088,128]{1,0:T(8,128)(2,1)S(1)}) custom-call(bf16[1040,128]{1,0:T(8,128)(2,1)S(1)} %collective-permute-done.rest_0_, bf16[1040,128]{1,0:T(8,128)(2,1)S(1)} %collective-permute-done.1.rest_1_, ...), custom_call_target="tpu_custom_call" | custom-call | bytes 4456448 | tf_op jit(solution)/shard_map/bucket_tiles/pallas_call | solution.py:155
  31.6 1.6 %collective-permute-start.10 = (bf16[1088,128]{1,0:T(8,128)(2,1)S(1)}, bf16[1088,128]{1,0:T(8,128)(2,1)S(1)}, u32[]{:S(2)}, u32[]{:S(2)}) collective-permute-start(bf16[1088,128]{1,0:T(8,128)(2,1)S(1)} %get-tuple-element.49), channel_id=1, source_target_pairs={{0,2},{1,3},{2,0},{3,1},{4,6},{5,7},{6,4},{7,5},{8,10},{9,11},{10,... | collective-permute-start | bytes 835592 | tf_op jit(solution)/shard_map/ppermute | solution.py:294
  33.1 0.0 collective-permute-done.8.rest_0_
  33.1 0.0 collective-permute-start.9
  33.1 1.5 %collective-permute-start.11 = (bf16[1088,128]{1,0:T(8,128)(2,1)S(1)}, bf16[1088,128]{1,0:T(8,128)(2,1)S(1)}, u32[]{:S(2)}, u32[]{:S(2)}) collective-permute-start(bf16[1088,128]{1,0:T(8,128)(2,1)S(1)} %get-tuple-element.50), channel_id=1, source_target_pairs={{0,4},{1,5},{2,6},{3,7},{4,0},{5,1},{6,2},{7,3},{8,12},{9,13},{10,... | collective-permute-start | bytes 835592 | tf_op jit(solution)/shard_map/ppermute | solution.py:294
  34.6 0.5 collective-permute-start.12
  35.1 0.0 collective-permute-done.9.rest_1_
  35.1 2.1 %bucket_tiles.5 = (bf16[544,128]{1,0:T(8,128)(2,1)S(1)}, bf16[544,128]{1,0:T(8,128)(2,1)S(1)}, bf16[544,128]{1,0:T(8,128)(2,1)S(1)}, bf16[544,128]{1,0:T(8,128)(2,1)S(1)}) custom-call(bf16[1040,128]{1,0:T(8,128)(2,1)S(1)} %collective-permute-done.8.rest_0_, bf16[1040,128]{1,0:T(8,128)(2,1)S(1)} %collective-permute-done.9.rest_1_), custom_call_target="tpu_custom_call" | custom-call | bytes 2228224 | tf_op jit(solution)/shard_map/bucket_tiles/pallas_call | solution.py:155
  37.2 1.6 %collective-permute-start.13 = (bf16[544,128]{1,0:T(8,128)(2,1)S(1)}, bf16[544,128]{1,0:T(8,128)(2,1)S(1)}, u32[]{:S(2)}, u32[]{:S(2)}) collective-permute-start(bf16[544,128]{1,0:T(8,128)(2,1)S(1)} %get-tuple-element.55), channel_id=1, source_target_pairs={{0,2},{1,3},{2,0},{3,1},{4,6},{5,7},{6,4},{7,5},{8,10},{9,11},{10,... | collective-permute-start | bytes 417800 | tf_op jit(solution)/shard_map/ppermute | solution.py:294
  38.7 1.5 %collective-permute-start.14 = (bf16[544,128]{1,0:T(8,128)(2,1)S(1)}, bf16[544,128]{1,0:T(8,128)(2,1)S(1)}, u32[]{:S(2)}, u32[]{:S(2)}) collective-permute-start(bf16[544,128]{1,0:T(8,128)(2,1)S(1)} %get-tuple-element.56), channel_id=1, source_target_pairs={{0,4},{1,5},{2,6},{3,7},{4,0},{5,1},{6,2},{7,3},{8,12},{9,13},{10,... | collective-permute-start | bytes 417800 | tf_op jit(solution)/shard_map/ppermute | solution.py:294
  40.3 1.0 %collective-permute-done.10.rest_5_ = bf16[1088,128]{1,0:T(8,128)(2,1)S(1)} collective-permute-done((bf16[1088,128]{1,0:T(8,128)(2,1)S(1)}, bf16[1088,128]{1,0:T(8,128)(2,1)S(1)}, u32[]{:S(2)}, u32[]{:S(2)}) %collective-permute-start.10) | collective-permute-done | bytes 278560 | tf_op jit(solution)/shard_map/ppermute | solution.py:294
  41.2 2.4 %collective-permute-start.15 = (bf16[544,128]{1,0:T(8,128)(2,1)S(1)}, bf16[544,128]{1,0:T(8,128)(2,1)S(1)}, u32[]{:S(2)}, u32[]{:S(2)}) collective-permute-start(bf16[544,128]{1,0:T(8,128)(2,1)S(1)} %get-tuple-element.57), channel_id=1, source_target_pairs={{0,6},{1,7},{2,4},{3,5},{4,2},{5,3},{6,0},{7,1},{8,14},{9,15},{10,... | collective-permute-start | bytes 417800 | tf_op jit(solution)/shard_map/ppermute | solution.py:294
  43.7 5.5 %collective-permute-done.11.rest_6_ = bf16[1088,128]{1,0:T(8,128)(2,1)S(1)} collective-permute-done((bf16[1088,128]{1,0:T(8,128)(2,1)S(1)}, bf16[1088,128]{1,0:T(8,128)(2,1)S(1)}, u32[]{:S(2)}, u32[]{:S(2)}) %collective-permute-start.11) | collective-permute-done | bytes 278560 | tf_op jit(solution)/shard_map/ppermute | solution.py:294
  49.2 0.0 collective-permute-done.12.rest_7_
  49.2 0.9 %collective-permute-done.13.rest_9_ = bf16[544,128]{1,0:T(8,128)(2,1)S(1)} collective-permute-done((bf16[544,128]{1,0:T(8,128)(2,1)S(1)}, bf16[544,128]{1,0:T(8,128)(2,1)S(1)}, u32[]{:S(2)}, u32[]{:S(2)}) %collective-permute-start.13) | collective-permute-done | bytes 139296 | tf_op jit(solution)/shard_map/ppermute | solution.py:294
  50.1 4.0 %collective-permute-done.14.rest_10_ = bf16[544,128]{1,0:T(8,128)(2,1)S(1)} collective-permute-done((bf16[544,128]{1,0:T(8,128)(2,1)S(1)}, bf16[544,128]{1,0:T(8,128)(2,1)S(1)}, u32[]{:S(2)}, u32[]{:S(2)}) %collective-permute-start.14) | collective-permute-done | bytes 139296 | tf_op jit(solution)/shard_map/ppermute | solution.py:294
  54.1 0.0 collective-permute-done.15.rest_11_
  54.1 6.8 %place_and_multiply.1 = (bf16[528,4096]{1,0:T(8,128)(2,1)S(1)}, f32[256,1024]{1,0:T(8,128)S(1)}) custom-call(bf16[544,128]{1,0:T(8,128)(2,1)S(1)} %get-tuple-element.39.rest_0_, bf16[544,128]{1,0:T(8,128)(2,1)S(1)} %collective-permute-done.4.rest_1_, bf16[544,128]{1,0:T(8,128)(2,1)S(1)} %collective-permute-done.6.rest_2_, ...), custom_call_target="tpu_custom_call" | custom-call | flops 4294967296 | bytes 16777216 | tf_op jit(solution)/shard_map/place_and_multiply/pallas_call | solution.py:255
  61.0 0.1 collective-permute-start.16
  61.0 2.4 %multiply_kept.1 = f32[256,1024]{1,0:T(8,128)S(1)} custom-call(bf16[528,4096]{1,0:T(8,128)(2,1)S(1)} %get-tuple-element.59.lam, bf16[1024,4096]{1,0:T(8,128)(2,1)S(1)} %stage_integrals.1.rest_12_.cols), custom_call_target="tpu_custom_call" | custom-call | flops 2147483648 | bytes 10485760 | tf_op jit(solution)/shard_map/multiply_kept/pallas_call | solution.py:282
  63.4 0.3 collective-permute-done.16
  63.7 0.1 slice_add_fusion.2
  63.8 0.6 collective-permute-start.17
  64.4 2.4 %collective-permute-start.19 = (f32[64,1024]{1,0:T(8,128)S(1)}, f32[64,1024]{1,0:T(8,128)S(1)}, u32[]{:S(2)}, u32[]{:S(2)}) collective-permute-start(f32[64,1024]{1,0:T(8,128)S(1)} %get-tuple-element.62), channel_id=1, source_target_pairs={{0,6},{1,7},{2,4},{3,5},{4,2},{5,3},{6,0},{7,1},{8,14},{9,15},{10,... | collective-permute-start | bytes 786440 | tf_op jit(solution)/shard_map/ppermute | solution.py:294
  66.9 0.5 collective-permute-start.18
  67.4 5.7 %collective-permute-done.17 = f32[64,1024]{1,0:T(8,128)S(1)} collective-permute-done((f32[64,1024]{1,0:T(8,128)S(1)}, f32[64,1024]{1,0:T(8,128)S(1)}, u32[]{:S(2)}, u32[]{:S(2)}) %collective-permute-start.17) | collective-permute-done | bytes 262176 | tf_op jit(solution)/shard_map/ppermute | solution.py:294
  73.0 6.0 %collective-permute-done.19 = f32[64,1024]{1,0:T(8,128)S(1)} collective-permute-done((f32[64,1024]{1,0:T(8,128)S(1)}, f32[64,1024]{1,0:T(8,128)S(1)}, u32[]{:S(2)}, u32[]{:S(2)}) %collective-permute-start.19) | collective-permute-done | bytes 262176 | tf_op jit(solution)/shard_map/ppermute | solution.py:294
  79.0 1.4 %collective-permute-done.18 = f32[64,1024]{1,0:T(8,128)S(1)} collective-permute-done((f32[64,1024]{1,0:T(8,128)S(1)}, f32[64,1024]{1,0:T(8,128)S(1)}, u32[]{:S(2)}, u32[]{:S(2)}) %collective-permute-start.18) | collective-permute-done | bytes 262176 | tf_op jit(solution)/shard_map/ppermute | solution.py:294
  80.3 0.8 fusion.3
Async XLA Ops:
  0.0 0.9 %copy-start.1 = (bf16[1,64,16,128]{3,2,1,0:T(8,128)(2,1)S(1)}, bf16[1,64,16,128]{3,2,1,0:T(8,128)(2,1)}, u32[]{:S(2)}) copy-start(bf16[1,64,16,128]{3,2,1,0:T(8,128)(2,1)} %param.3) | copy-start | bytes 786436
  1.0 0.7 copy-start.2
  2.0 5.8 %collective-permute-start.3 = (bf16[1040,128]{1,0:T(8,128)(2,1)S(1)}, bf16[1040,128]{1,0:T(8,128)(2,1)S(1)}, u32[]{:S(2)}, u32[]{:S(2)}) collective-permute-start(bf16[1040,128]{1,0:T(8,128)(2,1)S(1)} %pack_tiles.1.rest_0_), channel_id=1, source_target_pairs={{0,1},{1,0},{2,3},{3,2},{4,5},{5,4},{6,7},{7,6},{8,9},{9,8},{10,11... | collective-permute-start | bytes 798728 | tf_op jit(solution)/shard_map/ppermute | solution.py:294
  2.5 15.2 %collective-permute-start = (bf16[1040,128]{1,0:T(8,128)(2,1)S(1)}, bf16[1040,128]{1,0:T(8,128)(2,1)S(1)}, u32[]{:S(2)}, u32[]{:S(2)}) collective-permute-start(bf16[1040,128]{1,0:T(8,128)(2,1)S(1)} %pack_tiles.1.rest_0_), channel_id=1, source_target_pairs={{0,8},{8,0},{16,24},{24,16},{1,9},{9,1},{17,25},{25,17},{2,10},{10... | collective-permute-start | bytes 798728 | tf_op jit(solution)/shard_map/ppermute | solution.py:294
  5.1 15.1 %collective-permute-start.2 = (bf16[1040,128]{1,0:T(8,128)(2,1)S(1)}, bf16[1040,128]{1,0:T(8,128)(2,1)S(1)}, u32[]{:S(2)}, u32[]{:S(2)}) collective-permute-start(bf16[1040,128]{1,0:T(8,128)(2,1)S(1)} %pack_tiles.1.rest_0_), channel_id=1, source_target_pairs={{0,16},{8,24},{16,0},{24,8},{1,17},{9,25},{17,1},{25,9},{2,18},{10... | collective-permute-start | bytes 798728 | tf_op jit(solution)/shard_map/ppermute | solution.py:294
  9.8 10.5 %collective-permute-start.4 = (bf16[544,128]{1,0:T(8,128)(2,1)S(1)}, bf16[544,128]{1,0:T(8,128)(2,1)S(1)}, u32[]{:S(2)}, u32[]{:S(2)}) collective-permute-start(bf16[544,128]{1,0:T(8,128)(2,1)S(1)} %get-tuple-element.33), channel_id=1, source_target_pairs={{0,2},{1,3},{2,0},{3,1},{4,6},{5,7},{6,4},{7,5},{8,10},{9,11},{10,... | collective-permute-start | bytes 417800 | tf_op jit(solution)/shard_map/ppermute | solution.py:294
  11.4 3.4 %copy-start = (bf16[1024,4096]{1,0:T(8,128)(2,1)S(1)}, bf16[1024,4096]{1,0:T(8,128)(2,1)}, u32[]{:S(2)}) copy-start(bf16[1024,4096]{1,0:T(8,128)(2,1)} %source.1) | copy-start | bytes 25165828
  17.7 11.8 %collective-permute-start.1 = (bf16[1040,128]{1,0:T(8,128)(2,1)S(1)}, bf16[1040,128]{1,0:T(8,128)(2,1)S(1)}, u32[]{:S(2)}, u32[]{:S(2)}) collective-permute-start(bf16[1040,128]{1,0:T(8,128)(2,1)S(1)} %collective-permute-done.rest_0_), channel_id=1, source_target_pairs={{0,1},{1,0},{2,3},{3,2},{4,5},{5,4},{6,7},{7,6},{8,9},{9,8},{10,11... | collective-permute-start | bytes 798728 | tf_op jit(solution)/shard_map/ppermute | solution.py:294
  20.3 9.3 %collective-permute-start.5 = (bf16[1040,128]{1,0:T(8,128)(2,1)S(1)}, bf16[1040,128]{1,0:T(8,128)(2,1)S(1)}, u32[]{:S(2)}, u32[]{:S(2)}) collective-permute-start(bf16[1040,128]{1,0:T(8,128)(2,1)S(1)} %collective-permute-done.2.rest_2_), channel_id=1, source_target_pairs={{0,1},{1,0},{2,3},{3,2},{4,5},{5,4},{6,7},{7,6},{8,9},{9,8},{10,11... | collective-permute-start | bytes 798728 | tf_op jit(solution)/shard_map/ppermute | solution.py:294
  20.3 12.8 %collective-permute-start.8 = (bf16[1040,128]{1,0:T(8,128)(2,1)S(1)}, bf16[1040,128]{1,0:T(8,128)(2,1)S(1)}, u32[]{:S(2)}, u32[]{:S(2)}) collective-permute-start(bf16[1040,128]{1,0:T(8,128)(2,1)S(1)} %collective-permute-done.2.rest_2_), channel_id=1, source_target_pairs={{0,8},{8,0},{16,24},{24,16},{1,9},{9,1},{17,25},{25,17},{2,10},{10... | collective-permute-start | bytes 798728 | tf_op jit(solution)/shard_map/ppermute | solution.py:294
  20.7 8.8 %collective-permute-start.6 = (bf16[544,128]{1,0:T(8,128)(2,1)S(1)}, bf16[544,128]{1,0:T(8,128)(2,1)S(1)}, u32[]{:S(2)}, u32[]{:S(2)}) collective-permute-start(bf16[544,128]{1,0:T(8,128)(2,1)S(1)} %get-tuple-element.37), channel_id=1, source_target_pairs={{0,4},{1,5},{2,6},{3,7},{4,0},{5,1},{6,2},{7,3},{8,12},{9,13},{10,... | collective-permute-start | bytes 417800 | tf_op jit(solution)/shard_map/ppermute | solution.py:294
  22.2 7.3 %collective-permute-start.7 = (bf16[544,128]{1,0:T(8,128)(2,1)S(1)}, bf16[544,128]{1,0:T(8,128)(2,1)S(1)}, u32[]{:S(2)}, u32[]{:S(2)}) collective-permute-start(bf16[544,128]{1,0:T(8,128)(2,1)S(1)} %get-tuple-element.38), channel_id=1, source_target_pairs={{0,6},{1,7},{2,4},{3,5},{4,2},{5,3},{6,0},{7,1},{8,14},{9,15},{10,... | collective-permute-start | bytes 417800 | tf_op jit(solution)/shard_map/ppermute | solution.py:294
  31.6 9.7 %collective-permute-start.10 = (bf16[1088,128]{1,0:T(8,128)(2,1)S(1)}, bf16[1088,128]{1,0:T(8,128)(2,1)S(1)}, u32[]{:S(2)}, u32[]{:S(2)}) collective-permute-start(bf16[1088,128]{1,0:T(8,128)(2,1)S(1)} %get-tuple-element.49), channel_id=1, source_target_pairs={{0,2},{1,3},{2,0},{3,1},{4,6},{5,7},{6,4},{7,5},{8,10},{9,11},{10,... | collective-permute-start | bytes 835592 | tf_op jit(solution)/shard_map/ppermute | solution.py:294
  33.1 2.0 %collective-permute-start.9 = (bf16[1040,128]{1,0:T(8,128)(2,1)S(1)}, bf16[1040,128]{1,0:T(8,128)(2,1)S(1)}, u32[]{:S(2)}, u32[]{:S(2)}) collective-permute-start(bf16[1040,128]{1,0:T(8,128)(2,1)S(1)} %collective-permute-done.8.rest_0_), channel_id=1, source_target_pairs={{0,1},{1,0},{2,3},{3,2},{4,5},{5,4},{6,7},{7,6},{8,9},{9,8},{10,11... | collective-permute-start | bytes 798728 | tf_op jit(solution)/shard_map/ppermute | solution.py:294
  33.1 16.0 %collective-permute-start.11 = (bf16[1088,128]{1,0:T(8,128)(2,1)S(1)}, bf16[1088,128]{1,0:T(8,128)(2,1)S(1)}, u32[]{:S(2)}, u32[]{:S(2)}) collective-permute-start(bf16[1088,128]{1,0:T(8,128)(2,1)S(1)} %get-tuple-element.50), channel_id=1, source_target_pairs={{0,4},{1,5},{2,6},{3,7},{4,0},{5,1},{6,2},{7,3},{8,12},{9,13},{10,... | collective-permute-start | bytes 835592 | tf_op jit(solution)/shard_map/ppermute | solution.py:294
  34.6 14.5 %collective-permute-start.12 = (bf16[1088,128]{1,0:T(8,128)(2,1)S(1)}, bf16[1088,128]{1,0:T(8,128)(2,1)S(1)}, u32[]{:S(2)}, u32[]{:S(2)}) collective-permute-start(bf16[1088,128]{1,0:T(8,128)(2,1)S(1)} %get-tuple-element.51), channel_id=1, source_target_pairs={{0,6},{1,7},{2,4},{3,5},{4,2},{5,3},{6,0},{7,1},{8,14},{9,15},{10,... | collective-permute-start | bytes 835592 | tf_op jit(solution)/shard_map/ppermute | solution.py:294
  37.2 12.9 %collective-permute-start.13 = (bf16[544,128]{1,0:T(8,128)(2,1)S(1)}, bf16[544,128]{1,0:T(8,128)(2,1)S(1)}, u32[]{:S(2)}, u32[]{:S(2)}) collective-permute-start(bf16[544,128]{1,0:T(8,128)(2,1)S(1)} %get-tuple-element.55), channel_id=1, source_target_pairs={{0,2},{1,3},{2,0},{3,1},{4,6},{5,7},{6,4},{7,5},{8,10},{9,11},{10,... | collective-permute-start | bytes 417800 | tf_op jit(solution)/shard_map/ppermute | solution.py:294
  38.7 15.4 %collective-permute-start.14 = (bf16[544,128]{1,0:T(8,128)(2,1)S(1)}, bf16[544,128]{1,0:T(8,128)(2,1)S(1)}, u32[]{:S(2)}, u32[]{:S(2)}) collective-permute-start(bf16[544,128]{1,0:T(8,128)(2,1)S(1)} %get-tuple-element.56), channel_id=1, source_target_pairs={{0,4},{1,5},{2,6},{3,7},{4,0},{5,1},{6,2},{7,3},{8,12},{9,13},{10,... | collective-permute-start | bytes 417800 | tf_op jit(solution)/shard_map/ppermute | solution.py:294
  41.2 12.9 %collective-permute-start.15 = (bf16[544,128]{1,0:T(8,128)(2,1)S(1)}, bf16[544,128]{1,0:T(8,128)(2,1)S(1)}, u32[]{:S(2)}, u32[]{:S(2)}) collective-permute-start(bf16[544,128]{1,0:T(8,128)(2,1)S(1)} %get-tuple-element.57), channel_id=1, source_target_pairs={{0,6},{1,7},{2,4},{3,5},{4,2},{5,3},{6,0},{7,1},{8,14},{9,15},{10,... | collective-permute-start | bytes 417800 | tf_op jit(solution)/shard_map/ppermute | solution.py:294
  61.0 2.7 %collective-permute-start.16 = (f32[256,1024]{1,0:T(8,128)S(1)}, f32[256,1024]{1,0:T(8,128)S(1)}, u32[]{:S(2)}, u32[]{:S(2)}) collective-permute-start(f32[256,1024]{1,0:T(8,128)S(1)} %get-tuple-element.60), channel_id=1, source_target_pairs={{0,1},{1,0},{2,3},{3,2},{4,5},{5,4},{6,7},{7,6},{8,9},{9,8},{10,11... | collective-permute-start | bytes 3145736 | tf_op jit(solution)/shard_map/ppermute | solution.py:294
  63.8 9.2 %collective-permute-start.17 = (f32[64,1024]{1,0:T(8,128)S(1)}, f32[64,1024]{1,0:T(8,128)S(1)}, u32[]{:S(2)}, u32[]{:S(2)}) collective-permute-start(f32[64,1024]{1,0:T(8,128)S(1)} %get-tuple-element.61), channel_id=1, source_target_pairs={{0,2},{1,3},{2,0},{3,1},{4,6},{5,7},{6,4},{7,5},{8,10},{9,11},{10,... | collective-permute-start | bytes 786440 | tf_op jit(solution)/shard_map/ppermute | solution.py:294
  64.4 14.6 %collective-permute-start.19 = (f32[64,1024]{1,0:T(8,128)S(1)}, f32[64,1024]{1,0:T(8,128)S(1)}, u32[]{:S(2)}, u32[]{:S(2)}) collective-permute-start(f32[64,1024]{1,0:T(8,128)S(1)} %get-tuple-element.62), channel_id=1, source_target_pairs={{0,6},{1,7},{2,4},{3,5},{4,2},{5,3},{6,0},{7,1},{8,14},{9,15},{10,... | collective-permute-start | bytes 786440 | tf_op jit(solution)/shard_map/ppermute | solution.py:294
  66.9 13.5 %collective-permute-start.18 = (f32[64,1024]{1,0:T(8,128)S(1)}, f32[64,1024]{1,0:T(8,128)S(1)}, u32[]{:S(2)}, u32[]{:S(2)}) collective-permute-start(f32[64,1024]{1,0:T(8,128)S(1)} %get-tuple-element.63), channel_id=1, source_target_pairs={{0,4},{1,5},{2,6},{3,7},{4,0},{5,1},{6,2},{7,3},{8,12},{9,13},{10,... | collective-permute-start | bytes 786440 | tf_op jit(solution)/shard_map/ppermute | solution.py:294

commit v3 on v2

--- a/solution.py
+++ b/solution.py
@@ -99,8 +99,7 @@
 
 
 def bucket_kernel(plan, count, *rest):
-    packed, outs = rest[:count], rest[count : count + plan.n_pair]
-    bodies, tops, buf, heads, line, places, sem = rest[count + plan.n_pair :]
+    packed, (buf, bodies, tops, heads, line, places, sem) = rest[:count], rest[count:]
     rows, piece = plan.pairs, count * plan.bucket
     loads = []
     for i, ref in enumerate(packed):
@@ -138,13 +137,6 @@
             return 0
 
         lax.fori_loop(0, plan.slots, step, 0, unroll=16)
-    copies = []
-    for i, out in enumerate(outs):
-        part = buf.at[pl.ds(i * piece, piece)]
-        copies.append(pltpu.make_async_copy(part, out, sem.at[2 * count + 1 + i]))
-        copies[-1].start()
-    for copy in copies:
-        copy.wait()
 
 
 def bucket(plan, packed):
@@ -152,24 +144,24 @@
     piece = count * plan.bucket
     lines = -(-count // 8) * 8
     bf16 = jnp.bfloat16
-    return pl.pallas_call(
+    out = pl.pallas_call(
         functools.partial(bucket_kernel, plan, count),
-        out_shape=[jax.ShapeDtypeStruct((piece, plan.tile), bf16)] * plan.n_pair,
+        out_shape=pltpu.VMEM((plan.n_pair * piece + plan.pairs, plan.tile), bf16),
         in_specs=[HBM] * count,
-        out_specs=[HBM] * plan.n_pair,
+        out_specs=VMEM,
         scratch_shapes=[
             pltpu.VMEM((count * plan.body, plan.tile), bf16),
             pltpu.VMEM((count * plan.head, plan.tile), bf16),
-            pltpu.VMEM((plan.n_pair * piece + plan.pairs, plan.tile), bf16),
             pltpu.VMEM((count * plan.head, plan.tile), jnp.float32),
             pltpu.VMEM((lines, plan.tile), jnp.int32),
             pltpu.SMEM((lines, plan.tile), jnp.int32),
-            pltpu.SemaphoreType.DMA((2 * count + 1 + plan.n_pair,)),
+            pltpu.SemaphoreType.DMA((2 * count + 1,)),
         ],
-        compiler_params=pltpu.CompilerParams(vmem_limit_bytes=20 * 1024 * 1024),
+        compiler_params=pltpu.CompilerParams(vmem_limit_bytes=12 * 1024 * 1024),
         cost_estimate=cost(plan, 4 * plan.n_pair * piece * plan.tile * 2),
         name="bucket_tiles",
     )(*packed)
+    return [out[i * piece : (i + 1) * piece] for i in range(plan.n_pair)]
 
 
 def stage_kernel(steps, block, source, out, sem):
@@ -196,24 +188,19 @@
     )(integrals)
 
 
-def send_kernel(plan, groups, block, *rest):
-    n_in = len(groups) * plan.n_pair
-    parts, rest = rest[:n_in], rest[n_in:]
-    cols, lam, send, tiles, line, places, sem, part_sem = rest
+def place(plan, planes, parts, lam, tiles, line, places, sem, part_sem):
     rows = plan.pairs
     half = plan.n_pair * plan.owned
     sources, loads, at = [], [], 0
-    for g, planes in enumerate(groups):
-        for chip in range(plan.n_pair):
-            ref = parts[g * plan.n_pair + chip]
-            to = tiles.at[pl.ds(at, ref.shape[0])]
-            loads.append(pltpu.make_async_copy(ref, to, part_sem.at[len(loads)]))
-            loads[-1].start()
-            for d in planes:
+    for ref, (chips, ds) in zip(parts, planes, strict=True):
+        loads.append(pltpu.make_async_copy(ref, tiles.at[pl.ds(at, ref.shape[0])], part_sem.at[len(loads)]))
+        loads[-1].start()
+        for chip in chips:
+            for d in ds:
                 for side in range(2):
                     sources.append((at, d, 2 * chip + side))
                     at += plan.bucket
-    lam[...] = jnp.zeros(lam.shape, lam.dtype)
+    yield
     for load in loads:
         load.wait()
     for i, (base, _, _) in enumerate(sources):
@@ -234,7 +221,67 @@
             at = pl.multiple_of((at & (plan.kt - 1)) * plan.tile, plan.tile)
             tile = tiles[base + s * rows : base + (s + 1) * rows, :]
             lam[pl.ds(line_at, rows), pl.ds(at, plan.tile)] = tile
-    multiply(plan, block, lam, half, cols, send)
+    yield
+
+
+def place_scratch(plan, planes):
+    count = sum(2 * len(chips) * len(ds) for chips, ds in planes)
+    lines = -(-count // 8) * 8
+    return [
+        pltpu.VMEM((count * plan.bucket, plan.tile), jnp.bfloat16),
+        pltpu.VMEM((lines, plan.tile), jnp.int32),
+        pltpu.SMEM((lines, plan.tile), jnp.int32),
+        pltpu.SemaphoreType.DMA,
+        pltpu.SemaphoreType.DMA((len(planes),)),
+    ]
+
+
+def lam_shape(plan):
+    return pltpu.VMEM((2 * plan.n_pair * plan.owned + plan.pairs, plan.cd), jnp.bfloat16)
+
+
+def early_kernel(plan, planes, *rest):
+    parts, (lam, *scratch) = rest[: len(planes)], rest[len(planes) :]
+    placing = place(plan, planes, parts, lam, *scratch)
+    next(placing)
+    lam[...] = jnp.zeros(lam.shape, lam.dtype)
+    next(placing)
+
+
+def place_early(plan, planes, parts):
+    return pl.pallas_call(
+        functools.partial(early_kernel, plan, planes),
+        out_shape=lam_shape(plan),
+        in_specs=[HBM] * len(parts),
+        out_specs=VMEM,
+        scratch_shapes=place_scratch(plan, planes),
+        compiler_params=pltpu.CompilerParams(vmem_limit_bytes=12 * 1024 * 1024),
+        cost_estimate=cost(plan, 8 * 1024 * 1024),
+        name="place_early",
+    )(*parts)
+
+
+def send_kernel(plan, planes, block, _, cols, *rest):
+    parts, (lam, send, *scratch) = rest[: len(planes)], rest[len(planes) :]
+    placing = place(plan, planes, parts, lam, *scratch)
+    next(placing)
+    next(placing)
+    multiply(plan, block, lam, plan.n_pair * plan.owned, cols, send)
+
+
+def send_product(plan, lam, planes, parts, integrals, block=256):
+    half = plan.n_pair * plan.owned
+    return pl.pallas_call(
+        functools.partial(send_kernel, plan, planes, block),
+        out_shape=[lam_shape(plan), pltpu.VMEM((half, plan.ab), jnp.float32)],
+        in_specs=[VMEM, VMEM] + [HBM] * len(parts),
+        out_specs=[VMEM, VMEM],
+        input_output_aliases={0: 0},
+        scratch_shapes=place_scratch(plan, planes),
+        compiler_params=pltpu.CompilerParams(vmem_limit_bytes=20 * 1024 * 1024),
+        cost_estimate=cost(plan, plan.ab * plan.cd * 4, 4 * half * plan.ab * plan.cd),
+        name="place_and_multiply",
+    )(lam, integrals, *parts)
 
 
 def multiply(plan, block, lam, first, cols, out):
@@ -247,32 +294,6 @@
         )
 
 
-def send_product(plan, groups, parts, integrals, block=256):
-    half = plan.n_pair * plan.owned
-    n_src = plan.n_row * plan.n_col
-    flat = [part for group in parts for part in group]
-    bf16 = jnp.bfloat16
-    return pl.pallas_call(
-        functools.partial(send_kernel, plan, groups, block),
-        out_shape=[
-            pltpu.VMEM((2 * half + plan.pairs, plan.cd), bf16),
-            pltpu.VMEM((half, plan.ab), jnp.float32),
-        ],
-        in_specs=[HBM] * len(flat) + [VMEM],
-        out_specs=[VMEM, VMEM],
-        scratch_shapes=[
-            pltpu.VMEM((n_src * plan.bucket, plan.tile), bf16),
-            pltpu.VMEM((n_src, plan.tile), jnp.int32),
-            pltpu.SMEM((n_src, plan.tile), jnp.int32),
-            pltpu.SemaphoreType.DMA,
-            pltpu.SemaphoreType.DMA((len(flat),)),
-        ],
-        compiler_params=pltpu.CompilerParams(vmem_limit_bytes=28 * 1024 * 1024),
-        cost_estimate=cost(plan, plan.ab * plan.cd * 4, 4 * half * plan.ab * plan.cd),
-        name="place_and_multiply",
-    )(*flat, integrals)
-
-
 def keep_kernel(plan, block, lam, cols, out):
     multiply(plan, block, lam, 0, cols, out)
 
@@ -297,30 +318,29 @@
 def shards(lam_tiles, lam_ids, integrals):
     plan = Plan(lam_tiles, integrals)
     packed = pack(plan, lam_ids, lam_tiles.reshape(plan.body, plan.tile))
-    groups = [[0], list(range(1, plan.n_row - 1)), [plan.n_row - 1]]
-    parts = []
-
-    def spread(planes):
-        raws = [raw for d in planes for raw in (arrived[d], swap(arrived[d], "col", 1))]
-        if len(parts) == 1:
-            *raws, parts[0] = lax.optimization_barrier((*raws, parts[0]))
-        elif parts:
-            *raws, parts[-1][0] = lax.optimization_barrier((*raws, parts[-1][0]))
-        out = bucket(plan, raws)
-        parts.append([out[0]] + [swap(out[m], "col", 2 * m) for m in range(1, plan.n_pair)])
-
-    arrived = {0: packed}
+    chips = range(plan.n_pair)
+
+    def spread(ds):
+        out = bucket(plan, [raw for d in ds for raw in (arrived[d], swap(arrived[d], "col", 1))])
+        return [out[0]] + [swap(out[m], "col", 2 * m) for m in range(1, plan.n_pair)]
+
     bit = plan.n_row // 2
-    arrived[bit] = swap(packed, "row", bit)
-    spread(groups[0])
+    arrived = {0: packed, bit: swap(packed, "row", bit)}
+    own = spread([0])
     staged = stage(plan, integrals)
-    arrived[bit], parts[0][1], staged = lax.optimization_barrier((arrived[bit], parts[0][1], staged))
+    arrived[bit], own, staged = lax.optimization_barrier((arrived[bit], own, staged))
     while bit > 1:
         bit //= 2
-        arrived.update({d | bit: swap(raw, "row", bit) for d, raw in arrived.items()})
-    for group in groups[1:]:
-        spread(group)
-    lam, send = send_product(plan, groups, parts, staged)
+        arrived.update({d | bit: swap(raw, "row", bit) for d, raw in arrived.items() if d or bit > 1})
+    *middle, last = sorted(arrived)[1:]
+    early = spread(middle)
+    arrived[last], early[0], own[0] = lax.optimization_barrier((arrived[last], early[0], own[0]))
+    near = swap(jnp.concatenate(own, axis=0), "row", 1)
+    late = spread([last])
+    planes = [((chip,), (0,)) for chip in chips] + [((chip,), tuple(middle)) for chip in chips]
+    lam = place_early(plan, planes, own + early)
+    planes = [(chips, (1,))] + [((chip,), (last,)) for chip in chips]
+    lam, send = send_product(plan, lam, planes, [near] + late, staged)
     got = swap(send, "col", 1)
     keep = keep_product(plan, lam, staged)
     both = [

time: 81.3 us -> 69.5 us (0.85)
  waiting for transfers between devices: 35.4 us -> 26 us
  Pallas kernels: 16.3 us -> 14.9 us
  starting transfers between devices: 23.4 us -> 22.2 us
    ppermute x20 -> x19, waiting for transfers between devices: 35.4 us -> 26 us  [swap(): lax.ppermute(x, axis, [(i, i ^ m) for i in range(lax.axis_size(axis))])]
    pallas_call x4 -> x5, Pallas kernels: 13 us -> 11.6 us  [the longest x1 4.69 us: send_product(): pl.pallas_call(functools.partial(send_kernel, plan, planes, block), out_s...]
    ppermute x20 -> x19, starting transfers between devices: 23.4 us -> 22.2 us  [swap(): lax.ppermute(x, axis, [(i, i ^ m) for i in range(lax.axis_size(axis))])]
  transfers between devices with their start and end apart: 20 -> 19, of which waited for: 11 -> 10; matrix products, arithmetic and copies ran while one was open for 0% -> 0% of each run, Pallas kernels for 11% -> 14%
where the time goes in v3:
time: 69.5 us; the launch traced here: 69.4 us
  waiting for transfers between devices  26 us (37%)
  starting transfers between devices  22.2 us (32%)
  Pallas kernels  14.9 us (21%)
  local copies, waits for them, and re-layouts  5.1 us (7%)
  other arithmetic  0.96 us (1%)
    ppermute x19, waiting for transfers between devices, swap(): lax.ppermute(x, axis, [(i, i ^ m) for i in range(lax.axis_size(axis))])  26 us
    ppermute x19, starting transfers between devices, swap(): lax.ppermute(x, axis, [(i, i ^ m) for i in range(lax.axis_size(axis))])  22.2 us
    unnamed x6, local copies, waits for them, and re-layouts  4.99 us
    pallas_call x1, Pallas kernels, send_product(): pl.pallas_call(functools.partial(send_kernel, plan, planes, block), out_s...  4.69 us
    pallas_call x3, Pallas kernels, bucket(): pl.pallas_call(functools.partial(bucket_kernel, plan, count), out_shape=p...  3.45 us
    pallas_call x1, Pallas kernels, place_early(): pl.pallas_call(functools.partial(early_kernel, plan, planes), out_shape=l...  3.45 us
    pallas_call x1, Pallas kernels, keep_product(): pl.pallas_call(functools.partial(keep_kernel, plan, block), out_shape=plt...  2.35 us
  transfers between devices with their start and end apart: 19, of which 10 were waited for; matrix products, arithmetic and copies ran while one was open for 0% of the time, Pallas kernels for 14%

profile of v3, /device:TPU:0, one launch (start us, length us, event | category | flops | bytes accessed | tf_op | source)
XLA Modules:
  0.0 69.4 jit_solution(15980092940329297961)
XLA Ops:
  0.0 0.0 copy-start.1
  0.0 0.9 %copy-done.1 = bf16[1,64,16,128]{3,2,1,0:T(8,128)(2,1)S(1)} copy-done((bf16[1,64,16,128]{3,2,1,0:T(8,128)(2,1)S(1)}, bf16[1,64,16,128]{3,2,1,0:T(8,128)(2,1)}, u32[]{:S(2)}) %copy-start.1) | copy-done | bytes 262168
  1.0 0.0 copy-start.2
  1.0 0.7 copy-done.2
  1.6 0.4 pack_tiles.1.rest_0_
  2.0 0.5 collective-permute-start.1
  2.5 3.7 %collective-permute-start = (bf16[1040,128]{1,0:T(8,128)(2,1)S(1)}, bf16[1040,128]{1,0:T(8,128)(2,1)S(1)}, u32[]{:S(2)}, u32[]{:S(2)}) collective-permute-start(bf16[1040,128]{1,0:T(8,128)(2,1)S(1)} %pack_tiles.1.rest_0_), channel_id=1, source_target_pairs={{0,16},{8,24},{16,0},{24,8},{1,17},{9,25},{17,1},{25,9},{2,18},{10... | collective-permute-start | bytes 798728 | tf_op jit(solution)/shard_map/ppermute | solution.py:315
  6.2 0.0 collective-permute-done.1.rest_1_
  6.2 1.2 %bucket_tiles.3 = bf16[2192,128]{1,0:T(8,128)(2,1)S(1)} custom-call(bf16[1040,128]{1,0:T(8,128)(2,1)S(1)} %pack_tiles.1.rest_0_, bf16[1040,128]{1,0:T(8,128)(2,1)S(1)} %collective-permute-done.1.rest_1_), custom_call_target="tpu_custom_call" | custom-call | bytes 2228224 | tf_op jit(solution)/shard_map/bucket_tiles/pallas_call | solution.py:147
  7.4 2.5 %collective-permute-start.4 = (bf16[544,128]{1,0:T(8,128)(2,1)S(1)}, bf16[544,128]{1,0:T(8,128)(2,1)S(1)}, u32[]{:S(2)}, u32[]{:S(2)}) collective-permute-start(bf16[544,128]{1,0:T(8,128)(2,1)S(1)} %get-tuple-element.38), channel_id=1, source_target_pairs={{0,6},{1,7},{2,4},{3,5},{4,2},{5,3},{6,0},{7,1},{8,14},{9,15},{10,... | collective-permute-start | bytes 417800 | tf_op jit(solution)/shard_map/ppermute | solution.py:315
  9.9 0.5 collective-permute-start.3
  10.4 0.5 collective-permute-start.2
  10.9 0.0 copy-start
  10.9 3.4 %copy-done = bf16[1024,4096]{1,0:T(8,128)(2,1)S(1)} copy-done((bf16[1024,4096]{1,0:T(8,128)(2,1)S(1)}, bf16[1024,4096]{1,0:T(8,128)(2,1)}, u32[]{:S(2)}) %copy-start) | copy-done | bytes 8388632
  14.3 0.6 stage_integrals.1.cols
  14.9 3.9 %collective-permute-done.rest_0_ = bf16[1040,128]{1,0:T(8,128)(2,1)S(1)} collective-permute-done((bf16[1040,128]{1,0:T(8,128)(2,1)S(1)}, bf16[1040,128]{1,0:T(8,128)(2,1)S(1)}, u32[]{:S(2)}, u32[]{:S(2)}) %collective-permute-start) | collective-permute-done | bytes 266272 | tf_op jit(solution)/shard_map/ppermute | solution.py:315
  18.9 0.0 collective-permute-done.4.rest_3_
  18.9 0.0 collective-permute-done.3.rest_2_
  18.9 0.0 collective-permute-done.2.rest_1_
  18.9 0.1 collective-permute-start.6
  18.9 0.8 %collective-permute-start.5 = (bf16[1040,128]{1,0:T(8,128)(2,1)S(1)}, bf16[1040,128]{1,0:T(8,128)(2,1)S(1)}, u32[]{:S(2)}, u32[]{:S(2)}) collective-permute-start(bf16[1040,128]{1,0:T(8,128)(2,1)S(1)} %collective-permute-done.rest_0_), channel_id=1, source_target_pairs={{0,8},{8,0},{16,24},{24,16},{1,9},{9,1},{17,25},{25,17},{2,10},{10... | collective-permute-start | bytes 798728 | tf_op jit(solution)/shard_map/ppermute | solution.py:315
  19.8 0.7 %collective-permute-done.6.rest_1_ = bf16[1040,128]{1,0:T(8,128)(2,1)S(1)} collective-permute-done((bf16[1040,128]{1,0:T(8,128)(2,1)S(1)}, bf16[1040,128]{1,0:T(8,128)(2,1)S(1)}, u32[]{:S(2)}, u32[]{:S(2)}) %collective-permute-start.6) | collective-permute-done | bytes 266272 | tf_op jit(solution)/shard_map/ppermute | solution.py:315
  20.5 1.2 %bucket_tiles.4 = bf16[2192,128]{1,0:T(8,128)(2,1)S(1)} custom-call(bf16[1040,128]{1,0:T(8,128)(2,1)S(1)} %collective-permute-done.rest_0_, bf16[1040,128]{1,0:T(8,128)(2,1)S(1)} %collective-permute-done.6.rest_1_), custom_call_target="tpu_custom_call" | custom-call | bytes 2228224 | tf_op jit(solution)/shard_map/bucket_tiles/pallas_call | solution.py:147
  21.7 6.1 %collective-permute-done.5.rest_0_ = bf16[1040,128]{1,0:T(8,128)(2,1)S(1)} collective-permute-done((bf16[1040,128]{1,0:T(8,128)(2,1)S(1)}, bf16[1040,128]{1,0:T(8,128)(2,1)S(1)}, u32[]{:S(2)}, u32[]{:S(2)}) %collective-permute-start.5) | collective-permute-done | bytes 266272 | tf_op jit(solution)/shard_map/ppermute | solution.py:315
  27.8 0.0 collective-permute-start.11
  27.8 0.8 %collective-permute-start.10 = (bf16[2176,128]{1,0:T(8,128)(2,1)S(1)}, bf16[2176,128]{1,0:T(8,128)(2,1)S(1)}, u32[]{:S(2)}, u32[]{:S(2)}) collective-permute-start(bf16[2176,128]{1,0:T(8,128)(2,1)S(1)} %pad_maximum_fusion), channel_id=1, source_target_pairs={{0,8},{8,0},{16,24},{24,16},{1,9},{9,1},{17,25},{25,17},{2,10},{10... | collective-permute-start | bytes 1671176 | tf_op jit(solution)/shard_map/ppermute | solution.py:315
  28.6 2.4 %collective-permute-start.9 = (bf16[544,128]{1,0:T(8,128)(2,1)S(1)}, bf16[544,128]{1,0:T(8,128)(2,1)S(1)}, u32[]{:S(2)}, u32[]{:S(2)}) collective-permute-start(bf16[544,128]{1,0:T(8,128)(2,1)S(1)} %get-tuple-element.34), channel_id=1, source_target_pairs={{0,6},{1,7},{2,4},{3,5},{4,2},{5,3},{6,0},{7,1},{8,14},{9,15},{10,... | collective-permute-start | bytes 417800 | tf_op jit(solution)/shard_map/ppermute | solution.py:315
  31.1 0.5 collective-permute-start.8
  31.6 0.5 collective-permute-start.7
  32.1 0.0 collective-permute-done.11.rest_1_
  32.1 1.2 %bucket_tiles.5 = bf16[2192,128]{1,0:T(8,128)(2,1)S(1)} custom-call(bf16[1040,128]{1,0:T(8,128)(2,1)S(1)} %collective-permute-done.5.rest_0_, bf16[1040,128]{1,0:T(8,128)(2,1)S(1)} %collective-permute-done.11.rest_1_), custom_call_target="tpu_custom_call" | custom-call | bytes 2228224 | tf_op jit(solution)/shard_map/bucket_tiles/pallas_call | solution.py:147
  33.3 2.5 %collective-permute-start.14 = (bf16[544,128]{1,0:T(8,128)(2,1)S(1)}, bf16[544,128]{1,0:T(8,128)(2,1)S(1)}, u32[]{:S(2)}, u32[]{:S(2)}) collective-permute-start(bf16[544,128]{1,0:T(8,128)(2,1)S(1)} %get-tuple-element.30), channel_id=1, source_target_pairs={{0,6},{1,7},{2,4},{3,5},{4,2},{5,3},{6,0},{7,1},{8,14},{9,15},{10,... | collective-permute-start | bytes 417800 | tf_op jit(solution)/shard_map/ppermute | solution.py:315
  35.8 0.0 collective-permute-done.9.rest_7_
  35.8 1.8 %collective-permute-start.13 = (bf16[544,128]{1,0:T(8,128)(2,1)S(1)}, bf16[544,128]{1,0:T(8,128)(2,1)S(1)}, u32[]{:S(2)}, u32[]{:S(2)}) collective-permute-start(bf16[544,128]{1,0:T(8,128)(2,1)S(1)} %get-tuple-element.31), channel_id=1, source_target_pairs={{0,4},{1,5},{2,6},{3,7},{4,0},{5,1},{6,2},{7,3},{8,12},{9,13},{10,... | collective-permute-start | bytes 417800 | tf_op jit(solution)/shard_map/ppermute | solution.py:315
  37.6 1.6 %collective-permute-done.8.rest_6_ = bf16[544,128]{1,0:T(8,128)(2,1)S(1)} collective-permute-done((bf16[544,128]{1,0:T(8,128)(2,1)S(1)}, bf16[544,128]{1,0:T(8,128)(2,1)S(1)}, u32[]{:S(2)}, u32[]{:S(2)}) %collective-permute-start.8) | collective-permute-done | bytes 139296 | tf_op jit(solution)/shard_map/ppermute | solution.py:315
  39.2 1.4 %collective-permute-start.12 = (bf16[544,128]{1,0:T(8,128)(2,1)S(1)}, bf16[544,128]{1,0:T(8,128)(2,1)S(1)}, u32[]{:S(2)}, u32[]{:S(2)}) collective-permute-start(bf16[544,128]{1,0:T(8,128)(2,1)S(1)} %get-tuple-element.32), channel_id=1, source_target_pairs={{0,2},{1,3},{2,0},{3,1},{4,6},{5,7},{6,4},{7,5},{8,10},{9,11},{10,... | collective-permute-start | bytes 417800 | tf_op jit(solution)/shard_map/ppermute | solution.py:315
  40.6 0.0 collective-permute-done.7.rest_5_
  40.6 3.4 %place_early.1._ = bf16[528,4096]{1,0:T(8,128)(2,1)S(1)} custom-call(bf16[544,128]{1,0:T(8,128)(2,1)S(1)} %get-tuple-element.18.rest_0_, bf16[544,128]{1,0:T(8,128)(2,1)S(1)} %collective-permute-done.2.rest_1_, bf16[544,128]{1,0:T(8,128)(2,1)S(1)} %collective-permute-done.3.rest_2_, bf16[544,128]{1,0:T(8,128)(2,1)S(1)} %collective-permute-done.4.rest_3_, ...), custom_call_target="tpu_custom_call" | custom-call | bytes 8388608 | tf_op jit(solution)/shard_map/place_early/pallas_call | solution.py:252
  44.1 0.0 collective-permute-done.14.rest_4_
  44.1 0.2 collective-permute-done.13.rest_3_
  44.3 0.3 collective-permute-done.12.rest_2_
  44.6 0.0 collective-permute-done.10.rest_0_
  44.6 4.7 %place_and_multiply.1 = (bf16[528,4096]{1,0:T(8,128)(2,1)S(1)}, f32[256,1024]{1,0:T(8,128)S(1)}) custom-call(bf16[528,4096]{1,0:T(8,128)(2,1)S(1)} %place_early.1._, bf16[1024,4096]{1,0:T(8,128)(2,1)S(1)} %stage_integrals.1.cols, bf16[2176,128]{1,0:T(8,128)(2,1)S(1)} %collective-permute-done.10.rest_0_, ...), custom_call_target="tpu_custom_call", output_to_operand_aliasing={{0}: (0, {})} | custom-call | flops 4294967296 | bytes 16777216 | tf_op jit(solution)/shard_map/place_and_multiply/pallas_call | solution.py:274
  49.3 0.1 collective-permute-start.15
  49.4 2.4 %multiply_kept.1 = f32[256,1024]{1,0:T(8,128)S(1)} custom-call(bf16[528,4096]{1,0:T(8,128)(2,1)S(1)} %get-tuple-element.25.lam, bf16[1024,4096]{1,0:T(8,128)(2,1)S(1)} %stage_integrals.1.cols), custom_call_target="tpu_custom_call" | custom-call | flops 2147483648 | bytes 10485760 | tf_op jit(solution)/shard_map/multiply_kept/pallas_call | solution.py:303
  51.7 0.3 collective-permute-done.15
  52.0 0.1 slice_add_fusion.2
  52.2 1.4 %collective-permute-start.16 = (f32[64,1024]{1,0:T(8,128)S(1)}, f32[64,1024]{1,0:T(8,128)S(1)}, u32[]{:S(2)}, u32[]{:S(2)}) collective-permute-start(f32[64,1024]{1,0:T(8,128)S(1)} %get-tuple-element.27), channel_id=1, source_target_pairs={{0,2},{1,3},{2,0},{3,1},{4,6},{5,7},{6,4},{7,5},{8,10},{9,11},{10,... | collective-permute-start | bytes 786440 | tf_op jit(solution)/shard_map/ppermute | solution.py:315
  53.6 1.5 %collective-permute-start.18 = (f32[64,1024]{1,0:T(8,128)S(1)}, f32[64,1024]{1,0:T(8,128)S(1)}, u32[]{:S(2)}, u32[]{:S(2)}) collective-permute-start(f32[64,1024]{1,0:T(8,128)S(1)} %get-tuple-element.28), channel_id=1, source_target_pairs={{0,6},{1,7},{2,4},{3,5},{4,2},{5,3},{6,0},{7,1},{8,14},{9,15},{10,... | collective-permute-start | bytes 786440 | tf_op jit(solution)/shard_map/ppermute | solution.py:315
  55.1 0.7 collective-permute-start.17
  55.7 5.7 %collective-permute-done.16 = f32[64,1024]{1,0:T(8,128)S(1)} collective-permute-done((f32[64,1024]{1,0:T(8,128)S(1)}, f32[64,1024]{1,0:T(8,128)S(1)}, u32[]{:S(2)}, u32[]{:S(2)}) %collective-permute-start.16) | collective-permute-done | bytes 262176 | tf_op jit(solution)/shard_map/ppermute | solution.py:315
  61.4 5.8 %collective-permute-done.18 = f32[64,1024]{1,0:T(8,128)S(1)} collective-permute-done((f32[64,1024]{1,0:T(8,128)S(1)}, f32[64,1024]{1,0:T(8,128)S(1)}, u32[]{:S(2)}, u32[]{:S(2)}) %collective-permute-start.18) | collective-permute-done | bytes 262176 | tf_op jit(solution)/shard_map/ppermute | solution.py:315
  67.2 1.4 %collective-permute-done.17 = f32[64,1024]{1,0:T(8,128)S(1)} collective-permute-done((f32[64,1024]{1,0:T(8,128)S(1)}, f32[64,1024]{1,0:T(8,128)S(1)}, u32[]{:S(2)}, u32[]{:S(2)}) %collective-permute-start.17) | collective-permute-done | bytes 262176 | tf_op jit(solution)/shard_map/ppermute | solution.py:315
  68.5 0.8 %fusion.3 = f32[64,1024]{1,0:T(8,128)} fusion(f32[64,1024]{1,0:T(8,128)S(1)} %collective-permute-done.18, f32[64,1024]{1,0:T(8,128)S(1)} %collective-permute-done.17, f32[64,1024]{1,0:T(8,128)S(1)} %collective-permute-done.16, f32[256,1024]{1,0:T(8,128)S(1)} %collective-permute-done.15, f32[256,1024]{1,0:T(8,128)S(1)} %multiply_kept.1), kind=kLoop, calls=%fused_computation.8 | loop fusion | flops 327680 | bytes 1572864 | tf_op jit(solution)/shard_map/mul | solution.py:351
  (4 shorter events, 0.2 us)
Async XLA Ops:
  0.0 0.9 %copy-start.1 = (bf16[1,64,16,128]{3,2,1,0:T(8,128)(2,1)S(1)}, bf16[1,64,16,128]{3,2,1,0:T(8,128)(2,1)}, u32[]{:S(2)}) copy-start(bf16[1,64,16,128]{3,2,1,0:T(8,128)(2,1)} %param.3) | copy-start | bytes 786436
  1.0 0.7 copy-start.2
  2.0 4.2 %collective-permute-start.1 = (bf16[1040,128]{1,0:T(8,128)(2,1)S(1)}, bf16[1040,128]{1,0:T(8,128)(2,1)S(1)}, u32[]{:S(2)}, u32[]{:S(2)}) collective-permute-start(bf16[1040,128]{1,0:T(8,128)(2,1)S(1)} %pack_tiles.1.rest_0_), channel_id=1, source_target_pairs={{0,1},{1,0},{2,3},{3,2},{4,5},{5,4},{6,7},{7,6},{8,9},{9,8},{10,11... | collective-permute-start | bytes 798728 | tf_op jit(solution)/shard_map/ppermute | solution.py:315
  2.5 16.4 %collective-permute-start = (bf16[1040,128]{1,0:T(8,128)(2,1)S(1)}, bf16[1040,128]{1,0:T(8,128)(2,1)S(1)}, u32[]{:S(2)}, u32[]{:S(2)}) collective-permute-start(bf16[1040,128]{1,0:T(8,128)(2,1)S(1)} %pack_tiles.1.rest_0_), channel_id=1, source_target_pairs={{0,16},{8,24},{16,0},{24,8},{1,17},{9,25},{17,1},{25,9},{2,18},{10... | collective-permute-start | bytes 798728 | tf_op jit(solution)/shard_map/ppermute | solution.py:315
  7.4 11.5 %collective-permute-start.4 = (bf16[544,128]{1,0:T(8,128)(2,1)S(1)}, bf16[544,128]{1,0:T(8,128)(2,1)S(1)}, u32[]{:S(2)}, u32[]{:S(2)}) collective-permute-start(bf16[544,128]{1,0:T(8,128)(2,1)S(1)} %get-tuple-element.38), channel_id=1, source_target_pairs={{0,6},{1,7},{2,4},{3,5},{4,2},{5,3},{6,0},{7,1},{8,14},{9,15},{10,... | collective-permute-start | bytes 417800 | tf_op jit(solution)/shard_map/ppermute | solution.py:315
  9.9 9.0 %collective-permute-start.3 = (bf16[544,128]{1,0:T(8,128)(2,1)S(1)}, bf16[544,128]{1,0:T(8,128)(2,1)S(1)}, u32[]{:S(2)}, u32[]{:S(2)}) collective-permute-start(bf16[544,128]{1,0:T(8,128)(2,1)S(1)} %get-tuple-element.39), channel_id=1, source_target_pairs={{0,4},{1,5},{2,6},{3,7},{4,0},{5,1},{6,2},{7,3},{8,12},{9,13},{10,... | collective-permute-start | bytes 417800 | tf_op jit(solution)/shard_map/ppermute | solution.py:315
  10.4 8.5 %collective-permute-start.2 = (bf16[544,128]{1,0:T(8,128)(2,1)S(1)}, bf16[544,128]{1,0:T(8,128)(2,1)S(1)}, u32[]{:S(2)}, u32[]{:S(2)}) collective-permute-start(bf16[544,128]{1,0:T(8,128)(2,1)S(1)} %get-tuple-element.40), channel_id=1, source_target_pairs={{0,2},{1,3},{2,0},{3,1},{4,6},{5,7},{6,4},{7,5},{8,10},{9,11},{10,... | collective-permute-start | bytes 417800 | tf_op jit(solution)/shard_map/ppermute | solution.py:315
  10.9 3.4 %copy-start = (bf16[1024,4096]{1,0:T(8,128)(2,1)S(1)}, bf16[1024,4096]{1,0:T(8,128)(2,1)}, u32[]{:S(2)}) copy-start(bf16[1024,4096]{1,0:T(8,128)(2,1)} %source.1) | copy-start | bytes 25165828
  18.9 1.6 %collective-permute-start.6 = (bf16[1040,128]{1,0:T(8,128)(2,1)S(1)}, bf16[1040,128]{1,0:T(8,128)(2,1)S(1)}, u32[]{:S(2)}, u32[]{:S(2)}) collective-permute-start(bf16[1040,128]{1,0:T(8,128)(2,1)S(1)} %collective-permute-done.rest_0_), channel_id=1, source_target_pairs={{0,1},{1,0},{2,3},{3,2},{4,5},{5,4},{6,7},{7,6},{8,9},{9,8},{10,11... | collective-permute-start | bytes 798728 | tf_op jit(solution)/shard_map/ppermute | solution.py:315
  18.9 8.8 %collective-permute-start.5 = (bf16[1040,128]{1,0:T(8,128)(2,1)S(1)}, bf16[1040,128]{1,0:T(8,128)(2,1)S(1)}, u32[]{:S(2)}, u32[]{:S(2)}) collective-permute-start(bf16[1040,128]{1,0:T(8,128)(2,1)S(1)} %collective-permute-done.rest_0_), channel_id=1, source_target_pairs={{0,8},{8,0},{16,24},{24,16},{1,9},{9,1},{17,25},{25,17},{2,10},{10... | collective-permute-start | bytes 798728 | tf_op jit(solution)/shard_map/ppermute | solution.py:315
  27.8 4.4 %collective-permute-start.11 = (bf16[1040,128]{1,0:T(8,128)(2,1)S(1)}, bf16[1040,128]{1,0:T(8,128)(2,1)S(1)}, u32[]{:S(2)}, u32[]{:S(2)}) collective-permute-start(bf16[1040,128]{1,0:T(8,128)(2,1)S(1)} %collective-permute-done.5.rest_0_), channel_id=1, source_target_pairs={{0,1},{1,0},{2,3},{3,2},{4,5},{5,4},{6,7},{7,6},{8,9},{9,8},{10,11... | collective-permute-start | bytes 798728 | tf_op jit(solution)/shard_map/ppermute | solution.py:315
  27.8 16.8 %collective-permute-start.10 = (bf16[2176,128]{1,0:T(8,128)(2,1)S(1)}, bf16[2176,128]{1,0:T(8,128)(2,1)S(1)}, u32[]{:S(2)}, u32[]{:S(2)}) collective-permute-start(bf16[2176,128]{1,0:T(8,128)(2,1)S(1)} %pad_maximum_fusion), channel_id=1, source_target_pairs={{0,8},{8,0},{16,24},{24,16},{1,9},{9,1},{17,25},{25,17},{2,10},{10... | collective-permute-start | bytes 1671176 | tf_op jit(solution)/shard_map/ppermute | solution.py:315
  28.6 7.2 %collective-permute-start.9 = (bf16[544,128]{1,0:T(8,128)(2,1)S(1)}, bf16[544,128]{1,0:T(8,128)(2,1)S(1)}, u32[]{:S(2)}, u32[]{:S(2)}) collective-permute-start(bf16[544,128]{1,0:T(8,128)(2,1)S(1)} %get-tuple-element.34), channel_id=1, source_target_pairs={{0,6},{1,7},{2,4},{3,5},{4,2},{5,3},{6,0},{7,1},{8,14},{9,15},{10,... | collective-permute-start | bytes 417800 | tf_op jit(solution)/shard_map/ppermute | solution.py:315
  31.1 8.2 %collective-permute-start.8 = (bf16[544,128]{1,0:T(8,128)(2,1)S(1)}, bf16[544,128]{1,0:T(8,128)(2,1)S(1)}, u32[]{:S(2)}, u32[]{:S(2)}) collective-permute-start(bf16[544,128]{1,0:T(8,128)(2,1)S(1)} %get-tuple-element.35), channel_id=1, source_target_pairs={{0,4},{1,5},{2,6},{3,7},{4,0},{5,1},{6,2},{7,3},{8,12},{9,13},{10,... | collective-permute-start | bytes 417800 | tf_op jit(solution)/shard_map/ppermute | solution.py:315
  31.6 9.0 %collective-permute-start.7 = (bf16[544,128]{1,0:T(8,128)(2,1)S(1)}, bf16[544,128]{1,0:T(8,128)(2,1)S(1)}, u32[]{:S(2)}, u32[]{:S(2)}) collective-permute-start(bf16[544,128]{1,0:T(8,128)(2,1)S(1)} %get-tuple-element.36), channel_id=1, source_target_pairs={{0,2},{1,3},{2,0},{3,1},{4,6},{5,7},{6,4},{7,5},{8,10},{9,11},{10,... | collective-permute-start | bytes 417800 | tf_op jit(solution)/shard_map/ppermute | solution.py:315
  33.3 10.8 %collective-permute-start.14 = (bf16[544,128]{1,0:T(8,128)(2,1)S(1)}, bf16[544,128]{1,0:T(8,128)(2,1)S(1)}, u32[]{:S(2)}, u32[]{:S(2)}) collective-permute-start(bf16[544,128]{1,0:T(8,128)(2,1)S(1)} %get-tuple-element.30), channel_id=1, source_target_pairs={{0,6},{1,7},{2,4},{3,5},{4,2},{5,3},{6,0},{7,1},{8,14},{9,15},{10,... | collective-permute-start | bytes 417800 | tf_op jit(solution)/shard_map/ppermute | solution.py:315
  35.8 8.4 %collective-permute-start.13 = (bf16[544,128]{1,0:T(8,128)(2,1)S(1)}, bf16[544,128]{1,0:T(8,128)(2,1)S(1)}, u32[]{:S(2)}, u32[]{:S(2)}) collective-permute-start(bf16[544,128]{1,0:T(8,128)(2,1)S(1)} %get-tuple-element.31), channel_id=1, source_target_pairs={{0,4},{1,5},{2,6},{3,7},{4,0},{5,1},{6,2},{7,3},{8,12},{9,13},{10,... | collective-permute-start | bytes 417800 | tf_op jit(solution)/shard_map/ppermute | solution.py:315
  39.2 5.4 %collective-permute-start.12 = (bf16[544,128]{1,0:T(8,128)(2,1)S(1)}, bf16[544,128]{1,0:T(8,128)(2,1)S(1)}, u32[]{:S(2)}, u32[]{:S(2)}) collective-permute-start(bf16[544,128]{1,0:T(8,128)(2,1)S(1)} %get-tuple-element.32), channel_id=1, source_target_pairs={{0,2},{1,3},{2,0},{3,1},{4,6},{5,7},{6,4},{7,5},{8,10},{9,11},{10,... | collective-permute-start | bytes 417800 | tf_op jit(solution)/shard_map/ppermute | solution.py:315
  49.3 2.7 %collective-permute-start.15 = (f32[256,1024]{1,0:T(8,128)S(1)}, f32[256,1024]{1,0:T(8,128)S(1)}, u32[]{:S(2)}, u32[]{:S(2)}) collective-permute-start(f32[256,1024]{1,0:T(8,128)S(1)} %get-tuple-element.26), channel_id=1, source_target_pairs={{0,1},{1,0},{2,3},{3,2},{4,5},{5,4},{6,7},{7,6},{8,9},{9,8},{10,11... | collective-permute-start | bytes 3145736 | tf_op jit(solution)/shard_map/ppermute | solution.py:315
  52.2 9.2 %collective-permute-start.16 = (f32[64,1024]{1,0:T(8,128)S(1)}, f32[64,1024]{1,0:T(8,128)S(1)}, u32[]{:S(2)}, u32[]{:S(2)}) collective-permute-start(f32[64,1024]{1,0:T(8,128)S(1)} %get-tuple-element.27), channel_id=1, source_target_pairs={{0,2},{1,3},{2,0},{3,1},{4,6},{5,7},{6,4},{7,5},{8,10},{9,11},{10,... | collective-permute-start | bytes 786440 | tf_op jit(solution)/shard_map/ppermute | solution.py:315
  53.6 13.6 %collective-permute-start.18 = (f32[64,1024]{1,0:T(8,128)S(1)}, f32[64,1024]{1,0:T(8,128)S(1)}, u32[]{:S(2)}, u32[]{:S(2)}) collective-permute-start(f32[64,1024]{1,0:T(8,128)S(1)} %get-tuple-element.28), channel_id=1, source_target_pairs={{0,6},{1,7},{2,4},{3,5},{4,2},{5,3},{6,0},{7,1},{8,14},{9,15},{10,... | collective-permute-start | bytes 786440 | tf_op jit(solution)/shard_map/ppermute | solution.py:315
  55.1 13.5 %collective-permute-start.17 = (f32[64,1024]{1,0:T(8,128)S(1)}, f32[64,1024]{1,0:T(8,128)S(1)}, u32[]{:S(2)}, u32[]{:S(2)}) collective-permute-start(f32[64,1024]{1,0:T(8,128)S(1)} %get-tuple-element.29), channel_id=1, source_target_pairs={{0,4},{1,5},{2,6},{3,7},{4,0},{5,1},{6,2},{7,3},{8,12},{9,13},{10,... | collective-permute-start | bytes 786440 | tf_op jit(solution)/shard_map/ppermute | solution.py:315

commit v4 on v3

--- a/solution.py
+++ b/solution.py
@@ -311,6 +311,88 @@
     )(lam, integrals)
 
 
+def chunks_of(plan):
+    return plan.ab // plan.tile
+
+
+def words_shape(plan):
+    return (chunks_of(plan) // 2 * plan.owned + chunks_of(plan), plan.tile)
+
+
+def raised(x, power):
+    half = jnp.floor(power * 0.5)
+    return x * jnp.exp2(half) * jnp.exp2(power - half)
+
+
+def code_kernel(plan, keep, got, mine, *rest):
+    words, square = rest[:-1], rest[-1]
+    rows, tile, chunks = plan.owned, plan.tile, chunks_of(plan)
+    lane = lax.broadcasted_iota(jnp.int32, (rows, tile), 1)
+    mine[...] = keep[:rows, :] + got[:rows, :]
+    square[...] = jnp.zeros(square.shape, jnp.float32)
+    for m, out in enumerate(words, 1):
+        here = slice(m * rows, (m + 1) * rows)
+        cells = [slice(j * tile, (j + 1) * tile) for j in range(chunks)]
+        sums = [keep[here, cell] + got[here, cell] for cell in cells]
+        most = jnp.zeros((rows, tile), jnp.float32)
+        for j, part in enumerate(sums):
+            most = jnp.where(lane == j, jnp.max(jnp.abs(part), axis=1, keepdims=True), most)
+        power = jnp.floor(jnp.log2(jnp.maximum(most, 2.0**-120)) + 1.001)
+        square[:rows, :] = power
+        counts = []
+        for j, part in enumerate(sums):
+            count = jnp.floor(raised(part, 15.0 - power[:, j : j + 1]) + 0.5)
+            counts.append(jnp.clip(count, -32767.0, 32767.0).astype(jnp.int32))
+        for j in range(chunks // 2):
+            word = (counts[j] << 16) | (counts[j + chunks // 2] & 65535)
+            out[j * rows : (j + 1) * rows, :] = word
+        out[chunks // 2 * rows :, :] = square[...].T[:chunks, :].astype(jnp.int32)
+
+
+def code_sums(plan, keep, got):
+    block = pltpu.VMEM((plan.owned, plan.ab), jnp.float32)
+    return pl.pallas_call(
+        functools.partial(code_kernel, plan),
+        out_shape=[block] + [pltpu.VMEM(words_shape(plan), jnp.int32)] * (plan.n_pair - 1),
+        in_specs=[VMEM] * 2,
+        out_specs=[VMEM] * plan.n_pair,
+        scratch_shapes=[pltpu.VMEM((plan.tile, plan.tile), jnp.float32)],
+        compiler_params=pltpu.CompilerParams(vmem_limit_bytes=20 * 1024 * 1024),
+        cost_estimate=cost(plan, 4 * plan.n_pair * plan.owned * plan.ab * 4),
+        name="code_sums",
+    )(keep, got)
+
+
+def total_kernel(plan, mine, *rest):
+    words, (out, square) = rest[:-2], rest[-2:]
+    rows, tile, chunks = plan.owned, plan.tile, chunks_of(plan)
+    out[...] = mine[...]
+    square[...] = jnp.zeros(square.shape, jnp.float32)
+    for ref in words:
+        square[:chunks, :] = ref[chunks // 2 * rows :, :].astype(jnp.float32)
+        power = square[...].T[:rows, :] - 15.0
+        for j in range(chunks):
+            at = j % (chunks // 2) * rows
+            word = ref[at : at + rows, :]
+            count = (word if j < chunks // 2 else word << 16) >> 16
+            cell = slice(j * tile, (j + 1) * tile)
+            out[:, cell] += raised(count.astype(jnp.float32), power[:, j : j + 1])
+    out[...] = 0.5 * out[...]
+
+
+def total_sums(plan, mine, words):
+    return pl.pallas_call(
+        functools.partial(total_kernel, plan),
+        out_shape=jax.ShapeDtypeStruct((plan.owned, plan.ab), jnp.float32),
+        in_specs=[VMEM] * (1 + len(words)),
+        out_specs=VMEM,
+        scratch_shapes=[pltpu.VMEM((plan.tile, plan.tile), jnp.float32)],
+        compiler_params=pltpu.CompilerParams(vmem_limit_bytes=20 * 1024 * 1024),
+        cost_estimate=cost(plan, 4 * plan.n_pair * plan.owned * plan.ab * 4),
+        name="total_sums",
+    )(mine, *words)
+
+
 def swap(x, axis, m):
     return lax.ppermute(x, axis, [(i, i ^ m) for i in range(lax.axis_size(axis))])
 
@@ -334,7 +416,7 @@
         arrived.update({d | bit: swap(raw, "row", bit) for d, raw in arrived.items() if d or bit > 1})
     *middle, last = sorted(arrived)[1:]
     early = spread(middle)
-    arrived[last], early[0], own[0] = lax.optimization_barrier((arrived[last], early[0], own[0]))
+    arrived[last], early[1], own[0] = lax.optimization_barrier((arrived[last], early[1], own[0]))
     near = swap(jnp.concatenate(own, axis=0), "row", 1)
     late = spread([last])
     planes = [((chip,), (0,)) for chip in chips] + [((chip,), tuple(middle)) for chip in chips]
@@ -343,12 +425,8 @@
     lam, send = send_product(plan, lam, planes, [near] + late, staged)
     got = swap(send, "col", 1)
     keep = keep_product(plan, lam, staged)
-    both = [
-        keep[m * plan.owned : (m + 1) * plan.owned] + got[m * plan.owned : (m + 1) * plan.owned]
-        for m in range(plan.n_pair)
-    ]
-    others = [swap(both[m], "col", 2 * m) for m in range(1, plan.n_pair)]
-    return 0.5 * functools.reduce(jnp.add, others, both[0])
+    mine, *words = code_sums(plan, keep, got)
+    return total_sums(plan, mine, [swap(word, "col", 2 * m) for m, word in enumerate(words, 1)])
 
 
 def solution(mesh):

time: 69.5 us -> 64.9 us (0.934)
  waiting for transfers between devices: 26 us -> 20.5 us
  Pallas kernels: 14.9 us -> 17.4 us
  other arithmetic: 0.96 us -> 0.04 us
  starting transfers between devices: 22.2 us -> 21.4 us
    ppermute x19, waiting for transfers between devices: 26 us -> 20.5 us  [swap(): lax.ppermute(x, axis, [(i, i ^ m) for i in range(lax.axis_size(axis))])]
    pallas_call x0 -> x2, Pallas kernels: none -> 2.51 us  [the longest x1 1.27 us: total_sums(): pl.pallas_call(functools.partial(total_kernel, plan), out_shape=jax.Shape...]
    mul x1 -> x0, other arithmetic: 0.81 us -> none  [shards(): return 0.5 * functools.reduce(jnp.add, others, both[0])]
    ppermute x19, starting transfers between devices: 22.2 us -> 21.4 us  [swap(): lax.ppermute(x, axis, [(i, i ^ m) for i in range(lax.axis_size(axis))])]
  transfers between devices with their start and end apart: 19 -> 19, of which waited for: 10 -> 8; matrix products, arithmetic and copies ran while one was open for 0% -> 0% of each run, Pallas kernels for 14% -> 15%
where the time goes in v4:
time: 64.9 us; the launch traced here: 64.7 us
  starting transfers between devices  21.4 us (33%)
  waiting for transfers between devices  20.5 us (32%)
  Pallas kernels  17.4 us (27%)
  local copies, waits for them, and re-layouts  5.1 us (8%)
    ppermute x19, starting transfers between devices, swap(): lax.ppermute(x, axis, [(i, i ^ m) for i in range(lax.axis_size(axis))])  21.4 us
    ppermute x19, waiting for transfers between devices, swap(): lax.ppermute(x, axis, [(i, i ^ m) for i in range(lax.axis_size(axis))])  20.5 us
    unnamed x6, local copies, waits for them, and re-layouts  4.99 us
    pallas_call x1, Pallas kernels, send_product(): pl.pallas_call(functools.partial(send_kernel, plan, planes, block), out_s...  4.69 us
    pallas_call x3, Pallas kernels, bucket(): pl.pallas_call(functools.partial(bucket_kernel, plan, count), out_shape=p...  3.45 us
    pallas_call x1, Pallas kernels, place_early(): pl.pallas_call(functools.partial(early_kernel, plan, planes), out_shape=l...  3.44 us
    pallas_call x1, Pallas kernels, keep_product(): pl.pallas_call(functools.partial(keep_kernel, plan, block), out_shape=plt...  2.36 us
  transfers between devices with their start and end apart: 19, of which 8 were waited for; matrix products, arithmetic and copies ran while one was open for 0% of the time, Pallas kernels for 15%

profile of v4, /device:TPU:0, one launch (start us, length us, event | category | flops | bytes accessed | tf_op | source)
XLA Modules:
  0.0 64.7 jit_solution(11825717832550624275)
XLA Ops:
  0.0 0.0 copy-start.1
  0.0 0.9 %copy-done.1 = bf16[1,64,16,128]{3,2,1,0:T(8,128)(2,1)S(1)} copy-done((bf16[1,64,16,128]{3,2,1,0:T(8,128)(2,1)S(1)}, bf16[1,64,16,128]{3,2,1,0:T(8,128)(2,1)}, u32[]{:S(2)}) %copy-start.1) | copy-done | bytes 262168
  1.0 0.0 copy-start.2
  1.0 0.7 %copy-done.2 = s32[1,64]{1,0:T(1,128)S(1)} copy-done((s32[1,64]{1,0:T(1,128)S(1)}, s32[1,64]{1,0:T(1,128)}, u32[]{:S(2)}) %copy-start.2) | copy-done | bytes 280
  1.6 0.4 pack_tiles.1.rest_0_
  2.0 0.5 collective-permute-start.1
  2.5 3.7 %collective-permute-start = (bf16[1040,128]{1,0:T(8,128)(2,1)S(1)}, bf16[1040,128]{1,0:T(8,128)(2,1)S(1)}, u32[]{:S(2)}, u32[]{:S(2)}) collective-permute-start(bf16[1040,128]{1,0:T(8,128)(2,1)S(1)} %pack_tiles.1.rest_0_), channel_id=1, source_target_pairs={{0,16},{8,24},{16,0},{24,8},{1,17},{9,25},{17,1},{25,9},{2,18},{10... | collective-permute-start | bytes 798728 | tf_op jit(solution)/shard_map/ppermute | solution.py:397
  6.2 0.0 collective-permute-done.1.rest_1_
  6.2 1.2 %bucket_tiles.3 = bf16[2192,128]{1,0:T(8,128)(2,1)S(1)} custom-call(bf16[1040,128]{1,0:T(8,128)(2,1)S(1)} %pack_tiles.1.rest_0_, bf16[1040,128]{1,0:T(8,128)(2,1)S(1)} %collective-permute-done.1.rest_1_), custom_call_target="tpu_custom_call" | custom-call | bytes 2228224 | tf_op jit(solution)/shard_map/bucket_tiles/pallas_call | solution.py:147
  7.4 2.5 %collective-permute-start.4 = (bf16[544,128]{1,0:T(8,128)(2,1)S(1)}, bf16[544,128]{1,0:T(8,128)(2,1)S(1)}, u32[]{:S(2)}, u32[]{:S(2)}) collective-permute-start(bf16[544,128]{1,0:T(8,128)(2,1)S(1)} %get-tuple-element.43), channel_id=1, source_target_pairs={{0,6},{1,7},{2,4},{3,5},{4,2},{5,3},{6,0},{7,1},{8,14},{9,15},{10,... | collective-permute-start | bytes 417800 | tf_op jit(solution)/shard_map/ppermute | solution.py:397
  9.9 0.5 collective-permute-start.3
  10.4 0.5 collective-permute-start.2
  10.9 0.0 copy-start
  10.9 3.4 %copy-done = bf16[1024,4096]{1,0:T(8,128)(2,1)S(1)} copy-done((bf16[1024,4096]{1,0:T(8,128)(2,1)S(1)}, bf16[1024,4096]{1,0:T(8,128)(2,1)}, u32[]{:S(2)}) %copy-start) | copy-done | bytes 8388632
  14.3 0.6 stage_integrals.1.cols
  14.9 3.9 %collective-permute-done.rest_0_ = bf16[1040,128]{1,0:T(8,128)(2,1)S(1)} collective-permute-done((bf16[1040,128]{1,0:T(8,128)(2,1)S(1)}, bf16[1040,128]{1,0:T(8,128)(2,1)S(1)}, u32[]{:S(2)}, u32[]{:S(2)}) %collective-permute-start) | collective-permute-done | bytes 266272 | tf_op jit(solution)/shard_map/ppermute | solution.py:397
  18.9 0.0 collective-permute-done.4.rest_3_
  18.9 0.0 collective-permute-done.3.rest_2_
  18.9 0.0 collective-permute-done.2.rest_1_
  18.9 0.1 collective-permute-start.6
  18.9 0.8 %collective-permute-start.5 = (bf16[1040,128]{1,0:T(8,128)(2,1)S(1)}, bf16[1040,128]{1,0:T(8,128)(2,1)S(1)}, u32[]{:S(2)}, u32[]{:S(2)}) collective-permute-start(bf16[1040,128]{1,0:T(8,128)(2,1)S(1)} %collective-permute-done.rest_0_), channel_id=1, source_target_pairs={{0,8},{8,0},{16,24},{24,16},{1,9},{9,1},{17,25},{25,17},{2,10},{10... | collective-permute-start | bytes 798728 | tf_op jit(solution)/shard_map/ppermute | solution.py:397
  19.8 0.7 %collective-permute-done.6.rest_1_ = bf16[1040,128]{1,0:T(8,128)(2,1)S(1)} collective-permute-done((bf16[1040,128]{1,0:T(8,128)(2,1)S(1)}, bf16[1040,128]{1,0:T(8,128)(2,1)S(1)}, u32[]{:S(2)}, u32[]{:S(2)}) %collective-permute-start.6) | collective-permute-done | bytes 266272 | tf_op jit(solution)/shard_map/ppermute | solution.py:397
  20.5 1.2 %bucket_tiles.4 = bf16[2192,128]{1,0:T(8,128)(2,1)S(1)} custom-call(bf16[1040,128]{1,0:T(8,128)(2,1)S(1)} %collective-permute-done.rest_0_, bf16[1040,128]{1,0:T(8,128)(2,1)S(1)} %collective-permute-done.6.rest_1_), custom_call_target="tpu_custom_call" | custom-call | bytes 2228224 | tf_op jit(solution)/shard_map/bucket_tiles/pallas_call | solution.py:147
  21.7 1.6 %collective-permute-start.7 = (bf16[544,128]{1,0:T(8,128)(2,1)S(1)}, bf16[544,128]{1,0:T(8,128)(2,1)S(1)}, u32[]{:S(2)}, u32[]{:S(2)}) collective-permute-start(bf16[544,128]{1,0:T(8,128)(2,1)S(1)} %get-tuple-element.42), channel_id=1, source_target_pairs={{0,2},{1,3},{2,0},{3,1},{4,6},{5,7},{6,4},{7,5},{8,10},{9,11},{10,... | collective-permute-start | bytes 417800 | tf_op jit(solution)/shard_map/ppermute | solution.py:397
  23.3 4.5 %collective-permute-done.5.rest_0_ = bf16[1040,128]{1,0:T(8,128)(2,1)S(1)} collective-permute-done((bf16[1040,128]{1,0:T(8,128)(2,1)S(1)}, bf16[1040,128]{1,0:T(8,128)(2,1)S(1)}, u32[]{:S(2)}, u32[]{:S(2)}) %collective-permute-start.5) | collective-permute-done | bytes 266272 | tf_op jit(solution)/shard_map/ppermute | solution.py:397
  27.8 0.0 collective-permute-done.7.rest_5_
  27.8 0.0 collective-permute-start.11
  27.8 0.8 %collective-permute-start.10 = (bf16[2176,128]{1,0:T(8,128)(2,1)S(1)}, bf16[2176,128]{1,0:T(8,128)(2,1)S(1)}, u32[]{:S(2)}, u32[]{:S(2)}) collective-permute-start(bf16[2176,128]{1,0:T(8,128)(2,1)S(1)} %pad_maximum_fusion), channel_id=1, source_target_pairs={{0,8},{8,0},{16,24},{24,16},{1,9},{9,1},{17,25},{25,17},{2,10},{10... | collective-permute-start | bytes 1671176 | tf_op jit(solution)/shard_map/ppermute | solution.py:397
  28.6 2.4 %collective-permute-start.9 = (bf16[544,128]{1,0:T(8,128)(2,1)S(1)}, bf16[544,128]{1,0:T(8,128)(2,1)S(1)}, u32[]{:S(2)}, u32[]{:S(2)}) collective-permute-start(bf16[544,128]{1,0:T(8,128)(2,1)S(1)} %get-tuple-element.39), channel_id=1, source_target_pairs={{0,6},{1,7},{2,4},{3,5},{4,2},{5,3},{6,0},{7,1},{8,14},{9,15},{10,... | collective-permute-start | bytes 417800 | tf_op jit(solution)/shard_map/ppermute | solution.py:397
  31.1 0.5 collective-permute-start.8
  31.6 0.0 collective-permute-done.11.rest_1_
  31.6 1.2 %bucket_tiles.5 = bf16[2192,128]{1,0:T(8,128)(2,1)S(1)} custom-call(bf16[1040,128]{1,0:T(8,128)(2,1)S(1)} %collective-permute-done.5.rest_0_, bf16[1040,128]{1,0:T(8,128)(2,1)S(1)} %collective-permute-done.11.rest_1_), custom_call_target="tpu_custom_call" | custom-call | bytes 2228224 | tf_op jit(solution)/shard_map/bucket_tiles/pallas_call | solution.py:147
  32.8 1.6 %collective-permute-start.14 = (bf16[544,128]{1,0:T(8,128)(2,1)S(1)}, bf16[544,128]{1,0:T(8,128)(2,1)S(1)}, u32[]{:S(2)}, u32[]{:S(2)}) collective-permute-start(bf16[544,128]{1,0:T(8,128)(2,1)S(1)} %get-tuple-element.35), channel_id=1, source_target_pairs={{0,6},{1,7},{2,4},{3,5},{4,2},{5,3},{6,0},{7,1},{8,14},{9,15},{10,... | collective-permute-start | bytes 417800 | tf_op jit(solution)/shard_map/ppermute | solution.py:397
  34.3 0.5 collective-permute-start.13
  34.8 0.6 collective-permute-done.9.rest_7_
  35.4 1.7 %collective-permute-start.12 = (bf16[544,128]{1,0:T(8,128)(2,1)S(1)}, bf16[544,128]{1,0:T(8,128)(2,1)S(1)}, u32[]{:S(2)}, u32[]{:S(2)}) collective-permute-start(bf16[544,128]{1,0:T(8,128)(2,1)S(1)} %get-tuple-element.37), channel_id=1, source_target_pairs={{0,2},{1,3},{2,0},{3,1},{4,6},{5,7},{6,4},{7,5},{8,10},{9,11},{10,... | collective-permute-start | bytes 417800 | tf_op jit(solution)/shard_map/ppermute | solution.py:397
  37.2 4.2 %collective-permute-done.8.rest_6_ = bf16[544,128]{1,0:T(8,128)(2,1)S(1)} collective-permute-done((bf16[544,128]{1,0:T(8,128)(2,1)S(1)}, bf16[544,128]{1,0:T(8,128)(2,1)S(1)}, u32[]{:S(2)}, u32[]{:S(2)}) %collective-permute-start.8) | collective-permute-done | bytes 139296 | tf_op jit(solution)/shard_map/ppermute | solution.py:397
  41.4 3.4 %place_early.1._ = bf16[528,4096]{1,0:T(8,128)(2,1)S(1)} custom-call(bf16[544,128]{1,0:T(8,128)(2,1)S(1)} %get-tuple-element.22.rest_0_, bf16[544,128]{1,0:T(8,128)(2,1)S(1)} %collective-permute-done.2.rest_1_, bf16[544,128]{1,0:T(8,128)(2,1)S(1)} %collective-permute-done.3.rest_2_, bf16[544,128]{1,0:T(8,128)(2,1)S(1)} %collective-permute-done.4.rest_3_, ...), custom_call_target="tpu_custom_call" | custom-call | bytes 8388608 | tf_op jit(solution)/shard_map/place_early/pallas_call | solution.py:252
  44.8 0.0 collective-permute-done.14.rest_4_
  44.8 0.0 collective-permute-done.13.rest_3_
  44.9 0.0 collective-permute-done.12.rest_2_
  44.9 0.0 collective-permute-done.10.rest_0_
  44.9 4.7 %place_and_multiply.1 = (bf16[528,4096]{1,0:T(8,128)(2,1)S(1)}, f32[256,1024]{1,0:T(8,128)S(1)}) custom-call(bf16[528,4096]{1,0:T(8,128)(2,1)S(1)} %place_early.1._, bf16[1024,4096]{1,0:T(8,128)(2,1)S(1)} %stage_integrals.1.cols, bf16[2176,128]{1,0:T(8,128)(2,1)S(1)} %collective-permute-done.10.rest_0_, ...), custom_call_target="tpu_custom_call", output_to_operand_aliasing={{0}: (0, {})} | custom-call | flops 4294967296 | bytes 16777216 | tf_op jit(solution)/shard_map/place_and_multiply/pallas_call | solution.py:274
  49.6 0.1 collective-permute-start.15
  49.7 2.4 %multiply_kept.1.keep = f32[256,1024]{1,0:T(8,128)S(1)} custom-call(bf16[528,4096]{1,0:T(8,128)(2,1)S(1)} %get-tuple-element.29.lam, bf16[1024,4096]{1,0:T(8,128)(2,1)S(1)} %stage_integrals.1.cols), custom_call_target="tpu_custom_call" | custom-call | flops 2147483648 | bytes 10485760 | tf_op jit(solution)/shard_map/multiply_kept/pallas_call | solution.py:303
  52.0 0.3 collective-permute-done.15.got
  52.3 1.2 %code_sums.1 = (f32[64,1024]{1,0:T(8,128)S(1)}, s32[264,128]{1,0:T(8,128)S(1)}, s32[264,128]{1,0:T(8,128)S(1)}, s32[264,128]{1,0:T(8,128)S(1)}) custom-call(f32[256,1024]{1,0:T(8,128)S(1)} %multiply_kept.1.keep, f32[256,1024]{1,0:T(8,128)S(1)} %collective-permute-done.15.got), custom_call_target="tpu_custom_call" | custom-call | bytes 4194304 | tf_op jit(solution)/shard_map/code_sums/pallas_call | solution.py:354
  53.6 1.6 %collective-permute-start.16 = (s32[264,128]{1,0:T(8,128)S(1)}, s32[264,128]{1,0:T(8,128)S(1)}, u32[]{:S(2)}, u32[]{:S(2)}) collective-permute-start(s32[264,128]{1,0:T(8,128)S(1)} %get-tuple-element.32), channel_id=1, source_target_pairs={{0,2},{1,3},{2,0},{3,1},{4,6},{5,7},{6,4},{7,5},{8,10},{9,11},{10,... | collective-permute-start | bytes 405512 | tf_op jit(solution)/shard_map/ppermute | solution.py:397
  55.1 1.5 %collective-permute-start.17 = (s32[264,128]{1,0:T(8,128)S(1)}, s32[264,128]{1,0:T(8,128)S(1)}, u32[]{:S(2)}, u32[]{:S(2)}) collective-permute-start(s32[264,128]{1,0:T(8,128)S(1)} %get-tuple-element.33), channel_id=1, source_target_pairs={{0,4},{1,5},{2,6},{3,7},{4,0},{5,1},{6,2},{7,3},{8,12},{9,13},{10,... | collective-permute-start | bytes 405512 | tf_op jit(solution)/shard_map/ppermute | solution.py:397
  56.6 0.5 collective-permute-start.18
  57.1 2.7 %collective-permute-done.16.rest_0_ = s32[264,128]{1,0:T(8,128)S(1)} collective-permute-done((s32[264,128]{1,0:T(8,128)S(1)}, s32[264,128]{1,0:T(8,128)S(1)}, u32[]{:S(2)}, u32[]{:S(2)}) %collective-permute-start.16) | collective-permute-done | bytes 135200 | tf_op jit(solution)/shard_map/ppermute | solution.py:397
  59.8 3.7 %collective-permute-done.17.rest_1_ = s32[264,128]{1,0:T(8,128)S(1)} collective-permute-done((s32[264,128]{1,0:T(8,128)S(1)}, s32[264,128]{1,0:T(8,128)S(1)}, u32[]{:S(2)}, u32[]{:S(2)}) %collective-permute-start.17) | collective-permute-done | bytes 135200 | tf_op jit(solution)/shard_map/ppermute | solution.py:397
  63.4 0.0 collective-permute-done.18.rest_2_
  63.4 1.3 %total_sums.1 = f32[64,1024]{1,0:T(8,128)} custom-call(f32[64,1024]{1,0:T(8,128)S(1)} %get-tuple-element.31.mine, s32[264,128]{1,0:T(8,128)S(1)} %collective-permute-done.16.rest_0_, s32[264,128]{1,0:T(8,128)S(1)} %collective-permute-done.17.rest_1_, s32[264,128]{1,0:T(8,128)S(1)} %collective-permute-done.18.rest_2_), custom_call_target="tpu_custom_call" | custom-call | bytes 4194304 | tf_op jit(solution)/shard_map/total_sums/pallas_call | solution.py:384
  (4 shorter events, 0.2 us)
Async XLA Ops:
  0.0 0.9 %copy-start.1 = (bf16[1,64,16,128]{3,2,1,0:T(8,128)(2,1)S(1)}, bf16[1,64,16,128]{3,2,1,0:T(8,128)(2,1)}, u32[]{:S(2)}) copy-start(bf16[1,64,16,128]{3,2,1,0:T(8,128)(2,1)} %param.3) | copy-start | bytes 786436
  1.0 0.7 %copy-start.2 = (s32[1,64]{1,0:T(1,128)S(1)}, s32[1,64]{1,0:T(1,128)}, u32[]{:S(2)}) copy-start(s32[1,64]{1,0:T(1,128)} %ids.1) | copy-start | bytes 772
  2.0 4.2 %collective-permute-start.1 = (bf16[1040,128]{1,0:T(8,128)(2,1)S(1)}, bf16[1040,128]{1,0:T(8,128)(2,1)S(1)}, u32[]{:S(2)}, u32[]{:S(2)}) collective-permute-start(bf16[1040,128]{1,0:T(8,128)(2,1)S(1)} %pack_tiles.1.rest_0_), channel_id=1, source_target_pairs={{0,1},{1,0},{2,3},{3,2},{4,5},{5,4},{6,7},{7,6},{8,9},{9,8},{10,11... | collective-permute-start | bytes 798728 | tf_op jit(solution)/shard_map/ppermute | solution.py:397
  2.5 16.4 %collective-permute-start = (bf16[1040,128]{1,0:T(8,128)(2,1)S(1)}, bf16[1040,128]{1,0:T(8,128)(2,1)S(1)}, u32[]{:S(2)}, u32[]{:S(2)}) collective-permute-start(bf16[1040,128]{1,0:T(8,128)(2,1)S(1)} %pack_tiles.1.rest_0_), channel_id=1, source_target_pairs={{0,16},{8,24},{16,0},{24,8},{1,17},{9,25},{17,1},{25,9},{2,18},{10... | collective-permute-start | bytes 798728 | tf_op jit(solution)/shard_map/ppermute | solution.py:397
  7.4 11.5 %collective-permute-start.4 = (bf16[544,128]{1,0:T(8,128)(2,1)S(1)}, bf16[544,128]{1,0:T(8,128)(2,1)S(1)}, u32[]{:S(2)}, u32[]{:S(2)}) collective-permute-start(bf16[544,128]{1,0:T(8,128)(2,1)S(1)} %get-tuple-element.43), channel_id=1, source_target_pairs={{0,6},{1,7},{2,4},{3,5},{4,2},{5,3},{6,0},{7,1},{8,14},{9,15},{10,... | collective-permute-start | bytes 417800 | tf_op jit(solution)/shard_map/ppermute | solution.py:397
  9.9 9.0 %collective-permute-start.3 = (bf16[544,128]{1,0:T(8,128)(2,1)S(1)}, bf16[544,128]{1,0:T(8,128)(2,1)S(1)}, u32[]{:S(2)}, u32[]{:S(2)}) collective-permute-start(bf16[544,128]{1,0:T(8,128)(2,1)S(1)} %get-tuple-element.44), channel_id=1, source_target_pairs={{0,4},{1,5},{2,6},{3,7},{4,0},{5,1},{6,2},{7,3},{8,12},{9,13},{10,... | collective-permute-start | bytes 417800 | tf_op jit(solution)/shard_map/ppermute | solution.py:397
  10.4 8.5 %collective-permute-start.2 = (bf16[544,128]{1,0:T(8,128)(2,1)S(1)}, bf16[544,128]{1,0:T(8,128)(2,1)S(1)}, u32[]{:S(2)}, u32[]{:S(2)}) collective-permute-start(bf16[544,128]{1,0:T(8,128)(2,1)S(1)} %get-tuple-element.45), channel_id=1, source_target_pairs={{0,2},{1,3},{2,0},{3,1},{4,6},{5,7},{6,4},{7,5},{8,10},{9,11},{10,... | collective-permute-start | bytes 417800 | tf_op jit(solution)/shard_map/ppermute | solution.py:397
  10.9 3.4 %copy-start = (bf16[1024,4096]{1,0:T(8,128)(2,1)S(1)}, bf16[1024,4096]{1,0:T(8,128)(2,1)}, u32[]{:S(2)}) copy-start(bf16[1024,4096]{1,0:T(8,128)(2,1)} %source.1) | copy-start | bytes 25165828
  18.9 1.6 %collective-permute-start.6 = (bf16[1040,128]{1,0:T(8,128)(2,1)S(1)}, bf16[1040,128]{1,0:T(8,128)(2,1)S(1)}, u32[]{:S(2)}, u32[]{:S(2)}) collective-permute-start(bf16[1040,128]{1,0:T(8,128)(2,1)S(1)} %collective-permute-done.rest_0_), channel_id=1, source_target_pairs={{0,1},{1,0},{2,3},{3,2},{4,5},{5,4},{6,7},{7,6},{8,9},{9,8},{10,11... | collective-permute-start | bytes 798728 | tf_op jit(solution)/shard_map/ppermute | solution.py:397
  18.9 8.8 %collective-permute-start.5 = (bf16[1040,128]{1,0:T(8,128)(2,1)S(1)}, bf16[1040,128]{1,0:T(8,128)(2,1)S(1)}, u32[]{:S(2)}, u32[]{:S(2)}) collective-permute-start(bf16[1040,128]{1,0:T(8,128)(2,1)S(1)} %collective-permute-done.rest_0_), channel_id=1, source_target_pairs={{0,8},{8,0},{16,24},{24,16},{1,9},{9,1},{17,25},{25,17},{2,10},{10... | collective-permute-start | bytes 798728 | tf_op jit(solution)/shard_map/ppermute | solution.py:397
  21.7 6.1 %collective-permute-start.7 = (bf16[544,128]{1,0:T(8,128)(2,1)S(1)}, bf16[544,128]{1,0:T(8,128)(2,1)S(1)}, u32[]{:S(2)}, u32[]{:S(2)}) collective-permute-start(bf16[544,128]{1,0:T(8,128)(2,1)S(1)} %get-tuple-element.42), channel_id=1, source_target_pairs={{0,2},{1,3},{2,0},{3,1},{4,6},{5,7},{6,4},{7,5},{8,10},{9,11},{10,... | collective-permute-start | bytes 417800 | tf_op jit(solution)/shard_map/ppermute | solution.py:397
  27.8 3.8 %collective-permute-start.11 = (bf16[1040,128]{1,0:T(8,128)(2,1)S(1)}, bf16[1040,128]{1,0:T(8,128)(2,1)S(1)}, u32[]{:S(2)}, u32[]{:S(2)}) collective-permute-start(bf16[1040,128]{1,0:T(8,128)(2,1)S(1)} %collective-permute-done.5.rest_0_), channel_id=1, source_target_pairs={{0,1},{1,0},{2,3},{3,2},{4,5},{5,4},{6,7},{7,6},{8,9},{9,8},{10,11... | collective-permute-start | bytes 798728 | tf_op jit(solution)/shard_map/ppermute | solution.py:397
  27.8 17.1 %collective-permute-start.10 = (bf16[2176,128]{1,0:T(8,128)(2,1)S(1)}, bf16[2176,128]{1,0:T(8,128)(2,1)S(1)}, u32[]{:S(2)}, u32[]{:S(2)}) collective-permute-start(bf16[2176,128]{1,0:T(8,128)(2,1)S(1)} %pad_maximum_fusion), channel_id=1, source_target_pairs={{0,8},{8,0},{16,24},{24,16},{1,9},{9,1},{17,25},{25,17},{2,10},{10... | collective-permute-start | bytes 1671176 | tf_op jit(solution)/shard_map/ppermute | solution.py:397
  28.6 6.8 %collective-permute-start.9 = (bf16[544,128]{1,0:T(8,128)(2,1)S(1)}, bf16[544,128]{1,0:T(8,128)(2,1)S(1)}, u32[]{:S(2)}, u32[]{:S(2)}) collective-permute-start(bf16[544,128]{1,0:T(8,128)(2,1)S(1)} %get-tuple-element.39), channel_id=1, source_target_pairs={{0,6},{1,7},{2,4},{3,5},{4,2},{5,3},{6,0},{7,1},{8,14},{9,15},{10,... | collective-permute-start | bytes 417800 | tf_op jit(solution)/shard_map/ppermute | solution.py:397
  31.1 10.3 %collective-permute-start.8 = (bf16[544,128]{1,0:T(8,128)(2,1)S(1)}, bf16[544,128]{1,0:T(8,128)(2,1)S(1)}, u32[]{:S(2)}, u32[]{:S(2)}) collective-permute-start(bf16[544,128]{1,0:T(8,128)(2,1)S(1)} %get-tuple-element.40), channel_id=1, source_target_pairs={{0,4},{1,5},{2,6},{3,7},{4,0},{5,1},{6,2},{7,3},{8,12},{9,13},{10,... | collective-permute-start | bytes 417800 | tf_op jit(solution)/shard_map/ppermute | solution.py:397
  32.8 12.1 %collective-permute-start.14 = (bf16[544,128]{1,0:T(8,128)(2,1)S(1)}, bf16[544,128]{1,0:T(8,128)(2,1)S(1)}, u32[]{:S(2)}, u32[]{:S(2)}) collective-permute-start(bf16[544,128]{1,0:T(8,128)(2,1)S(1)} %get-tuple-element.35), channel_id=1, source_target_pairs={{0,6},{1,7},{2,4},{3,5},{4,2},{5,3},{6,0},{7,1},{8,14},{9,15},{10,... | collective-permute-start | bytes 417800 | tf_op jit(solution)/shard_map/ppermute | solution.py:397
  34.3 10.5 %collective-permute-start.13 = (bf16[544,128]{1,0:T(8,128)(2,1)S(1)}, bf16[544,128]{1,0:T(8,128)(2,1)S(1)}, u32[]{:S(2)}, u32[]{:S(2)}) collective-permute-start(bf16[544,128]{1,0:T(8,128)(2,1)S(1)} %get-tuple-element.36), channel_id=1, source_target_pairs={{0,4},{1,5},{2,6},{3,7},{4,0},{5,1},{6,2},{7,3},{8,12},{9,13},{10,... | collective-permute-start | bytes 417800 | tf_op jit(solution)/shard_map/ppermute | solution.py:397
  35.4 9.4 %collective-permute-start.12 = (bf16[544,128]{1,0:T(8,128)(2,1)S(1)}, bf16[544,128]{1,0:T(8,128)(2,1)S(1)}, u32[]{:S(2)}, u32[]{:S(2)}) collective-permute-start(bf16[544,128]{1,0:T(8,128)(2,1)S(1)} %get-tuple-element.37), channel_id=1, source_target_pairs={{0,2},{1,3},{2,0},{3,1},{4,6},{5,7},{6,4},{7,5},{8,10},{9,11},{10,... | collective-permute-start | bytes 417800 | tf_op jit(solution)/shard_map/ppermute | solution.py:397
  49.6 2.7 %collective-permute-start.15 = (f32[256,1024]{1,0:T(8,128)S(1)}, f32[256,1024]{1,0:T(8,128)S(1)}, u32[]{:S(2)}, u32[]{:S(2)}) collective-permute-start(f32[256,1024]{1,0:T(8,128)S(1)} %get-tuple-element.30), channel_id=1, source_target_pairs={{0,1},{1,0},{2,3},{3,2},{4,5},{5,4},{6,7},{7,6},{8,9},{9,8},{10,11... | collective-permute-start | bytes 3145736 | tf_op jit(solution)/shard_map/ppermute | solution.py:397
  53.6 6.2 %collective-permute-start.16 = (s32[264,128]{1,0:T(8,128)S(1)}, s32[264,128]{1,0:T(8,128)S(1)}, u32[]{:S(2)}, u32[]{:S(2)}) collective-permute-start(s32[264,128]{1,0:T(8,128)S(1)} %get-tuple-element.32), channel_id=1, source_target_pairs={{0,2},{1,3},{2,0},{3,1},{4,6},{5,7},{6,4},{7,5},{8,10},{9,11},{10,... | collective-permute-start | bytes 405512 | tf_op jit(solution)/shard_map/ppermute | solution.py:397
  55.1 8.3 %collective-permute-start.17 = (s32[264,128]{1,0:T(8,128)S(1)}, s32[264,128]{1,0:T(8,128)S(1)}, u32[]{:S(2)}, u32[]{:S(2)}) collective-permute-start(s32[264,128]{1,0:T(8,128)S(1)} %get-tuple-element.33), channel_id=1, source_target_pairs={{0,4},{1,5},{2,6},{3,7},{4,0},{5,1},{6,2},{7,3},{8,12},{9,13},{10,... | collective-permute-start | bytes 405512 | tf_op jit(solution)/shard_map/ppermute | solution.py:397
  56.6 6.8 %collective-permute-start.18 = (s32[264,128]{1,0:T(8,128)S(1)}, s32[264,128]{1,0:T(8,128)S(1)}, u32[]{:S(2)}, u32[]{:S(2)}) collective-permute-start(s32[264,128]{1,0:T(8,128)S(1)} %get-tuple-element.34), channel_id=1, source_target_pairs={{0,6},{1,7},{2,4},{3,5},{4,2},{5,3},{6,0},{7,1},{8,14},{9,15},{10,... | collective-permute-start | bytes 405512 | tf_op jit(solution)/shard_map/ppermute | solution.py:397

commit v5 on v4

--- a/solution.py
+++ b/solution.py
@@ -78,6 +78,7 @@
 
 
 def pack(plan, ids, tiles):
+    ids, tiles = (pltpu.with_memory_space_constraint(x, pltpu.HBM) for x in (ids, tiles))
     return pl.pallas_call(
         functools.partial(pack_kernel, plan),
         out_shape=jax.ShapeDtypeStruct((plan.packed, plan.tile), jnp.bfloat16),
@@ -162,30 +163,6 @@
         name="bucket_tiles",
     )(*packed)
     return [out[i * piece : (i + 1) * piece] for i in range(plan.n_pair)]
-
-
-def stage_kernel(steps, block, source, out, sem):
-    copies = []
-    for i in range(steps):
-        here = pl.ds(i * block, block)
-        copies.append(pltpu.make_async_copy(source.at[here], out.at[here], sem.at[i]))
-        copies[-1].start()
-    for copy in copies:
-        copy.wait()
-
-
-def stage(plan, integrals, block=256):
-    steps = plan.ab // block
-    return pl.pallas_call(
-        functools.partial(stage_kernel, steps, block),
-        out_shape=pltpu.VMEM(integrals.shape, integrals.dtype),
-        in_specs=[HBM],
-        out_specs=VMEM,
-        scratch_shapes=[pltpu.SemaphoreType.DMA((steps,))],
-        compiler_params=pltpu.CompilerParams(vmem_limit_bytes=2 * 1024 * 1024),
-        cost_estimate=cost(plan, 2 * plan.ab * plan.cd * 2),
-        name="stage_integrals",
-    )(integrals)
 
 
 def place(plan, planes, parts, lam, tiles, line, places, sem, part_sem):
@@ -240,25 +217,54 @@
     return pltpu.VMEM((2 * plan.n_pair * plan.owned + plan.pairs, plan.cd), jnp.bfloat16)
 
 
-def early_kernel(plan, planes, *rest):
+def early_kernel(plan, planes, block, integrals, *rest):
+    parts, (lam, staged, *scratch, stage_sem) = rest[: len(planes)], rest[len(planes) :]
+    placing = place(plan, planes, parts, lam, *scratch)
+    next(placing)
+    copies = []
+    for i in range(plan.ab // block):
+        here = pl.ds(i * block, block)
+        copies.append(pltpu.make_async_copy(integrals.at[here], staged.at[here], stage_sem.at[i]))
+        copies[-1].start()
+    lam[...] = jnp.zeros(lam.shape, lam.dtype)
+    next(placing)
+    for copy in copies:
+        copy.wait()
+
+
+def place_early(plan, planes, parts, integrals, block=256):
+    integrals = pltpu.with_memory_space_constraint(integrals, pltpu.HBM)
+    return pl.pallas_call(
+        functools.partial(early_kernel, plan, planes, block),
+        out_shape=[lam_shape(plan), pltpu.VMEM(integrals.shape, integrals.dtype)],
+        in_specs=[HBM] * (1 + len(parts)),
+        out_specs=[VMEM, VMEM],
+        scratch_shapes=place_scratch(plan, planes) + [pltpu.SemaphoreType.DMA((plan.ab // block,))],
+        compiler_params=pltpu.CompilerParams(vmem_limit_bytes=12 * 1024 * 1024),
+        cost_estimate=cost(plan, 2 * plan.ab * plan.cd * 2),
+        name="place_early",
+    )(integrals, *parts)
+
+
+def more_kernel(plan, planes, _, *rest):
     parts, (lam, *scratch) = rest[: len(planes)], rest[len(planes) :]
     placing = place(plan, planes, parts, lam, *scratch)
     next(placing)
-    lam[...] = jnp.zeros(lam.shape, lam.dtype)
-    next(placing)
-
-
-def place_early(plan, planes, parts):
-    return pl.pallas_call(
-        functools.partial(early_kernel, plan, planes),
+    next(placing)
+
+
+def place_more(plan, lam, planes, parts):
+    return pl.pallas_call(
+        functools.partial(more_kernel, plan, planes),
         out_shape=lam_shape(plan),
-        in_specs=[HBM] * len(parts),
+        in_specs=[VMEM] + [HBM] * len(parts),
         out_specs=VMEM,
+        input_output_aliases={0: 0},
         scratch_shapes=place_scratch(plan, planes),
         compiler_params=pltpu.CompilerParams(vmem_limit_bytes=12 * 1024 * 1024),
-        cost_estimate=cost(plan, 8 * 1024 * 1024),
-        name="place_early",
-    )(*parts)
+        cost_estimate=cost(plan, 4 * 1024 * 1024),
+        name="place_more",
+    )(lam, *parts)
 
 
 def send_kernel(plan, planes, block, _, cols, *rest):
@@ -317,11 +323,6 @@
 
 def words_shape(plan):
     return (chunks_of(plan) // 2 * plan.owned + chunks_of(plan), plan.tile)
-
-
-def raised(x, power):
-    half = jnp.floor(power * 0.5)
-    return x * jnp.exp2(half) * jnp.exp2(power - half)
 
 
 def code_kernel(plan, keep, got, mine, *rest):
@@ -337,11 +338,12 @@
         most = jnp.zeros((rows, tile), jnp.float32)
         for j, part in enumerate(sums):
             most = jnp.where(lane == j, jnp.max(jnp.abs(part), axis=1, keepdims=True), most)
-        power = jnp.floor(jnp.log2(jnp.maximum(most, 2.0**-120)) + 1.001)
+        power = jnp.floor(jnp.log2(jnp.maximum(most, 2.0**-106)) + 1.001)
         square[:rows, :] = power
+        scale = jnp.exp2(15.0 - power)
         counts = []
         for j, part in enumerate(sums):
-            count = jnp.floor(raised(part, 15.0 - power[:, j : j + 1]) + 0.5)
+            count = jnp.floor(part * scale[:, j : j + 1] + 0.5)
             counts.append(jnp.clip(count, -32767.0, 32767.0).astype(jnp.int32))
         for j in range(chunks // 2):
             word = (counts[j] << 16) | (counts[j + chunks // 2] & 65535)
@@ -370,13 +372,13 @@
     square[...] = jnp.zeros(square.shape, jnp.float32)
     for ref in words:
         square[:chunks, :] = ref[chunks // 2 * rows :, :].astype(jnp.float32)
-        power = square[...].T[:rows, :] - 15.0
+        scale = jnp.exp2(square[...].T[:rows, :] - 15.0)
         for j in range(chunks):
             at = j % (chunks // 2) * rows
             word = ref[at : at + rows, :]
             count = (word if j < chunks // 2 else word << 16) >> 16
             cell = slice(j * tile, (j + 1) * tile)
-            out[:, cell] += raised(count.astype(jnp.float32), power[:, j : j + 1])
+            out[:, cell] += count.astype(jnp.float32) * scale[:, j : j + 1]
     out[...] = 0.5 * out[...]
 
 
@@ -409,18 +411,20 @@
     bit = plan.n_row // 2
     arrived = {0: packed, bit: swap(packed, "row", bit)}
     own = spread([0])
-    staged = stage(plan, integrals)
-    arrived[bit], own, staged = lax.optimization_barrier((arrived[bit], own, staged))
+    arrived[bit], own = lax.optimization_barrier((arrived[bit], own))
     while bit > 1:
         bit //= 2
         arrived.update({d | bit: swap(raw, "row", bit) for d, raw in arrived.items() if d or bit > 1})
     *middle, last = sorted(arrived)[1:]
     early = spread(middle)
-    arrived[last], early[1], own[0] = lax.optimization_barrier((arrived[last], early[1], own[0]))
+    planes = [((chip,), (0,)) for chip in chips]
+    lam, staged = place_early(plan, planes, own, integrals)
+    arrived[last], early[1], lam, staged = lax.optimization_barrier(
+        (arrived[last], early[1], lam, staged)
+    )
     near = swap(jnp.concatenate(own, axis=0), "row", 1)
     late = spread([last])
-    planes = [((chip,), (0,)) for chip in chips] + [((chip,), tuple(middle)) for chip in chips]
-    lam = place_early(plan, planes, own + early)
+    lam = place_more(plan, lam, [((chip,), tuple(middle)) for chip in chips], early)
     planes = [(chips, (1,))] + [((chip,), (last,)) for chip in chips]
     lam, send = send_product(plan, lam, planes, [near] + late, staged)
     got = swap(send, "col", 1)

time: 64.9 us -> 62.9 us (0.969)
  local copies, waits for them, and re-layouts: 5.1 us -> 0.12 us
  Pallas kernels: 17.4 us -> 19.7 us
  waiting for transfers between devices: 20.5 us -> 21.3 us
    unnamed x6 -> x0, local copies, waits for them, and re-layouts: 4.99 us -> none
    pallas_call x2, Pallas kernels: 4.04 us -> 6.09 us  [the longest x1 4.23 us: place_early(): pl.pallas_call(functools.partial(early_kernel, plan, planes, block), out_...]
    ppermute x19, waiting for transfers between devices: 20.5 us -> 21.3 us  [swap(): lax.ppermute(x, axis, [(i, i ^ m) for i in range(lax.axis_size(axis))])]
  transfers between devices with their start and end apart: 19 -> 19, of which waited for: 8 -> 9; matrix products, arithmetic and copies ran while one was open for 0% -> 0% of each run, Pallas kernels for 15% -> 19%
where the time goes in v5:
time: 62.9 us; the launch traced here: 62.7 us
  starting transfers between devices  21.5 us (34%)
  waiting for transfers between devices  21.3 us (34%)
  Pallas kernels  19.7 us (31%)
    ppermute x19, starting transfers between devices, swap(): lax.ppermute(x, axis, [(i, i ^ m) for i in range(lax.axis_size(axis))])  21.5 us
    ppermute x19, waiting for transfers between devices, swap(): lax.ppermute(x, axis, [(i, i ^ m) for i in range(lax.axis_size(axis))])  21.3 us
    pallas_call x1, Pallas kernels, send_product(): pl.pallas_call(functools.partial(send_kernel, plan, planes, block), out_s...  4.69 us
    pallas_call x1, Pallas kernels, place_early(): pl.pallas_call(functools.partial(early_kernel, plan, planes, block), out_...  4.23 us
    pallas_call x3, Pallas kernels, bucket(): pl.pallas_call(functools.partial(bucket_kernel, plan, count), out_shape=p...  3.45 us
    pallas_call x1, Pallas kernels, keep_product(): pl.pallas_call(functools.partial(keep_kernel, plan, block), out_shape=plt...  2.35 us
    pallas_call x1, Pallas kernels, place_more(): pl.pallas_call(functools.partial(more_kernel, plan, planes), out_shape=la...  1.86 us
  transfers between devices with their start and end apart: 19, of which 9 were waited for; matrix products, arithmetic and copies ran while one was open for 0% of the time, Pallas kernels for 19%

profile of v5, /device:TPU:0, one launch (start us, length us, event | category | flops | bytes accessed | tf_op | source)
XLA Modules:
  0.0 62.7 jit_solution(3825632201265318382)
XLA Ops:
  0.0 1.0 %pack_tiles.1.rest_0_ = bf16[1040,128]{1,0:T(8,128)(2,1)S(1)} custom-call(s32[1,64]{1,0:T(1,128)} %ids.1, bf16[1024,128]{1,0:T(8,128)(2,1)} %bitcast.1), custom_call_target="tpu_custom_call" | custom-call | bytes 532480 | tf_op jit(solution)/shard_map/pack_tiles/pallas_call | solution.py:82
  1.0 0.5 collective-permute-start.1
  1.5 3.7 %collective-permute-start = (bf16[1040,128]{1,0:T(8,128)(2,1)S(1)}, bf16[1040,128]{1,0:T(8,128)(2,1)S(1)}, u32[]{:S(2)}, u32[]{:S(2)}) collective-permute-start(bf16[1040,128]{1,0:T(8,128)(2,1)S(1)} %pack_tiles.1.rest_0_), channel_id=1, source_target_pairs={{0,16},{8,24},{16,0},{24,8},{1,17},{9,25},{17,1},{25,9},{2,18},{10... | collective-permute-start | bytes 798728 | tf_op jit(solution)/shard_map/ppermute | solution.py:399
  5.2 0.0 collective-permute-done.1.rest_1_
  5.2 1.2 %bucket_tiles.3 = bf16[2192,128]{1,0:T(8,128)(2,1)S(1)} custom-call(bf16[1040,128]{1,0:T(8,128)(2,1)S(1)} %pack_tiles.1.rest_0_, bf16[1040,128]{1,0:T(8,128)(2,1)S(1)} %collective-permute-done.1.rest_1_), custom_call_target="tpu_custom_call" | custom-call | bytes 2228224 | tf_op jit(solution)/shard_map/bucket_tiles/pallas_call | solution.py:148
  6.4 2.5 %collective-permute-start.4 = (bf16[544,128]{1,0:T(8,128)(2,1)S(1)}, bf16[544,128]{1,0:T(8,128)(2,1)S(1)}, u32[]{:S(2)}, u32[]{:S(2)}) collective-permute-start(bf16[544,128]{1,0:T(8,128)(2,1)S(1)} %get-tuple-element.47), channel_id=1, source_target_pairs={{0,6},{1,7},{2,4},{3,5},{4,2},{5,3},{6,0},{7,1},{8,14},{9,15},{10,... | collective-permute-start | bytes 417800 | tf_op jit(solution)/shard_map/ppermute | solution.py:399
  8.9 0.5 collective-permute-start.3
  9.4 0.5 collective-permute-start.2
  10.0 7.9 %collective-permute-done.rest_0_ = bf16[1040,128]{1,0:T(8,128)(2,1)S(1)} collective-permute-done((bf16[1040,128]{1,0:T(8,128)(2,1)S(1)}, bf16[1040,128]{1,0:T(8,128)(2,1)S(1)}, u32[]{:S(2)}, u32[]{:S(2)}) %collective-permute-start) | collective-permute-done | bytes 266272 | tf_op jit(solution)/shard_map/ppermute | solution.py:399
  17.9 0.0 collective-permute-done.4.rest_3_
  17.9 0.0 collective-permute-done.3.rest_2_
  17.9 0.0 collective-permute-done.2.rest_1_
  17.9 0.1 collective-permute-start.6
  18.0 0.8 %collective-permute-start.5 = (bf16[1040,128]{1,0:T(8,128)(2,1)S(1)}, bf16[1040,128]{1,0:T(8,128)(2,1)S(1)}, u32[]{:S(2)}, u32[]{:S(2)}) collective-permute-start(bf16[1040,128]{1,0:T(8,128)(2,1)S(1)} %collective-permute-done.rest_0_), channel_id=1, source_target_pairs={{0,8},{8,0},{16,24},{24,16},{1,9},{9,1},{17,25},{25,17},{2,10},{10... | collective-permute-start | bytes 798728 | tf_op jit(solution)/shard_map/ppermute | solution.py:399
  18.8 0.7 %collective-permute-done.6.rest_1_ = bf16[1040,128]{1,0:T(8,128)(2,1)S(1)} collective-permute-done((bf16[1040,128]{1,0:T(8,128)(2,1)S(1)}, bf16[1040,128]{1,0:T(8,128)(2,1)S(1)}, u32[]{:S(2)}, u32[]{:S(2)}) %collective-permute-start.6) | collective-permute-done | bytes 266272 | tf_op jit(solution)/shard_map/ppermute | solution.py:399
  19.5 1.2 %bucket_tiles.4 = bf16[2192,128]{1,0:T(8,128)(2,1)S(1)} custom-call(bf16[1040,128]{1,0:T(8,128)(2,1)S(1)} %collective-permute-done.rest_0_, bf16[1040,128]{1,0:T(8,128)(2,1)S(1)} %collective-permute-done.6.rest_1_), custom_call_target="tpu_custom_call" | custom-call | bytes 2228224 | tf_op jit(solution)/shard_map/bucket_tiles/pallas_call | solution.py:148
  20.7 1.6 %collective-permute-start.7 = (bf16[544,128]{1,0:T(8,128)(2,1)S(1)}, bf16[544,128]{1,0:T(8,128)(2,1)S(1)}, u32[]{:S(2)}, u32[]{:S(2)}) collective-permute-start(bf16[544,128]{1,0:T(8,128)(2,1)S(1)} %get-tuple-element.46), channel_id=1, source_target_pairs={{0,2},{1,3},{2,0},{3,1},{4,6},{5,7},{6,4},{7,5},{8,10},{9,11},{10,... | collective-permute-start | bytes 417800 | tf_op jit(solution)/shard_map/ppermute | solution.py:399
  22.3 4.2 %place_early.1 = (bf16[528,4096]{1,0:T(8,128)(2,1)S(1)}, bf16[1024,4096]{1,0:T(8,128)(2,1)S(1)}) custom-call(bf16[1024,4096]{1,0:T(8,128)(2,1)} %integrals.1, bf16[544,128]{1,0:T(8,128)(2,1)S(1)} %get-tuple-element.23.rest_0_, bf16[544,128]{1,0:T(8,128)(2,1)S(1)} %collective-permute-done.2.rest_1_, bf16[544,128]{1,0:T(8,128)(2,1)S(1)} %collective-permute-done.3.rest_2_, ...), custom_call_target="tpu_custom_call" | custom-call | bytes 16777216 | tf_op jit(solution)/shard_map/place_early/pallas_call | solution.py:237
  26.6 0.2 collective-permute-done.5.rest_0_
  26.8 0.0 collective-permute-done.7.rest_1_
  26.8 0.0 collective-permute-start.11
  26.8 0.8 %collective-permute-start.10 = (bf16[2176,128]{1,0:T(8,128)(2,1)S(1)}, bf16[2176,128]{1,0:T(8,128)(2,1)S(1)}, u32[]{:S(2)}, u32[]{:S(2)}) collective-permute-start(bf16[2176,128]{1,0:T(8,128)(2,1)S(1)} %pad_maximum_fusion), channel_id=1, source_target_pairs={{0,8},{8,0},{16,24},{24,16},{1,9},{9,1},{17,25},{25,17},{2,10},{10... | collective-permute-start | bytes 1671176 | tf_op jit(solution)/shard_map/ppermute | solution.py:399
  27.7 2.4 %collective-permute-start.9 = (bf16[544,128]{1,0:T(8,128)(2,1)S(1)}, bf16[544,128]{1,0:T(8,128)(2,1)S(1)}, u32[]{:S(2)}, u32[]{:S(2)}) collective-permute-start(bf16[544,128]{1,0:T(8,128)(2,1)S(1)} %get-tuple-element.43), channel_id=1, source_target_pairs={{0,6},{1,7},{2,4},{3,5},{4,2},{5,3},{6,0},{7,1},{8,14},{9,15},{10,... | collective-permute-start | bytes 417800 | tf_op jit(solution)/shard_map/ppermute | solution.py:399
  30.1 0.5 collective-permute-start.8
  30.6 0.0 collective-permute-done.11.rest_1_
  30.6 1.2 %bucket_tiles.5 = bf16[2192,128]{1,0:T(8,128)(2,1)S(1)} custom-call(bf16[1040,128]{1,0:T(8,128)(2,1)S(1)} %collective-permute-done.5.rest_0_, bf16[1040,128]{1,0:T(8,128)(2,1)S(1)} %collective-permute-done.11.rest_1_), custom_call_target="tpu_custom_call" | custom-call | bytes 2228224 | tf_op jit(solution)/shard_map/bucket_tiles/pallas_call | solution.py:148
  31.8 1.6 %collective-permute-start.14 = (bf16[544,128]{1,0:T(8,128)(2,1)S(1)}, bf16[544,128]{1,0:T(8,128)(2,1)S(1)}, u32[]{:S(2)}, u32[]{:S(2)}) collective-permute-start(bf16[544,128]{1,0:T(8,128)(2,1)S(1)} %get-tuple-element.39), channel_id=1, source_target_pairs={{0,6},{1,7},{2,4},{3,5},{4,2},{5,3},{6,0},{7,1},{8,14},{9,15},{10,... | collective-permute-start | bytes 417800 | tf_op jit(solution)/shard_map/ppermute | solution.py:399
  33.4 0.5 collective-permute-start.13
  33.9 0.6 collective-permute-done.9.rest_3_
  34.5 1.7 %collective-permute-start.12 = (bf16[544,128]{1,0:T(8,128)(2,1)S(1)}, bf16[544,128]{1,0:T(8,128)(2,1)S(1)}, u32[]{:S(2)}, u32[]{:S(2)}) collective-permute-start(bf16[544,128]{1,0:T(8,128)(2,1)S(1)} %get-tuple-element.41), channel_id=1, source_target_pairs={{0,2},{1,3},{2,0},{3,1},{4,6},{5,7},{6,4},{7,5},{8,10},{9,11},{10,... | collective-permute-start | bytes 417800 | tf_op jit(solution)/shard_map/ppermute | solution.py:399
  36.2 4.2 %collective-permute-done.8.rest_2_ = bf16[544,128]{1,0:T(8,128)(2,1)S(1)} collective-permute-done((bf16[544,128]{1,0:T(8,128)(2,1)S(1)}, bf16[544,128]{1,0:T(8,128)(2,1)S(1)}, u32[]{:S(2)}, u32[]{:S(2)}) %collective-permute-start.8) | collective-permute-done | bytes 139296 | tf_op jit(solution)/shard_map/ppermute | solution.py:399
  40.4 1.9 %place_more.1._ = bf16[528,4096]{1,0:T(8,128)(2,1)S(1)} custom-call(bf16[528,4096]{1,0:T(8,128)(2,1)S(1)} %get-tuple-element.29._, bf16[544,128]{1,0:T(8,128)(2,1)S(1)} %get-tuple-element.45.rest_0_, bf16[544,128]{1,0:T(8,128)(2,1)S(1)} %collective-permute-done.7.rest_1_, ...), custom_call_target="tpu_custom_call", output_to_operand_aliasing={{}: (0, {})} | custom-call | bytes 4194304 | tf_op jit(solution)/shard_map/place_more/pallas_call | solution.py:257
  42.3 0.0 collective-permute-done.10.rest_0_
  42.3 0.0 collective-permute-done.14.rest_4_
  42.3 1.0 %collective-permute-done.13.rest_3_ = bf16[544,128]{1,0:T(8,128)(2,1)S(1)} collective-permute-done((bf16[544,128]{1,0:T(8,128)(2,1)S(1)}, bf16[544,128]{1,0:T(8,128)(2,1)S(1)}, u32[]{:S(2)}, u32[]{:S(2)}) %collective-permute-start.13) | collective-permute-done | bytes 139296 | tf_op jit(solution)/shard_map/ppermute | solution.py:399
  43.3 0.0 collective-permute-done.12.rest_2_
  43.3 4.7 %place_and_multiply.1 = (bf16[528,4096]{1,0:T(8,128)(2,1)S(1)}, f32[256,1024]{1,0:T(8,128)S(1)}) custom-call(bf16[528,4096]{1,0:T(8,128)(2,1)S(1)} %place_more.1._, bf16[1024,4096]{1,0:T(8,128)(2,1)S(1)} %get-tuple-element.31.cols, bf16[2176,128]{1,0:T(8,128)(2,1)S(1)} %collective-permute-done.10.rest_0_, ...), custom_call_target="tpu_custom_call", output_to_operand_aliasing={{0}: (0, {})} | custom-call | flops 4294967296 | bytes 16777216 | tf_op jit(solution)/shard_map/place_and_multiply/pallas_call | solution.py:280
  48.0 0.1 collective-permute-start.15
  48.1 2.4 %multiply_kept.1.keep = f32[256,1024]{1,0:T(8,128)S(1)} custom-call(bf16[528,4096]{1,0:T(8,128)(2,1)S(1)} %get-tuple-element.33.lam, bf16[1024,4096]{1,0:T(8,128)(2,1)S(1)} %get-tuple-element.31.cols), custom_call_target="tpu_custom_call" | custom-call | flops 2147483648 | bytes 10485760 | tf_op jit(solution)/shard_map/multiply_kept/pallas_call | solution.py:309
  50.5 0.3 collective-permute-done.15.got
  50.7 0.9 %code_sums.1 = (f32[64,1024]{1,0:T(8,128)S(1)}, s32[264,128]{1,0:T(8,128)S(1)}, s32[264,128]{1,0:T(8,128)S(1)}, s32[264,128]{1,0:T(8,128)S(1)}) custom-call(f32[256,1024]{1,0:T(8,128)S(1)} %multiply_kept.1.keep, f32[256,1024]{1,0:T(8,128)S(1)} %collective-permute-done.15.got), custom_call_target="tpu_custom_call" | custom-call | bytes 4194304 | tf_op jit(solution)/shard_map/code_sums/pallas_call | solution.py:356
  51.7 1.6 %collective-permute-start.16 = (s32[264,128]{1,0:T(8,128)S(1)}, s32[264,128]{1,0:T(8,128)S(1)}, u32[]{:S(2)}, u32[]{:S(2)}) collective-permute-start(s32[264,128]{1,0:T(8,128)S(1)} %get-tuple-element.36), channel_id=1, source_target_pairs={{0,2},{1,3},{2,0},{3,1},{4,6},{5,7},{6,4},{7,5},{8,10},{9,11},{10,... | collective-permute-start | bytes 405512 | tf_op jit(solution)/shard_map/ppermute | solution.py:399
  53.2 0.8 %collective-permute-start.17 = (s32[264,128]{1,0:T(8,128)S(1)}, s32[264,128]{1,0:T(8,128)S(1)}, u32[]{:S(2)}, u32[]{:S(2)}) collective-permute-start(s32[264,128]{1,0:T(8,128)S(1)} %get-tuple-element.37), channel_id=1, source_target_pairs={{0,4},{1,5},{2,6},{3,7},{4,0},{5,1},{6,2},{7,3},{8,12},{9,13},{10,... | collective-permute-start | bytes 405512 | tf_op jit(solution)/shard_map/ppermute | solution.py:399
  54.0 1.2 %collective-permute-start.18 = (s32[264,128]{1,0:T(8,128)S(1)}, s32[264,128]{1,0:T(8,128)S(1)}, u32[]{:S(2)}, u32[]{:S(2)}) collective-permute-start(s32[264,128]{1,0:T(8,128)S(1)} %get-tuple-element.38), channel_id=1, source_target_pairs={{0,6},{1,7},{2,4},{3,5},{4,2},{5,3},{6,0},{7,1},{8,14},{9,15},{10,... | collective-permute-start | bytes 405512 | tf_op jit(solution)/shard_map/ppermute | solution.py:399
  55.2 2.7 %collective-permute-done.16.rest_0_ = s32[264,128]{1,0:T(8,128)S(1)} collective-permute-done((s32[264,128]{1,0:T(8,128)S(1)}, s32[264,128]{1,0:T(8,128)S(1)}, u32[]{:S(2)}, u32[]{:S(2)}) %collective-permute-start.16) | collective-permute-done | bytes 135200 | tf_op jit(solution)/shard_map/ppermute | solution.py:399
  57.9 3.7 %collective-permute-done.17.rest_1_ = s32[264,128]{1,0:T(8,128)S(1)} collective-permute-done((s32[264,128]{1,0:T(8,128)S(1)}, s32[264,128]{1,0:T(8,128)S(1)}, u32[]{:S(2)}, u32[]{:S(2)}) %collective-permute-start.17) | collective-permute-done | bytes 135200 | tf_op jit(solution)/shard_map/ppermute | solution.py:399
  61.6 0.0 collective-permute-done.18.rest_2_
  61.6 1.2 %total_sums.1 = f32[64,1024]{1,0:T(8,128)} custom-call(f32[64,1024]{1,0:T(8,128)S(1)} %get-tuple-element.35.mine, s32[264,128]{1,0:T(8,128)S(1)} %collective-permute-done.16.rest_0_, s32[264,128]{1,0:T(8,128)S(1)} %collective-permute-done.17.rest_1_, s32[264,128]{1,0:T(8,128)S(1)} %collective-permute-done.18.rest_2_), custom_call_target="tpu_custom_call" | custom-call | bytes 4194304 | tf_op jit(solution)/shard_map/total_sums/pallas_call | solution.py:386
  (4 shorter events, 0.2 us)
Async XLA Ops:
  1.0 4.2 %collective-permute-start.1 = (bf16[1040,128]{1,0:T(8,128)(2,1)S(1)}, bf16[1040,128]{1,0:T(8,128)(2,1)S(1)}, u32[]{:S(2)}, u32[]{:S(2)}) collective-permute-start(bf16[1040,128]{1,0:T(8,128)(2,1)S(1)} %pack_tiles.1.rest_0_), channel_id=1, source_target_pairs={{0,1},{1,0},{2,3},{3,2},{4,5},{5,4},{6,7},{7,6},{8,9},{9,8},{10,11... | collective-permute-start | bytes 798728 | tf_op jit(solution)/shard_map/ppermute | solution.py:399
  1.5 16.4 %collective-permute-start = (bf16[1040,128]{1,0:T(8,128)(2,1)S(1)}, bf16[1040,128]{1,0:T(8,128)(2,1)S(1)}, u32[]{:S(2)}, u32[]{:S(2)}) collective-permute-start(bf16[1040,128]{1,0:T(8,128)(2,1)S(1)} %pack_tiles.1.rest_0_), channel_id=1, source_target_pairs={{0,16},{8,24},{16,0},{24,8},{1,17},{9,25},{17,1},{25,9},{2,18},{10... | collective-permute-start | bytes 798728 | tf_op jit(solution)/shard_map/ppermute | solution.py:399
  6.4 11.5 %collective-permute-start.4 = (bf16[544,128]{1,0:T(8,128)(2,1)S(1)}, bf16[544,128]{1,0:T(8,128)(2,1)S(1)}, u32[]{:S(2)}, u32[]{:S(2)}) collective-permute-start(bf16[544,128]{1,0:T(8,128)(2,1)S(1)} %get-tuple-element.47), channel_id=1, source_target_pairs={{0,6},{1,7},{2,4},{3,5},{4,2},{5,3},{6,0},{7,1},{8,14},{9,15},{10,... | collective-permute-start | bytes 417800 | tf_op jit(solution)/shard_map/ppermute | solution.py:399
  8.9 9.0 %collective-permute-start.3 = (bf16[544,128]{1,0:T(8,128)(2,1)S(1)}, bf16[544,128]{1,0:T(8,128)(2,1)S(1)}, u32[]{:S(2)}, u32[]{:S(2)}) collective-permute-start(bf16[544,128]{1,0:T(8,128)(2,1)S(1)} %get-tuple-element.48), channel_id=1, source_target_pairs={{0,4},{1,5},{2,6},{3,7},{4,0},{5,1},{6,2},{7,3},{8,12},{9,13},{10,... | collective-permute-start | bytes 417800 | tf_op jit(solution)/shard_map/ppermute | solution.py:399
  9.4 8.5 %collective-permute-start.2 = (bf16[544,128]{1,0:T(8,128)(2,1)S(1)}, bf16[544,128]{1,0:T(8,128)(2,1)S(1)}, u32[]{:S(2)}, u32[]{:S(2)}) collective-permute-start(bf16[544,128]{1,0:T(8,128)(2,1)S(1)} %get-tuple-element.49), channel_id=1, source_target_pairs={{0,2},{1,3},{2,0},{3,1},{4,6},{5,7},{6,4},{7,5},{8,10},{9,11},{10,... | collective-permute-start | bytes 417800 | tf_op jit(solution)/shard_map/ppermute | solution.py:399
  17.9 1.6 %collective-permute-start.6 = (bf16[1040,128]{1,0:T(8,128)(2,1)S(1)}, bf16[1040,128]{1,0:T(8,128)(2,1)S(1)}, u32[]{:S(2)}, u32[]{:S(2)}) collective-permute-start(bf16[1040,128]{1,0:T(8,128)(2,1)S(1)} %collective-permute-done.rest_0_), channel_id=1, source_target_pairs={{0,1},{1,0},{2,3},{3,2},{4,5},{5,4},{6,7},{7,6},{8,9},{9,8},{10,11... | collective-permute-start | bytes 798728 | tf_op jit(solution)/shard_map/ppermute | solution.py:399
  18.0 8.8 %collective-permute-start.5 = (bf16[1040,128]{1,0:T(8,128)(2,1)S(1)}, bf16[1040,128]{1,0:T(8,128)(2,1)S(1)}, u32[]{:S(2)}, u32[]{:S(2)}) collective-permute-start(bf16[1040,128]{1,0:T(8,128)(2,1)S(1)} %collective-permute-done.rest_0_), channel_id=1, source_target_pairs={{0,8},{8,0},{16,24},{24,16},{1,9},{9,1},{17,25},{25,17},{2,10},{10... | collective-permute-start | bytes 798728 | tf_op jit(solution)/shard_map/ppermute | solution.py:399
  20.7 6.1 %collective-permute-start.7 = (bf16[544,128]{1,0:T(8,128)(2,1)S(1)}, bf16[544,128]{1,0:T(8,128)(2,1)S(1)}, u32[]{:S(2)}, u32[]{:S(2)}) collective-permute-start(bf16[544,128]{1,0:T(8,128)(2,1)S(1)} %get-tuple-element.46), channel_id=1, source_target_pairs={{0,2},{1,3},{2,0},{3,1},{4,6},{5,7},{6,4},{7,5},{8,10},{9,11},{10,... | collective-permute-start | bytes 417800 | tf_op jit(solution)/shard_map/ppermute | solution.py:399
  26.8 3.8 %collective-permute-start.11 = (bf16[1040,128]{1,0:T(8,128)(2,1)S(1)}, bf16[1040,128]{1,0:T(8,128)(2,1)S(1)}, u32[]{:S(2)}, u32[]{:S(2)}) collective-permute-start(bf16[1040,128]{1,0:T(8,128)(2,1)S(1)} %collective-permute-done.5.rest_0_), channel_id=1, source_target_pairs={{0,1},{1,0},{2,3},{3,2},{4,5},{5,4},{6,7},{7,6},{8,9},{9,8},{10,11... | collective-permute-start | bytes 798728 | tf_op jit(solution)/shard_map/ppermute | solution.py:399
  26.8 15.5 %collective-permute-start.10 = (bf16[2176,128]{1,0:T(8,128)(2,1)S(1)}, bf16[2176,128]{1,0:T(8,128)(2,1)S(1)}, u32[]{:S(2)}, u32[]{:S(2)}) collective-permute-start(bf16[2176,128]{1,0:T(8,128)(2,1)S(1)} %pad_maximum_fusion), channel_id=1, source_target_pairs={{0,8},{8,0},{16,24},{24,16},{1,9},{9,1},{17,25},{25,17},{2,10},{10... | collective-permute-start | bytes 1671176 | tf_op jit(solution)/shard_map/ppermute | solution.py:399
  27.7 6.8 %collective-permute-start.9 = (bf16[544,128]{1,0:T(8,128)(2,1)S(1)}, bf16[544,128]{1,0:T(8,128)(2,1)S(1)}, u32[]{:S(2)}, u32[]{:S(2)}) collective-permute-start(bf16[544,128]{1,0:T(8,128)(2,1)S(1)} %get-tuple-element.43), channel_id=1, source_target_pairs={{0,6},{1,7},{2,4},{3,5},{4,2},{5,3},{6,0},{7,1},{8,14},{9,15},{10,... | collective-permute-start | bytes 417800 | tf_op jit(solution)/shard_map/ppermute | solution.py:399
  30.1 10.3 %collective-permute-start.8 = (bf16[544,128]{1,0:T(8,128)(2,1)S(1)}, bf16[544,128]{1,0:T(8,128)(2,1)S(1)}, u32[]{:S(2)}, u32[]{:S(2)}) collective-permute-start(bf16[544,128]{1,0:T(8,128)(2,1)S(1)} %get-tuple-element.44), channel_id=1, source_target_pairs={{0,4},{1,5},{2,6},{3,7},{4,0},{5,1},{6,2},{7,3},{8,12},{9,13},{10,... | collective-permute-start | bytes 417800 | tf_op jit(solution)/shard_map/ppermute | solution.py:399
  31.8 10.5 %collective-permute-start.14 = (bf16[544,128]{1,0:T(8,128)(2,1)S(1)}, bf16[544,128]{1,0:T(8,128)(2,1)S(1)}, u32[]{:S(2)}, u32[]{:S(2)}) collective-permute-start(bf16[544,128]{1,0:T(8,128)(2,1)S(1)} %get-tuple-element.39), channel_id=1, source_target_pairs={{0,6},{1,7},{2,4},{3,5},{4,2},{5,3},{6,0},{7,1},{8,14},{9,15},{10,... | collective-permute-start | bytes 417800 | tf_op jit(solution)/shard_map/ppermute | solution.py:399
  33.4 9.9 %collective-permute-start.13 = (bf16[544,128]{1,0:T(8,128)(2,1)S(1)}, bf16[544,128]{1,0:T(8,128)(2,1)S(1)}, u32[]{:S(2)}, u32[]{:S(2)}) collective-permute-start(bf16[544,128]{1,0:T(8,128)(2,1)S(1)} %get-tuple-element.40), channel_id=1, source_target_pairs={{0,4},{1,5},{2,6},{3,7},{4,0},{5,1},{6,2},{7,3},{8,12},{9,13},{10,... | collective-permute-start | bytes 417800 | tf_op jit(solution)/shard_map/ppermute | solution.py:399
  34.5 8.9 %collective-permute-start.12 = (bf16[544,128]{1,0:T(8,128)(2,1)S(1)}, bf16[544,128]{1,0:T(8,128)(2,1)S(1)}, u32[]{:S(2)}, u32[]{:S(2)}) collective-permute-start(bf16[544,128]{1,0:T(8,128)(2,1)S(1)} %get-tuple-element.41), channel_id=1, source_target_pairs={{0,2},{1,3},{2,0},{3,1},{4,6},{5,7},{6,4},{7,5},{8,10},{9,11},{10,... | collective-permute-start | bytes 417800 | tf_op jit(solution)/shard_map/ppermute | solution.py:399
  48.0 2.7 %collective-permute-start.15 = (f32[256,1024]{1,0:T(8,128)S(1)}, f32[256,1024]{1,0:T(8,128)S(1)}, u32[]{:S(2)}, u32[]{:S(2)}) collective-permute-start(f32[256,1024]{1,0:T(8,128)S(1)} %get-tuple-element.34), channel_id=1, source_target_pairs={{0,1},{1,0},{2,3},{3,2},{4,5},{5,4},{6,7},{7,6},{8,9},{9,8},{10,11... | collective-permute-start | bytes 3145736 | tf_op jit(solution)/shard_map/ppermute | solution.py:399
  51.7 6.2 %collective-permute-start.16 = (s32[264,128]{1,0:T(8,128)S(1)}, s32[264,128]{1,0:T(8,128)S(1)}, u32[]{:S(2)}, u32[]{:S(2)}) collective-permute-start(s32[264,128]{1,0:T(8,128)S(1)} %get-tuple-element.36), channel_id=1, source_target_pairs={{0,2},{1,3},{2,0},{3,1},{4,6},{5,7},{6,4},{7,5},{8,10},{9,11},{10,... | collective-permute-start | bytes 405512 | tf_op jit(solution)/shard_map/ppermute | solution.py:399
  53.2 8.3 %collective-permute-start.17 = (s32[264,128]{1,0:T(8,128)S(1)}, s32[264,128]{1,0:T(8,128)S(1)}, u32[]{:S(2)}, u32[]{:S(2)}) collective-permute-start(s32[264,128]{1,0:T(8,128)S(1)} %get-tuple-element.37), channel_id=1, source_target_pairs={{0,4},{1,5},{2,6},{3,7},{4,0},{5,1},{6,2},{7,3},{8,12},{9,13},{10,... | collective-permute-start | bytes 405512 | tf_op jit(solution)/shard_map/ppermute | solution.py:399
  54.0 7.5 %collective-permute-start.18 = (s32[264,128]{1,0:T(8,128)S(1)}, s32[264,128]{1,0:T(8,128)S(1)}, u32[]{:S(2)}, u32[]{:S(2)}) collective-permute-start(s32[264,128]{1,0:T(8,128)S(1)} %get-tuple-element.38), channel_id=1, source_target_pairs={{0,6},{1,7},{2,4},{3,5},{4,2},{5,3},{6,0},{7,1},{8,14},{9,15},{10,... | collective-permute-start | bytes 405512 | tf_op jit(solution)/shard_map/ppermute | solution.py:399

commit v6 on v5

--- a/solution.py
+++ b/solution.py
@@ -99,9 +99,9 @@
     return pl.CostEstimate(flops=flops, bytes_accessed=moved, transcendentals=0)
 
 
-def bucket_kernel(plan, count, *rest):
+def bucket_kernel(plan, count, both, *rest):
     packed, (buf, bodies, tops, heads, line, places, sem) = rest[:count], rest[count:]
-    rows, piece = plan.pairs, count * plan.bucket
+    rows, piece = plan.pairs, (2 if both else count) * plan.bucket
     loads = []
     for i, ref in enumerate(packed):
         top = tops.at[pl.ds(i * plan.head, plan.head)]
@@ -118,13 +118,17 @@
         heads[i * plan.head : (i + 1) * plan.head, :] = head
         slot = head[plan.n_col : plan.n_col + 1, :].astype(jnp.int32)
         m = (slot >> shift_of(CAP)) ^ col
-        at = (m >> 1) * piece + i * plan.bucket + (slot & (CAP - 1)) * rows
-        line[i : i + 1, :] = jnp.where((m & 1) == 0, at, plan.n_pair * piece)
+        at = (m >> 1) * piece + (slot & (CAP - 1)) * rows
+        if both:
+            line[i : i + 1, :] = at + (m & 1) * plan.bucket
+        else:
+            line[i : i + 1, :] = jnp.where((m & 1) == 0, at + i * plan.bucket, plan.n_pair * piece)
     copy = pltpu.make_async_copy(line, places, sem.at[2 * count])
     copy.start()
-    for i in range(count):
+    for i in range(2 if both else count):
         for chip in range(plan.n_pair):
-            ids = heads[pl.ds(i * plan.head + (col ^ (2 * chip)), 1), :]
+            at_line = (col ^ (2 * chip + i)) if both else i * plan.head + (col ^ (2 * chip))
+            ids = heads[pl.ds(at_line, 1), :]
             at = chip * piece + i * plan.bucket + CAP * rows
             buf[at : at + rows, :] = jnp.broadcast_to(ids, (rows, plan.tile)).astype(jnp.bfloat16)
     copy.wait()
@@ -140,13 +144,13 @@
         lax.fori_loop(0, plan.slots, step, 0, unroll=16)
 
 
-def bucket(plan, packed):
+def bucket(plan, packed, both=False):
     count = len(packed)
-    piece = count * plan.bucket
+    piece = (2 if both else count) * plan.bucket
     lines = -(-count // 8) * 8
     bf16 = jnp.bfloat16
     out = pl.pallas_call(
-        functools.partial(bucket_kernel, plan, count),
+        functools.partial(bucket_kernel, plan, count, both),
         out_shape=pltpu.VMEM((plan.n_pair * piece + plan.pairs, plan.tile), bf16),
         in_specs=[HBM] * count,
         out_specs=VMEM,
@@ -169,12 +173,15 @@
     rows = plan.pairs
     half = plan.n_pair * plan.owned
     sources, loads, at = [], [], 0
-    for ref, (chips, ds) in zip(parts, planes, strict=True):
-        loads.append(pltpu.make_async_copy(ref, tiles.at[pl.ds(at, ref.shape[0])], part_sem.at[len(loads)]))
+    for ref, (chips, ds, *sides) in zip(parts, planes, strict=True):
+        sides = sides or (0, 1)
+        size = len(chips) * len(ds) * len(sides) * plan.bucket
+        here = tiles.at[pl.ds(at, size)]
+        loads.append(pltpu.make_async_copy(ref.at[pl.ds(0, size)], here, part_sem.at[len(loads)]))
         loads[-1].start()
         for chip in chips:
             for d in ds:
-                for side in range(2):
+                for side in sides:
                     sources.append((at, d, 2 * chip + side))
                     at += plan.bucket
     yield
@@ -202,7 +209,7 @@
 
 
 def place_scratch(plan, planes):
-    count = sum(2 * len(chips) * len(ds) for chips, ds in planes)
+    count = sum(len(chips) * len(ds) * len(sides or (0, 1)) for chips, ds, *sides in planes)
     lines = -(-count // 8) * 8
     return [
         pltpu.VMEM((count * plan.bucket, plan.tile), jnp.bfloat16),
@@ -217,33 +224,49 @@
     return pltpu.VMEM((2 * plan.n_pair * plan.owned + plan.pairs, plan.cd), jnp.bfloat16)
 
 
-def early_kernel(plan, planes, block, integrals, *rest):
-    parts, (lam, staged, *scratch, stage_sem) = rest[: len(planes)], rest[len(planes) :]
-    placing = place(plan, planes, parts, lam, *scratch)
-    next(placing)
+def stage_kernel(plan, block, integrals, staged, sem):
     copies = []
     for i in range(plan.ab // block):
         here = pl.ds(i * block, block)
-        copies.append(pltpu.make_async_copy(integrals.at[here], staged.at[here], stage_sem.at[i]))
+        copies.append(pltpu.make_async_copy(integrals.at[here], staged.at[here], sem.at[i]))
         copies[-1].start()
-    lam[...] = jnp.zeros(lam.shape, lam.dtype)
-    next(placing)
     for copy in copies:
         copy.wait()
 
 
-def place_early(plan, planes, parts, integrals, block=256):
+def stage(plan, integrals, block=256):
     integrals = pltpu.with_memory_space_constraint(integrals, pltpu.HBM)
     return pl.pallas_call(
-        functools.partial(early_kernel, plan, planes, block),
-        out_shape=[lam_shape(plan), pltpu.VMEM(integrals.shape, integrals.dtype)],
-        in_specs=[HBM] * (1 + len(parts)),
-        out_specs=[VMEM, VMEM],
-        scratch_shapes=place_scratch(plan, planes) + [pltpu.SemaphoreType.DMA((plan.ab // block,))],
+        functools.partial(stage_kernel, plan, block),
+        out_shape=pltpu.VMEM(integrals.shape, integrals.dtype),
+        in_specs=[HBM],
+        out_specs=VMEM,
+        scratch_shapes=[pltpu.SemaphoreType.DMA((plan.ab // block,))],
+        compiler_params=pltpu.CompilerParams(vmem_limit_bytes=2 * 1024 * 1024),
+        cost_estimate=cost(plan, 2 * plan.ab * plan.cd * 2),
+        name="stage_integrals",
+    )(integrals)
+
+
+def early_kernel(plan, planes, *rest):
+    parts, (lam, *scratch) = rest[: len(planes)], rest[len(planes) :]
+    placing = place(plan, planes, parts, lam, *scratch)
+    next(placing)
+    lam[...] = jnp.zeros(lam.shape, lam.dtype)
+    next(placing)
+
+
+def place_early(plan, planes, parts):
+    return pl.pallas_call(
+        functools.partial(early_kernel, plan, planes),
+        out_shape=lam_shape(plan),
+        in_specs=[HBM] * len(parts),
+        out_specs=VMEM,
+        scratch_shapes=place_scratch(plan, planes),
         compiler_params=pltpu.CompilerParams(vmem_limit_bytes=12 * 1024 * 1024),
-        cost_estimate=cost(plan, 2 * plan.ab * plan.cd * 2),
+        cost_estimate=cost(plan, 4 * 1024 * 1024),
         name="place_early",
-    )(integrals, *parts)
+    )(*parts)
 
 
 def more_kernel(plan, planes, _, *rest):
@@ -366,20 +389,27 @@
 
 
 def total_kernel(plan, mine, *rest):
-    words, (out, square) = rest[:-2], rest[-2:]
+    words, (out, sums, square, sem) = rest[:-4], rest[-4:]
     rows, tile, chunks = plan.owned, plan.tile, chunks_of(plan)
-    out[...] = mine[...]
     square[...] = jnp.zeros(square.shape, jnp.float32)
+    scales = []
     for ref in words:
         square[:chunks, :] = ref[chunks // 2 * rows :, :].astype(jnp.float32)
-        scale = jnp.exp2(square[...].T[:rows, :] - 15.0)
-        for j in range(chunks):
-            at = j % (chunks // 2) * rows
+        scales.append(jnp.exp2(square[...].T[:rows, :] - 16.0))
+    copies = []
+    for j in range(chunks):
+        cell = slice(j * tile, (j + 1) * tile)
+        at = j % (chunks // 2) * rows
+        total = 0.5 * mine[:, cell]
+        for ref, scale in zip(words, scales, strict=True):
             word = ref[at : at + rows, :]
             count = (word if j < chunks // 2 else word << 16) >> 16
-            cell = slice(j * tile, (j + 1) * tile)
-            out[:, cell] += count.astype(jnp.float32) * scale[:, j : j + 1]
-    out[...] = 0.5 * out[...]
+            total += count.astype(jnp.float32) * scale[:, j : j + 1]
+        sums[:, cell] = total
+        copies.append(pltpu.make_async_copy(sums.at[:, cell], out.at[:, cell], sem.at[j]))
+        copies[-1].start()
+    for copy in copies:
+        copy.wait()
 
 
 def total_sums(plan, mine, words):
@@ -387,8 +417,12 @@
         functools.partial(total_kernel, plan),
         out_shape=jax.ShapeDtypeStruct((plan.owned, plan.ab), jnp.float32),
         in_specs=[VMEM] * (1 + len(words)),
-        out_specs=VMEM,
-        scratch_shapes=[pltpu.VMEM((plan.tile, plan.tile), jnp.float32)],
+        out_specs=HBM,
+        scratch_shapes=[
+            pltpu.VMEM((plan.owned, plan.ab), jnp.float32),
+            pltpu.VMEM((plan.tile, plan.tile), jnp.float32),
+            pltpu.SemaphoreType.DMA((chunks_of(plan),)),
+        ],
         compiler_params=pltpu.CompilerParams(vmem_limit_bytes=20 * 1024 * 1024),
         cost_estimate=cost(plan, 4 * plan.n_pair * plan.owned * plan.ab * 4),
         name="total_sums",
@@ -411,22 +445,24 @@
     bit = plan.n_row // 2
     arrived = {0: packed, bit: swap(packed, "row", bit)}
     own = spread([0])
-    arrived[bit], own = lax.optimization_barrier((arrived[bit], own))
+    staged = stage(plan, integrals)
+    arrived[bit], own, staged = lax.optimization_barrier((arrived[bit], own, staged))
     while bit > 1:
         bit //= 2
         arrived.update({d | bit: swap(raw, "row", bit) for d, raw in arrived.items() if d or bit > 1})
     *middle, last = sorted(arrived)[1:]
     early = spread(middle)
-    planes = [((chip,), (0,)) for chip in chips]
-    lam, staged = place_early(plan, planes, own, integrals)
-    arrived[last], early[1], lam, staged = lax.optimization_barrier(
-        (arrived[last], early[1], lam, staged)
-    )
+    arrived[last], early[1] = lax.optimization_barrier((arrived[last], early[1]))
     near = swap(jnp.concatenate(own, axis=0), "row", 1)
-    late = spread([last])
+    late = bucket(plan, [arrived[last]], both=True)
+    late = [late[0]] + [swap(late[m], "col", 2 * m) for m in range(1, plan.n_pair)]
+    lam = place_early(plan, [((chip,), (0,)) for chip in chips], own)
     lam = place_more(plan, lam, [((chip,), tuple(middle)) for chip in chips], early)
-    planes = [(chips, (1,))] + [((chip,), (last,)) for chip in chips]
-    lam, send = send_product(plan, lam, planes, [near] + late, staged)
+    late, lam, near = lax.optimization_barrier((late, lam, near))
+    cross = swap(jnp.concatenate([part[plan.bucket :] for part in late], axis=0), "col", 1)
+    lam = place_more(plan, lam, [(chips, (1,))], [near])
+    planes = [((chip,), (last,), 0) for chip in chips] + [(chips, (last,), 1)]
+    lam, send = send_product(plan, lam, planes, late + [cross], staged)
     got = swap(send, "col", 1)
     keep = keep_product(plan, lam, staged)
     mine, *words = code_sums(plan, keep, got)

time: 62.9 us -> 59 us (0.938)
  waiting for transfers between devices: 21.3 us -> 16.2 us
  Pallas kernels: 19.7 us -> 20.9 us
    ppermute x19, waiting for transfers between devices: 21.3 us -> 16.2 us  [swap(): lax.ppermute(x, axis, [(i, i ^ m) for i in range(lax.axis_size(axis))])]
    pallas_call x1 -> x2, Pallas kernels: 1.86 us -> 3.06 us  [place_more(): pl.pallas_call(functools.partial(more_kernel, plan, planes), out_shape=la...]
    pallas_call x4 -> x5, Pallas kernels: 7.68 us -> 8.75 us  [the longest x1 3.5 us: stage(): pl.pallas_call(functools.partial(stage_kernel, plan, block), out_shape=pl...]
    pallas_call x1, Pallas kernels: 4.69 us -> 3.76 us  [send_product(): pl.pallas_call(functools.partial(send_kernel, plan, planes, block), out_s...]
  transfers between devices with their start and end apart: 19 -> 19, of which waited for: 9 -> 9; matrix products, arithmetic and copies ran while one was open for 0% -> 0% of each run, Pallas kernels for 19% -> 24%
where the time goes in v6:
time: 59 us; the launch traced here: 58.9 us
  starting transfers between devices  21.4 us (36%)
  Pallas kernels  20.9 us (35%)
  waiting for transfers between devices  16.2 us (27%)
    ppermute x19, starting transfers between devices, swap(): lax.ppermute(x, axis, [(i, i ^ m) for i in range(lax.axis_size(axis))])  21.4 us
    ppermute x19, waiting for transfers between devices, swap(): lax.ppermute(x, axis, [(i, i ^ m) for i in range(lax.axis_size(axis))])  16.2 us
    pallas_call x1, Pallas kernels, send_product(): pl.pallas_call(functools.partial(send_kernel, plan, planes, block), out_s...  3.76 us
    pallas_call x1, Pallas kernels, stage(): pl.pallas_call(functools.partial(stage_kernel, plan, block), out_shape=pl...  3.5 us
    pallas_call x3, Pallas kernels, bucket(): pl.pallas_call(functools.partial(bucket_kernel, plan, count, both), out_s...  3.13 us
    pallas_call x2, Pallas kernels, place_more(): pl.pallas_call(functools.partial(more_kernel, plan, planes), out_shape=la...  3.06 us
    pallas_call x1, Pallas kernels, keep_product(): pl.pallas_call(functools.partial(keep_kernel, plan, block), out_shape=plt...  2.35 us
    pallas_call x1, Pallas kernels, place_early(): pl.pallas_call(functools.partial(early_kernel, plan, planes), out_shape=l...  2.12 us
  transfers between devices with their start and end apart: 19, of which 9 were waited for; matrix products, arithmetic and copies ran while one was open for 0% of the time, Pallas kernels for 24%

profile of v6, /device:TPU:0, one launch (start us, length us, event | category | flops | bytes accessed | tf_op | source)
XLA Modules:
  0.0 58.9 jit_solution(15679445162395440864)
XLA Ops:
  0.0 1.0 %pack_tiles.1.rest_0_ = bf16[1040,128]{1,0:T(8,128)(2,1)S(1)} custom-call(s32[1,64]{1,0:T(1,128)} %ids.1, bf16[1024,128]{1,0:T(8,128)(2,1)} %bitcast.1), custom_call_target="tpu_custom_call" | custom-call | bytes 532480 | tf_op jit(solution)/shard_map/pack_tiles/pallas_call | solution.py:82
  1.0 0.5 collective-permute-start.1
  1.5 3.7 %collective-permute-start = (bf16[1040,128]{1,0:T(8,128)(2,1)S(1)}, bf16[1040,128]{1,0:T(8,128)(2,1)S(1)}, u32[]{:S(2)}, u32[]{:S(2)}) collective-permute-start(bf16[1040,128]{1,0:T(8,128)(2,1)S(1)} %pack_tiles.1.rest_0_), channel_id=1, source_target_pairs={{0,16},{8,24},{16,0},{24,8},{1,17},{9,25},{17,1},{25,9},{2,18},{10... | collective-permute-start | bytes 798728 | tf_op jit(solution)/shard_map/ppermute | solution.py:433
  5.2 0.0 collective-permute-done.1.rest_1_
  5.2 1.2 %bucket_tiles.3 = bf16[2192,128]{1,0:T(8,128)(2,1)S(1)} custom-call(bf16[1040,128]{1,0:T(8,128)(2,1)S(1)} %pack_tiles.1.rest_0_, bf16[1040,128]{1,0:T(8,128)(2,1)S(1)} %collective-permute-done.1.rest_1_), custom_call_target="tpu_custom_call" | custom-call | bytes 2228224 | tf_op jit(solution)/shard_map/bucket_tiles/pallas_call | solution.py:152
  6.4 2.5 %collective-permute-start.4 = (bf16[544,128]{1,0:T(8,128)(2,1)S(1)}, bf16[544,128]{1,0:T(8,128)(2,1)S(1)}, u32[]{:S(2)}, u32[]{:S(2)}) collective-permute-start(bf16[544,128]{1,0:T(8,128)(2,1)S(1)} %get-tuple-element.53), channel_id=1, source_target_pairs={{0,6},{1,7},{2,4},{3,5},{4,2},{5,3},{6,0},{7,1},{8,14},{9,15},{10,... | collective-permute-start | bytes 417800 | tf_op jit(solution)/shard_map/ppermute | solution.py:433
  8.9 0.5 collective-permute-start.3
  9.4 0.5 collective-permute-start.2
  10.0 3.5 %stage_integrals.1.cols = bf16[1024,4096]{1,0:T(8,128)(2,1)S(1)} custom-call(bf16[1024,4096]{1,0:T(8,128)(2,1)} %integrals.1), custom_call_target="tpu_custom_call" | custom-call | bytes 16777216 | tf_op jit(solution)/shard_map/stage_integrals/pallas_call | solution.py:239
  13.5 4.4 %collective-permute-done.rest_0_ = bf16[1040,128]{1,0:T(8,128)(2,1)S(1)} collective-permute-done((bf16[1040,128]{1,0:T(8,128)(2,1)S(1)}, bf16[1040,128]{1,0:T(8,128)(2,1)S(1)}, u32[]{:S(2)}, u32[]{:S(2)}) %collective-permute-start) | collective-permute-done | bytes 266272 | tf_op jit(solution)/shard_map/ppermute | solution.py:433
  17.9 0.0 collective-permute-done.4.rest_3_
  17.9 0.0 collective-permute-done.3.rest_2_
  17.9 0.0 collective-permute-done.2.rest_1_
  17.9 0.1 collective-permute-start.6
  18.0 0.8 %collective-permute-start.5 = (bf16[1040,128]{1,0:T(8,128)(2,1)S(1)}, bf16[1040,128]{1,0:T(8,128)(2,1)S(1)}, u32[]{:S(2)}, u32[]{:S(2)}) collective-permute-start(bf16[1040,128]{1,0:T(8,128)(2,1)S(1)} %collective-permute-done.rest_0_), channel_id=1, source_target_pairs={{0,8},{8,0},{16,24},{24,16},{1,9},{9,1},{17,25},{25,17},{2,10},{10... | collective-permute-start | bytes 798728 | tf_op jit(solution)/shard_map/ppermute | solution.py:433
  18.8 1.3 %collective-permute-start.13 = (bf16[2176,128]{1,0:T(8,128)(2,1)S(1)}, bf16[2176,128]{1,0:T(8,128)(2,1)S(1)}, u32[]{:S(2)}, u32[]{:S(2)}) collective-permute-start(bf16[2176,128]{1,0:T(8,128)(2,1)S(1)} %pad_maximum_fusion), channel_id=1, source_target_pairs={{0,8},{8,0},{16,24},{24,16},{1,9},{9,1},{17,25},{25,17},{2,10},{10... | collective-permute-start | bytes 1671176 | tf_op jit(solution)/shard_map/ppermute | solution.py:433
  20.2 0.0 collective-permute-done.6.rest_1_
  20.2 1.2 %bucket_tiles.4 = bf16[2192,128]{1,0:T(8,128)(2,1)S(1)} custom-call(bf16[1040,128]{1,0:T(8,128)(2,1)S(1)} %collective-permute-done.rest_0_, bf16[1040,128]{1,0:T(8,128)(2,1)S(1)} %collective-permute-done.6.rest_1_), custom_call_target="tpu_custom_call" | custom-call | bytes 2228224 | tf_op jit(solution)/shard_map/bucket_tiles/pallas_call | solution.py:152
  21.4 1.6 %collective-permute-start.7 = (bf16[544,128]{1,0:T(8,128)(2,1)S(1)}, bf16[544,128]{1,0:T(8,128)(2,1)S(1)}, u32[]{:S(2)}, u32[]{:S(2)}) collective-permute-start(bf16[544,128]{1,0:T(8,128)(2,1)S(1)} %get-tuple-element.48), channel_id=1, source_target_pairs={{0,2},{1,3},{2,0},{3,1},{4,6},{5,7},{6,4},{7,5},{8,10},{9,11},{10,... | collective-permute-start | bytes 417800 | tf_op jit(solution)/shard_map/ppermute | solution.py:433
  23.0 1.5 %collective-permute-start.12 = (bf16[544,128]{1,0:T(8,128)(2,1)S(1)}, bf16[544,128]{1,0:T(8,128)(2,1)S(1)}, u32[]{:S(2)}, u32[]{:S(2)}) collective-permute-start(bf16[544,128]{1,0:T(8,128)(2,1)S(1)} %get-tuple-element.45), channel_id=1, source_target_pairs={{0,6},{1,7},{2,4},{3,5},{4,2},{5,3},{6,0},{7,1},{8,14},{9,15},{10,... | collective-permute-start | bytes 417800 | tf_op jit(solution)/shard_map/ppermute | solution.py:433
  24.5 0.4 collective-permute-start.11
  24.9 2.3 %collective-permute-done.5.rest_0_ = bf16[1040,128]{1,0:T(8,128)(2,1)S(1)} collective-permute-done((bf16[1040,128]{1,0:T(8,128)(2,1)S(1)}, bf16[1040,128]{1,0:T(8,128)(2,1)S(1)}, u32[]{:S(2)}, u32[]{:S(2)}) %collective-permute-start.5) | collective-permute-done | bytes 266272 | tf_op jit(solution)/shard_map/ppermute | solution.py:433
  27.2 0.4 collective-permute-done.7.rest_1_
  27.6 0.8 %bucket_tiles.5 = bf16[2192,128]{1,0:T(8,128)(2,1)S(1)} custom-call(bf16[1040,128]{1,0:T(8,128)(2,1)S(1)} %collective-permute-done.5.rest_0_), custom_call_target="tpu_custom_call" | custom-call | bytes 2228224 | tf_op jit(solution)/shard_map/bucket_tiles/pallas_call | solution.py:152
  28.5 2.9 %collective-permute-start.10 = (bf16[544,128]{1,0:T(8,128)(2,1)S(1)}, bf16[544,128]{1,0:T(8,128)(2,1)S(1)}, u32[]{:S(2)}, u32[]{:S(2)}) collective-permute-start(bf16[544,128]{1,0:T(8,128)(2,1)S(1)} %get-tuple-element.49), channel_id=1, source_target_pairs={{0,6},{1,7},{2,4},{3,5},{4,2},{5,3},{6,0},{7,1},{8,14},{9,15},{10,... | collective-permute-start | bytes 417800 | tf_op jit(solution)/shard_map/ppermute | solution.py:433
  31.5 0.5 collective-permute-start.9
  32.0 0.0 collective-permute-done.12.rest_3_
  32.0 0.5 collective-permute-start.8
  32.5 2.1 %place_early.1._ = bf16[528,4096]{1,0:T(8,128)(2,1)S(1)} custom-call(bf16[544,128]{1,0:T(8,128)(2,1)S(1)} %get-tuple-element.27.rest_0_, bf16[544,128]{1,0:T(8,128)(2,1)S(1)} %collective-permute-done.2.rest_1_, bf16[544,128]{1,0:T(8,128)(2,1)S(1)} %collective-permute-done.3.rest_2_, bf16[544,128]{1,0:T(8,128)(2,1)S(1)} %collective-permute-done.4.rest_3_), custom_call_target="tpu_custom_call" | custom-call | bytes 4194304 | tf_op jit(solution)/shard_map/place_early/pallas_call | solution.py:260
  34.6 1.8 %collective-permute-done.11.rest_2_ = bf16[544,128]{1,0:T(8,128)(2,1)S(1)} collective-permute-done((bf16[544,128]{1,0:T(8,128)(2,1)S(1)}, bf16[544,128]{1,0:T(8,128)(2,1)S(1)}, u32[]{:S(2)}, u32[]{:S(2)}) %collective-permute-start.11) | collective-permute-done | bytes 139296 | tf_op jit(solution)/shard_map/ppermute | solution.py:433
  36.5 1.8 %place_more.2._ = bf16[528,4096]{1,0:T(8,128)(2,1)S(1)} custom-call(bf16[528,4096]{1,0:T(8,128)(2,1)S(1)} %place_early.1._, bf16[544,128]{1,0:T(8,128)(2,1)S(1)} %get-tuple-element.47.rest_0_, bf16[544,128]{1,0:T(8,128)(2,1)S(1)} %collective-permute-done.7.rest_1_, ...), custom_call_target="tpu_custom_call", output_to_operand_aliasing={{}: (0, {})} | custom-call | bytes 4194304 | tf_op jit(solution)/shard_map/place_more/pallas_call | solution.py:280
  38.3 0.0 collective-permute-done.10.rest_3_
  38.3 0.0 collective-permute-done.9.rest_2_
  38.4 0.0 collective-permute-done.8.rest_1_
  38.4 0.4 collective-permute-done.13.rest_0_
  38.8 0.1 collective-permute-start.14
  38.9 1.2 %place_more.3._ = bf16[528,4096]{1,0:T(8,128)(2,1)S(1)} custom-call(bf16[528,4096]{1,0:T(8,128)(2,1)S(1)} %place_more.2._, bf16[2176,128]{1,0:T(8,128)(2,1)S(1)} %collective-permute-done.13.rest_0_), custom_call_target="tpu_custom_call", output_to_operand_aliasing={{}: (0, {})} | custom-call | bytes 4194304 | tf_op jit(solution)/shard_map/place_more/pallas_call | solution.py:280
  40.1 0.3 collective-permute-done.14.rest_4_
  40.4 3.8 %place_and_multiply.1 = (bf16[528,4096]{1,0:T(8,128)(2,1)S(1)}, f32[256,1024]{1,0:T(8,128)S(1)}) custom-call(bf16[528,4096]{1,0:T(8,128)(2,1)S(1)} %place_more.3._, bf16[1024,4096]{1,0:T(8,128)(2,1)S(1)} %stage_integrals.1.cols, bf16[544,128]{1,0:T(8,128)(2,1)S(1)} %get-tuple-element.35.rest_0_, ...), custom_call_target="tpu_custom_call", output_to_operand_aliasing={{0}: (0, {})} | custom-call | flops 4294967296 | bytes 16777216 | tf_op jit(solution)/shard_map/place_and_multiply/pallas_call | solution.py:303
  44.2 0.3 collective-permute-start.15
  44.5 2.4 %multiply_kept.1.keep = f32[256,1024]{1,0:T(8,128)S(1)} custom-call(bf16[528,4096]{1,0:T(8,128)(2,1)S(1)} %get-tuple-element.39.lam, bf16[1024,4096]{1,0:T(8,128)(2,1)S(1)} %stage_integrals.1.cols), custom_call_target="tpu_custom_call" | custom-call | flops 2147483648 | bytes 10485760 | tf_op jit(solution)/shard_map/multiply_kept/pallas_call | solution.py:332
  46.8 0.1 collective-permute-done.15.got
  46.9 0.9 %code_sums.1 = (f32[64,1024]{1,0:T(8,128)S(1)}, s32[264,128]{1,0:T(8,128)S(1)}, s32[264,128]{1,0:T(8,128)S(1)}, s32[264,128]{1,0:T(8,128)S(1)}) custom-call(f32[256,1024]{1,0:T(8,128)S(1)} %multiply_kept.1.keep, f32[256,1024]{1,0:T(8,128)S(1)} %collective-permute-done.15.got), custom_call_target="tpu_custom_call" | custom-call | bytes 4194304 | tf_op jit(solution)/shard_map/code_sums/pallas_call | solution.py:379
  47.9 1.6 %collective-permute-start.16 = (s32[264,128]{1,0:T(8,128)S(1)}, s32[264,128]{1,0:T(8,128)S(1)}, u32[]{:S(2)}, u32[]{:S(2)}) collective-permute-start(s32[264,128]{1,0:T(8,128)S(1)} %get-tuple-element.42), channel_id=1, source_target_pairs={{0,2},{1,3},{2,0},{3,1},{4,6},{5,7},{6,4},{7,5},{8,10},{9,11},{10,... | collective-permute-start | bytes 405512 | tf_op jit(solution)/shard_map/ppermute | solution.py:433
  49.5 1.5 %collective-permute-start.17 = (s32[264,128]{1,0:T(8,128)S(1)}, s32[264,128]{1,0:T(8,128)S(1)}, u32[]{:S(2)}, u32[]{:S(2)}) collective-permute-start(s32[264,128]{1,0:T(8,128)S(1)} %get-tuple-element.43), channel_id=1, source_target_pairs={{0,4},{1,5},{2,6},{3,7},{4,0},{5,1},{6,2},{7,3},{8,12},{9,13},{10,... | collective-permute-start | bytes 405512 | tf_op jit(solution)/shard_map/ppermute | solution.py:433
  51.0 0.4 collective-permute-start.18
  51.4 2.6 %collective-permute-done.16.rest_0_ = s32[264,128]{1,0:T(8,128)S(1)} collective-permute-done((s32[264,128]{1,0:T(8,128)S(1)}, s32[264,128]{1,0:T(8,128)S(1)}, u32[]{:S(2)}, u32[]{:S(2)}) %collective-permute-start.16) | collective-permute-done | bytes 135200 | tf_op jit(solution)/shard_map/ppermute | solution.py:433
  54.0 3.8 %collective-permute-done.17.rest_1_ = s32[264,128]{1,0:T(8,128)S(1)} collective-permute-done((s32[264,128]{1,0:T(8,128)S(1)}, s32[264,128]{1,0:T(8,128)S(1)}, u32[]{:S(2)}, u32[]{:S(2)}) %collective-permute-start.17) | collective-permute-done | bytes 135200 | tf_op jit(solution)/shard_map/ppermute | solution.py:433
  57.8 0.0 collective-permute-done.18.rest_2_
  57.8 1.1 %total_sums.1 = f32[64,1024]{1,0:T(8,128)} custom-call(f32[64,1024]{1,0:T(8,128)S(1)} %get-tuple-element.41.mine, s32[264,128]{1,0:T(8,128)S(1)} %collective-permute-done.16.rest_0_, s32[264,128]{1,0:T(8,128)S(1)} %collective-permute-done.17.rest_1_, s32[264,128]{1,0:T(8,128)S(1)} %collective-permute-done.18.rest_2_), custom_call_target="tpu_custom_call" | custom-call | bytes 4194304 | tf_op jit(solution)/shard_map/total_sums/pallas_call | solution.py:416
  (9 shorter events, 0.2 us)
Async XLA Ops:
  1.0 4.2 %collective-permute-start.1 = (bf16[1040,128]{1,0:T(8,128)(2,1)S(1)}, bf16[1040,128]{1,0:T(8,128)(2,1)S(1)}, u32[]{:S(2)}, u32[]{:S(2)}) collective-permute-start(bf16[1040,128]{1,0:T(8,128)(2,1)S(1)} %pack_tiles.1.rest_0_), channel_id=1, source_target_pairs={{0,1},{1,0},{2,3},{3,2},{4,5},{5,4},{6,7},{7,6},{8,9},{9,8},{10,11... | collective-permute-start | bytes 798728 | tf_op jit(solution)/shard_map/ppermute | solution.py:433
  1.5 16.4 %collective-permute-start = (bf16[1040,128]{1,0:T(8,128)(2,1)S(1)}, bf16[1040,128]{1,0:T(8,128)(2,1)S(1)}, u32[]{:S(2)}, u32[]{:S(2)}) collective-permute-start(bf16[1040,128]{1,0:T(8,128)(2,1)S(1)} %pack_tiles.1.rest_0_), channel_id=1, source_target_pairs={{0,16},{8,24},{16,0},{24,8},{1,17},{9,25},{17,1},{25,9},{2,18},{10... | collective-permute-start | bytes 798728 | tf_op jit(solution)/shard_map/ppermute | solution.py:433
  6.4 11.5 %collective-permute-start.4 = (bf16[544,128]{1,0:T(8,128)(2,1)S(1)}, bf16[544,128]{1,0:T(8,128)(2,1)S(1)}, u32[]{:S(2)}, u32[]{:S(2)}) collective-permute-start(bf16[544,128]{1,0:T(8,128)(2,1)S(1)} %get-tuple-element.53), channel_id=1, source_target_pairs={{0,6},{1,7},{2,4},{3,5},{4,2},{5,3},{6,0},{7,1},{8,14},{9,15},{10,... | collective-permute-start | bytes 417800 | tf_op jit(solution)/shard_map/ppermute | solution.py:433
  8.9 9.0 %collective-permute-start.3 = (bf16[544,128]{1,0:T(8,128)(2,1)S(1)}, bf16[544,128]{1,0:T(8,128)(2,1)S(1)}, u32[]{:S(2)}, u32[]{:S(2)}) collective-permute-start(bf16[544,128]{1,0:T(8,128)(2,1)S(1)} %get-tuple-element.54), channel_id=1, source_target_pairs={{0,4},{1,5},{2,6},{3,7},{4,0},{5,1},{6,2},{7,3},{8,12},{9,13},{10,... | collective-permute-start | bytes 417800 | tf_op jit(solution)/shard_map/ppermute | solution.py:433
  9.4 8.5 %collective-permute-start.2 = (bf16[544,128]{1,0:T(8,128)(2,1)S(1)}, bf16[544,128]{1,0:T(8,128)(2,1)S(1)}, u32[]{:S(2)}, u32[]{:S(2)}) collective-permute-start(bf16[544,128]{1,0:T(8,128)(2,1)S(1)} %get-tuple-element.55), channel_id=1, source_target_pairs={{0,2},{1,3},{2,0},{3,1},{4,6},{5,7},{6,4},{7,5},{8,10},{9,11},{10,... | collective-permute-start | bytes 417800 | tf_op jit(solution)/shard_map/ppermute | solution.py:433
  17.9 2.3 %collective-permute-start.6 = (bf16[1040,128]{1,0:T(8,128)(2,1)S(1)}, bf16[1040,128]{1,0:T(8,128)(2,1)S(1)}, u32[]{:S(2)}, u32[]{:S(2)}) collective-permute-start(bf16[1040,128]{1,0:T(8,128)(2,1)S(1)} %collective-permute-done.rest_0_), channel_id=1, source_target_pairs={{0,1},{1,0},{2,3},{3,2},{4,5},{5,4},{6,7},{7,6},{8,9},{9,8},{10,11... | collective-permute-start | bytes 798728 | tf_op jit(solution)/shard_map/ppermute | solution.py:433
  18.0 9.3 %collective-permute-start.5 = (bf16[1040,128]{1,0:T(8,128)(2,1)S(1)}, bf16[1040,128]{1,0:T(8,128)(2,1)S(1)}, u32[]{:S(2)}, u32[]{:S(2)}) collective-permute-start(bf16[1040,128]{1,0:T(8,128)(2,1)S(1)} %collective-permute-done.rest_0_), channel_id=1, source_target_pairs={{0,8},{8,0},{16,24},{24,16},{1,9},{9,1},{17,25},{25,17},{2,10},{10... | collective-permute-start | bytes 798728 | tf_op jit(solution)/shard_map/ppermute | solution.py:433
  18.8 19.9 %collective-permute-start.13 = (bf16[2176,128]{1,0:T(8,128)(2,1)S(1)}, bf16[2176,128]{1,0:T(8,128)(2,1)S(1)}, u32[]{:S(2)}, u32[]{:S(2)}) collective-permute-start(bf16[2176,128]{1,0:T(8,128)(2,1)S(1)} %pad_maximum_fusion), channel_id=1, source_target_pairs={{0,8},{8,0},{16,24},{24,16},{1,9},{9,1},{17,25},{25,17},{2,10},{10... | collective-permute-start | bytes 1671176 | tf_op jit(solution)/shard_map/ppermute | solution.py:433
  21.4 6.3 %collective-permute-start.7 = (bf16[544,128]{1,0:T(8,128)(2,1)S(1)}, bf16[544,128]{1,0:T(8,128)(2,1)S(1)}, u32[]{:S(2)}, u32[]{:S(2)}) collective-permute-start(bf16[544,128]{1,0:T(8,128)(2,1)S(1)} %get-tuple-element.48), channel_id=1, source_target_pairs={{0,2},{1,3},{2,0},{3,1},{4,6},{5,7},{6,4},{7,5},{8,10},{9,11},{10,... | collective-permute-start | bytes 417800 | tf_op jit(solution)/shard_map/ppermute | solution.py:433
  23.0 9.0 %collective-permute-start.12 = (bf16[544,128]{1,0:T(8,128)(2,1)S(1)}, bf16[544,128]{1,0:T(8,128)(2,1)S(1)}, u32[]{:S(2)}, u32[]{:S(2)}) collective-permute-start(bf16[544,128]{1,0:T(8,128)(2,1)S(1)} %get-tuple-element.45), channel_id=1, source_target_pairs={{0,6},{1,7},{2,4},{3,5},{4,2},{5,3},{6,0},{7,1},{8,14},{9,15},{10,... | collective-permute-start | bytes 417800 | tf_op jit(solution)/shard_map/ppermute | solution.py:433
  24.5 12.0 %collective-permute-start.11 = (bf16[544,128]{1,0:T(8,128)(2,1)S(1)}, bf16[544,128]{1,0:T(8,128)(2,1)S(1)}, u32[]{:S(2)}, u32[]{:S(2)}) collective-permute-start(bf16[544,128]{1,0:T(8,128)(2,1)S(1)} %get-tuple-element.46), channel_id=1, source_target_pairs={{0,4},{1,5},{2,6},{3,7},{4,0},{5,1},{6,2},{7,3},{8,12},{9,13},{10,... | collective-permute-start | bytes 417800 | tf_op jit(solution)/shard_map/ppermute | solution.py:433
  28.5 9.8 %collective-permute-start.10 = (bf16[544,128]{1,0:T(8,128)(2,1)S(1)}, bf16[544,128]{1,0:T(8,128)(2,1)S(1)}, u32[]{:S(2)}, u32[]{:S(2)}) collective-permute-start(bf16[544,128]{1,0:T(8,128)(2,1)S(1)} %get-tuple-element.49), channel_id=1, source_target_pairs={{0,6},{1,7},{2,4},{3,5},{4,2},{5,3},{6,0},{7,1},{8,14},{9,15},{10,... | collective-permute-start | bytes 417800 | tf_op jit(solution)/shard_map/ppermute | solution.py:433
  31.5 6.9 %collective-permute-start.9 = (bf16[544,128]{1,0:T(8,128)(2,1)S(1)}, bf16[544,128]{1,0:T(8,128)(2,1)S(1)}, u32[]{:S(2)}, u32[]{:S(2)}) collective-permute-start(bf16[544,128]{1,0:T(8,128)(2,1)S(1)} %get-tuple-element.50), channel_id=1, source_target_pairs={{0,4},{1,5},{2,6},{3,7},{4,0},{5,1},{6,2},{7,3},{8,12},{9,13},{10,... | collective-permute-start | bytes 417800 | tf_op jit(solution)/shard_map/ppermute | solution.py:433
  32.0 6.4 %collective-permute-start.8 = (bf16[544,128]{1,0:T(8,128)(2,1)S(1)}, bf16[544,128]{1,0:T(8,128)(2,1)S(1)}, u32[]{:S(2)}, u32[]{:S(2)}) collective-permute-start(bf16[544,128]{1,0:T(8,128)(2,1)S(1)} %get-tuple-element.51), channel_id=1, source_target_pairs={{0,2},{1,3},{2,0},{3,1},{4,6},{5,7},{6,4},{7,5},{8,10},{9,11},{10,... | collective-permute-start | bytes 417800 | tf_op jit(solution)/shard_map/ppermute | solution.py:433
  38.8 1.6 %collective-permute-start.14 = (bf16[1088,128]{1,0:T(8,128)(2,1)S(1)}, bf16[1088,128]{1,0:T(8,128)(2,1)S(1)}, u32[]{:S(2)}, u32[]{:S(2)}) collective-permute-start(bf16[1088,128]{1,0:T(8,128)(2,1)S(1)} %pad_maximum_fusion.1), channel_id=1, source_target_pairs={{0,1},{1,0},{2,3},{3,2},{4,5},{5,4},{6,7},{7,6},{8,9},{9,8},{10,11... | collective-permute-start | bytes 835592 | tf_op jit(solution)/shard_map/ppermute | solution.py:433
  44.2 2.7 %collective-permute-start.15 = (f32[256,1024]{1,0:T(8,128)S(1)}, f32[256,1024]{1,0:T(8,128)S(1)}, u32[]{:S(2)}, u32[]{:S(2)}) collective-permute-start(f32[256,1024]{1,0:T(8,128)S(1)} %get-tuple-element.40), channel_id=1, source_target_pairs={{0,1},{1,0},{2,3},{3,2},{4,5},{5,4},{6,7},{7,6},{8,9},{9,8},{10,11... | collective-permute-start | bytes 3145736 | tf_op jit(solution)/shard_map/ppermute | solution.py:433
  47.9 6.2 %collective-permute-start.16 = (s32[264,128]{1,0:T(8,128)S(1)}, s32[264,128]{1,0:T(8,128)S(1)}, u32[]{:S(2)}, u32[]{:S(2)}) collective-permute-start(s32[264,128]{1,0:T(8,128)S(1)} %get-tuple-element.42), channel_id=1, source_target_pairs={{0,2},{1,3},{2,0},{3,1},{4,6},{5,7},{6,4},{7,5},{8,10},{9,11},{10,... | collective-permute-start | bytes 405512 | tf_op jit(solution)/shard_map/ppermute | solution.py:433
  49.5 8.3 %collective-permute-start.17 = (s32[264,128]{1,0:T(8,128)S(1)}, s32[264,128]{1,0:T(8,128)S(1)}, u32[]{:S(2)}, u32[]{:S(2)}) collective-permute-start(s32[264,128]{1,0:T(8,128)S(1)} %get-tuple-element.43), channel_id=1, source_target_pairs={{0,4},{1,5},{2,6},{3,7},{4,0},{5,1},{6,2},{7,3},{8,12},{9,13},{10,... | collective-permute-start | bytes 405512 | tf_op jit(solution)/shard_map/ppermute | solution.py:433
  51.0 6.8 %collective-permute-start.18 = (s32[264,128]{1,0:T(8,128)S(1)}, s32[264,128]{1,0:T(8,128)S(1)}, u32[]{:S(2)}, u32[]{:S(2)}) collective-permute-start(s32[264,128]{1,0:T(8,128)S(1)} %get-tuple-element.44), channel_id=1, source_target_pairs={{0,6},{1,7},{2,4},{3,5},{4,2},{5,3},{6,0},{7,1},{8,14},{9,15},{10,... | collective-permute-start | bytes 405512 | tf_op jit(solution)/shard_map/ppermute | solution.py:433

commit v7 on v6

--- a/solution.py
+++ b/solution.py
@@ -37,8 +37,8 @@
         self.packed = self.body + self.head
 
 
-def pack_kernel(plan, ids, tiles, packed, ids_row, buf, sem):
-    load = pltpu.make_async_copy(tiles, buf.at[pl.ds(0, plan.body)], sem.at[0])
+def pack_kernel(plan, ids, tiles, packed, ids_row, sem):
+    load = pltpu.make_async_copy(tiles, packed.at[pl.ds(0, plan.body)], sem.at[0])
     load_ids = pltpu.make_async_copy(ids, ids_row, sem.at[1])
     load_ids.start()
     load.start()
@@ -70,23 +70,19 @@
     slots = spread(slot, tile_at == lane)
     top = lax.broadcasted_iota(jnp.int32, (plan.head, plan.tile), 0)
     head = jnp.where(top == plan.n_col, slots, places)
-    buf[plan.body :, :] = head.astype(jnp.bfloat16)
+    packed[plan.body :, :] = head.astype(jnp.bfloat16)
     load.wait()
-    store = pltpu.make_async_copy(buf, packed, sem.at[0])
-    store.start()
-    store.wait()
 
 
 def pack(plan, ids, tiles):
     ids, tiles = (pltpu.with_memory_space_constraint(x, pltpu.HBM) for x in (ids, tiles))
     return pl.pallas_call(
         functools.partial(pack_kernel, plan),
-        out_shape=jax.ShapeDtypeStruct((plan.packed, plan.tile), jnp.bfloat16),
+        out_shape=pltpu.VMEM((plan.packed, plan.tile), jnp.bfloat16),
         in_specs=[HBM, HBM],
-        out_specs=HBM,
+        out_specs=VMEM,
         scratch_shapes=[
             pltpu.VMEM(ids.shape, jnp.int32),
-            pltpu.VMEM((plan.packed, plan.tile), jnp.bfloat16),
             pltpu.SemaphoreType.DMA((2,)),
         ],
         compiler_params=pltpu.CompilerParams(vmem_limit_bytes=8 * 1024 * 1024),
@@ -348,14 +344,16 @@
     return (chunks_of(plan) // 2 * plan.owned + chunks_of(plan), plan.tile)
 
 
-def code_kernel(plan, keep, got, mine, *rest):
-    words, square = rest[:-1], rest[-1]
+def code_kernel(plan, parts, keep, got, *rest):
+    *words, square = rest
     rows, tile, chunks = plan.owned, plan.tile, chunks_of(plan)
     lane = lax.broadcasted_iota(jnp.int32, (rows, tile), 1)
-    mine[...] = keep[:rows, :] + got[:rows, :]
     square[...] = jnp.zeros(square.shape, jnp.float32)
-    for m, out in enumerate(words, 1):
+    for m, out in zip(parts, words, strict=True):
         here = slice(m * rows, (m + 1) * rows)
+        if not m:
+            out[...] = keep[here, :] + got[here, :]
+            continue
         cells = [slice(j * tile, (j + 1) * tile) for j in range(chunks)]
         sums = [keep[here, cell] + got[here, cell] for cell in cells]
         most = jnp.zeros((rows, tile), jnp.float32)
@@ -374,13 +372,14 @@
         out[chunks // 2 * rows :, :] = square[...].T[:chunks, :].astype(jnp.int32)
 
 
-def code_sums(plan, keep, got):
+def code_sums(plan, parts, keep, got):
     block = pltpu.VMEM((plan.owned, plan.ab), jnp.float32)
-    return pl.pallas_call(
-        functools.partial(code_kernel, plan),
-        out_shape=[block] + [pltpu.VMEM(words_shape(plan), jnp.int32)] * (plan.n_pair - 1),
+    coded = pltpu.VMEM(words_shape(plan), jnp.int32)
+    return pl.pallas_call(
+        functools.partial(code_kernel, plan, parts),
+        out_shape=[coded if m else block for m in parts],
         in_specs=[VMEM] * 2,
-        out_specs=[VMEM] * plan.n_pair,
+        out_specs=[VMEM] * len(parts),
         scratch_shapes=[pltpu.VMEM((plan.tile, plan.tile), jnp.float32)],
         compiler_params=pltpu.CompilerParams(vmem_limit_bytes=20 * 1024 * 1024),
         cost_estimate=cost(plan, 4 * plan.n_pair * plan.owned * plan.ab * 4),
@@ -460,13 +459,17 @@
     lam = place_more(plan, lam, [((chip,), tuple(middle)) for chip in chips], early)
     late, lam, near = lax.optimization_barrier((late, lam, near))
     cross = swap(jnp.concatenate([part[plan.bucket :] for part in late], axis=0), "col", 1)
-    lam = place_more(plan, lam, [(chips, (1,))], [near])
-    planes = [((chip,), (last,), 0) for chip in chips] + [(chips, (last,), 1)]
-    lam, send = send_product(plan, lam, planes, late + [cross], staged)
+    planes = [(chips, (1,))] + [((chip,), (last,), 0) for chip in chips]
+    lam = place_more(plan, lam, planes, [near] + late)
+    lam, send = send_product(plan, lam, [(chips, (last,), 1)], [cross], staged)
     got = swap(send, "col", 1)
     keep = keep_product(plan, lam, staged)
-    mine, *words = code_sums(plan, keep, got)
-    return total_sums(plan, mine, [swap(word, "col", 2 * m) for m, word in enumerate(words, 1)])
+    *near_parts, far_part = range(1, plan.n_pair)
+    (word,) = code_sums(plan, [far_part], keep, got)
+    words = [swap(word, "col", 2 * far_part)]
+    mine, *coded = code_sums(plan, [0] + near_parts, keep, got)
+    words += [swap(word, "col", 2 * m) for m, word in zip(near_parts, coded, strict=True)]
+    return total_sums(plan, mine, words)
 
 
 def solution(mesh):

time: 59 us -> 58.3 us (0.988)
  waiting for transfers between devices: 16.2 us -> 14.1 us
  starting transfers between devices: 21.4 us -> 22.4 us
    ppermute x19, waiting for transfers between devices: 16.2 us -> 14.1 us  [swap(): lax.ppermute(x, axis, [(i, i ^ m) for i in range(lax.axis_size(axis))])]
    ppermute x19, starting transfers between devices: 21.4 us -> 22.4 us  [swap(): lax.ppermute(x, axis, [(i, i ^ m) for i in range(lax.axis_size(axis))])]
    pallas_call x2, Pallas kernels: 3.06 us -> 3.85 us  [place_more(): pl.pallas_call(functools.partial(more_kernel, plan, planes), out_shape=la...]
    pallas_call x2 -> x3, Pallas kernels: 1.93 us -> 1.96 us  [the longest x1 0.98 us: pack(): pl.pallas_call(functools.partial(pack_kernel, plan), out_shape=pltpu.VMEM...]
  transfers between devices with their start and end apart: 19 -> 19, of which waited for: 9 -> 7; matrix products, arithmetic and copies ran while one was open for 0% -> 0% of each run, Pallas kernels for 24% -> 27%
where the time goes in v7:
time: 58.3 us; the launch traced here: 58.1 us
  starting transfers between devices  22.4 us (38%)
  Pallas kernels  21.2 us (36%)
  waiting for transfers between devices  14.1 us (24%)
    ppermute x19, starting transfers between devices, swap(): lax.ppermute(x, axis, [(i, i ^ m) for i in range(lax.axis_size(axis))])  22.4 us
    ppermute x19, waiting for transfers between devices, swap(): lax.ppermute(x, axis, [(i, i ^ m) for i in range(lax.axis_size(axis))])  14.1 us
    pallas_call x2, Pallas kernels, place_more(): pl.pallas_call(functools.partial(more_kernel, plan, planes), out_shape=la...  3.85 us
    pallas_call x1, Pallas kernels, stage(): pl.pallas_call(functools.partial(stage_kernel, plan, block), out_shape=pl...  3.5 us
    pallas_call x1, Pallas kernels, send_product(): pl.pallas_call(functools.partial(send_kernel, plan, planes, block), out_s...  3.18 us
    pallas_call x3, Pallas kernels, bucket(): pl.pallas_call(functools.partial(bucket_kernel, plan, count, both), out_s...  3.13 us
    pallas_call x1, Pallas kernels, keep_product(): pl.pallas_call(functools.partial(keep_kernel, plan, block), out_shape=plt...  2.35 us
    pallas_call x1, Pallas kernels, place_early(): pl.pallas_call(functools.partial(early_kernel, plan, planes), out_shape=l...  2.14 us
  transfers between devices with their start and end apart: 19, of which 7 were waited for; matrix products, arithmetic and copies ran while one was open for 0% of the time, Pallas kernels for 27%

profile of v7, /device:TPU:0, one launch (start us, length us, event | category | flops | bytes accessed | tf_op | source)
XLA Modules:
  0.0 58.1 jit_solution(5418578628464986353)
XLA Ops:
  0.0 1.0 %pack_tiles.1.rest_0_ = bf16[1040,128]{1,0:T(8,128)(2,1)S(1)} custom-call(s32[1,64]{1,0:T(1,128)} %ids.1, bf16[1024,128]{1,0:T(8,128)(2,1)} %bitcast.1), custom_call_target="tpu_custom_call" | custom-call | bytes 532480 | tf_op jit(solution)/shard_map/pack_tiles/pallas_call | solution.py:79
  1.0 0.5 collective-permute-start.1
  1.5 3.7 %collective-permute-start = (bf16[1040,128]{1,0:T(8,128)(2,1)S(1)}, bf16[1040,128]{1,0:T(8,128)(2,1)S(1)}, u32[]{:S(2)}, u32[]{:S(2)}) collective-permute-start(bf16[1040,128]{1,0:T(8,128)(2,1)S(1)} %pack_tiles.1.rest_0_), channel_id=1, source_target_pairs={{0,16},{8,24},{16,0},{24,8},{1,17},{9,25},{17,1},{25,9},{2,18},{10... | collective-permute-start | bytes 798728 | tf_op jit(solution)/shard_map/ppermute | solution.py:432
  5.2 0.0 collective-permute-done.1.rest_1_
  5.2 1.2 %bucket_tiles.3 = bf16[2192,128]{1,0:T(8,128)(2,1)S(1)} custom-call(bf16[1040,128]{1,0:T(8,128)(2,1)S(1)} %pack_tiles.1.rest_0_, bf16[1040,128]{1,0:T(8,128)(2,1)S(1)} %collective-permute-done.1.rest_1_), custom_call_target="tpu_custom_call" | custom-call | bytes 2228224 | tf_op jit(solution)/shard_map/bucket_tiles/pallas_call | solution.py:148
  6.4 1.6 %collective-permute-start.2 = (bf16[544,128]{1,0:T(8,128)(2,1)S(1)}, bf16[544,128]{1,0:T(8,128)(2,1)S(1)}, u32[]{:S(2)}, u32[]{:S(2)}) collective-permute-start(bf16[544,128]{1,0:T(8,128)(2,1)S(1)} %get-tuple-element.53), channel_id=1, source_target_pairs={{0,2},{1,3},{2,0},{3,1},{4,6},{5,7},{6,4},{7,5},{8,10},{9,11},{10,... | collective-permute-start | bytes 417800 | tf_op jit(solution)/shard_map/ppermute | solution.py:432
  7.9 1.5 %collective-permute-start.3 = (bf16[544,128]{1,0:T(8,128)(2,1)S(1)}, bf16[544,128]{1,0:T(8,128)(2,1)S(1)}, u32[]{:S(2)}, u32[]{:S(2)}) collective-permute-start(bf16[544,128]{1,0:T(8,128)(2,1)S(1)} %get-tuple-element.52), channel_id=1, source_target_pairs={{0,4},{1,5},{2,6},{3,7},{4,0},{5,1},{6,2},{7,3},{8,12},{9,13},{10,... | collective-permute-start | bytes 417800 | tf_op jit(solution)/shard_map/ppermute | solution.py:432
  9.5 0.5 collective-permute-start.4
  9.9 3.5 %stage_integrals.1.cols = bf16[1024,4096]{1,0:T(8,128)(2,1)S(1)} custom-call(bf16[1024,4096]{1,0:T(8,128)(2,1)} %integrals.1), custom_call_target="tpu_custom_call" | custom-call | bytes 16777216 | tf_op jit(solution)/shard_map/stage_integrals/pallas_call | solution.py:235
  13.4 4.4 %collective-permute-done.rest_0_ = bf16[1040,128]{1,0:T(8,128)(2,1)S(1)} collective-permute-done((bf16[1040,128]{1,0:T(8,128)(2,1)S(1)}, bf16[1040,128]{1,0:T(8,128)(2,1)S(1)}, u32[]{:S(2)}, u32[]{:S(2)}) %collective-permute-start) | collective-permute-done | bytes 266272 | tf_op jit(solution)/shard_map/ppermute | solution.py:432
  17.9 0.0 collective-permute-done.2.rest_1_
  17.9 0.0 collective-permute-done.3.rest_2_
  17.9 0.0 collective-permute-done.4.rest_3_
  17.9 0.1 collective-permute-start.6
  18.0 0.8 %collective-permute-start.5 = (bf16[1040,128]{1,0:T(8,128)(2,1)S(1)}, bf16[1040,128]{1,0:T(8,128)(2,1)S(1)}, u32[]{:S(2)}, u32[]{:S(2)}) collective-permute-start(bf16[1040,128]{1,0:T(8,128)(2,1)S(1)} %collective-permute-done.rest_0_), channel_id=1, source_target_pairs={{0,8},{8,0},{16,24},{24,16},{1,9},{9,1},{17,25},{25,17},{2,10},{10... | collective-permute-start | bytes 798728 | tf_op jit(solution)/shard_map/ppermute | solution.py:432
  18.8 1.3 %collective-permute-start.13 = (bf16[2176,128]{1,0:T(8,128)(2,1)S(1)}, bf16[2176,128]{1,0:T(8,128)(2,1)S(1)}, u32[]{:S(2)}, u32[]{:S(2)}) collective-permute-start(bf16[2176,128]{1,0:T(8,128)(2,1)S(1)} %pad_maximum_fusion), channel_id=1, source_target_pairs={{0,8},{8,0},{16,24},{24,16},{1,9},{9,1},{17,25},{25,17},{2,10},{10... | collective-permute-start | bytes 1671176 | tf_op jit(solution)/shard_map/ppermute | solution.py:432
  20.2 0.0 collective-permute-done.6.rest_1_
  20.2 1.2 %bucket_tiles.4 = bf16[2192,128]{1,0:T(8,128)(2,1)S(1)} custom-call(bf16[1040,128]{1,0:T(8,128)(2,1)S(1)} %collective-permute-done.rest_0_, bf16[1040,128]{1,0:T(8,128)(2,1)S(1)} %collective-permute-done.6.rest_1_), custom_call_target="tpu_custom_call" | custom-call | bytes 2228224 | tf_op jit(solution)/shard_map/bucket_tiles/pallas_call | solution.py:148
  21.4 1.6 %collective-permute-start.7 = (bf16[544,128]{1,0:T(8,128)(2,1)S(1)}, bf16[544,128]{1,0:T(8,128)(2,1)S(1)}, u32[]{:S(2)}, u32[]{:S(2)}) collective-permute-start(bf16[544,128]{1,0:T(8,128)(2,1)S(1)} %get-tuple-element.46), channel_id=1, source_target_pairs={{0,2},{1,3},{2,0},{3,1},{4,6},{5,7},{6,4},{7,5},{8,10},{9,11},{10,... | collective-permute-start | bytes 417800 | tf_op jit(solution)/shard_map/ppermute | solution.py:432
  23.0 1.5 %collective-permute-start.11 = (bf16[544,128]{1,0:T(8,128)(2,1)S(1)}, bf16[544,128]{1,0:T(8,128)(2,1)S(1)}, u32[]{:S(2)}, u32[]{:S(2)}) collective-permute-start(bf16[544,128]{1,0:T(8,128)(2,1)S(1)} %get-tuple-element.44), channel_id=1, source_target_pairs={{0,4},{1,5},{2,6},{3,7},{4,0},{5,1},{6,2},{7,3},{8,12},{9,13},{10,... | collective-permute-start | bytes 417800 | tf_op jit(solution)/shard_map/ppermute | solution.py:432
  24.5 0.4 collective-permute-start.12
  24.9 2.3 %collective-permute-done.5.rest_0_ = bf16[1040,128]{1,0:T(8,128)(2,1)S(1)} collective-permute-done((bf16[1040,128]{1,0:T(8,128)(2,1)S(1)}, bf16[1040,128]{1,0:T(8,128)(2,1)S(1)}, u32[]{:S(2)}, u32[]{:S(2)}) %collective-permute-start.5) | collective-permute-done | bytes 266272 | tf_op jit(solution)/shard_map/ppermute | solution.py:432
  27.2 0.1 collective-permute-done.7.rest_1_
  27.4 0.8 %bucket_tiles.5 = bf16[2192,128]{1,0:T(8,128)(2,1)S(1)} custom-call(bf16[1040,128]{1,0:T(8,128)(2,1)S(1)} %collective-permute-done.5.rest_0_), custom_call_target="tpu_custom_call" | custom-call | bytes 2228224 | tf_op jit(solution)/shard_map/bucket_tiles/pallas_call | solution.py:148
  28.2 3.2 %collective-permute-start.10 = (bf16[544,128]{1,0:T(8,128)(2,1)S(1)}, bf16[544,128]{1,0:T(8,128)(2,1)S(1)}, u32[]{:S(2)}, u32[]{:S(2)}) collective-permute-start(bf16[544,128]{1,0:T(8,128)(2,1)S(1)} %get-tuple-element.47), channel_id=1, source_target_pairs={{0,6},{1,7},{2,4},{3,5},{4,2},{5,3},{6,0},{7,1},{8,14},{9,15},{10,... | collective-permute-start | bytes 417800 | tf_op jit(solution)/shard_map/ppermute | solution.py:432
  31.4 0.0 collective-permute-start.8
  31.4 1.3 %collective-permute-done.11.rest_2_ = bf16[544,128]{1,0:T(8,128)(2,1)S(1)} collective-permute-done((bf16[544,128]{1,0:T(8,128)(2,1)S(1)}, bf16[544,128]{1,0:T(8,128)(2,1)S(1)}, u32[]{:S(2)}, u32[]{:S(2)}) %collective-permute-start.11) | collective-permute-done | bytes 139296 | tf_op jit(solution)/shard_map/ppermute | solution.py:432
  32.7 1.5 %collective-permute-start.9 = (bf16[544,128]{1,0:T(8,128)(2,1)S(1)}, bf16[544,128]{1,0:T(8,128)(2,1)S(1)}, u32[]{:S(2)}, u32[]{:S(2)}) collective-permute-start(bf16[544,128]{1,0:T(8,128)(2,1)S(1)} %get-tuple-element.48), channel_id=1, source_target_pairs={{0,4},{1,5},{2,6},{3,7},{4,0},{5,1},{6,2},{7,3},{8,12},{9,13},{10,... | collective-permute-start | bytes 417800 | tf_op jit(solution)/shard_map/ppermute | solution.py:432
  34.2 2.1 %place_early.1._ = bf16[528,4096]{1,0:T(8,128)(2,1)S(1)} custom-call(bf16[544,128]{1,0:T(8,128)(2,1)S(1)} %get-tuple-element.26.rest_0_, bf16[544,128]{1,0:T(8,128)(2,1)S(1)} %collective-permute-done.2.rest_1_, bf16[544,128]{1,0:T(8,128)(2,1)S(1)} %collective-permute-done.3.rest_2_, bf16[544,128]{1,0:T(8,128)(2,1)S(1)} %collective-permute-done.4.rest_3_), custom_call_target="tpu_custom_call" | custom-call | bytes 4194304 | tf_op jit(solution)/shard_map/place_early/pallas_call | solution.py:256
  36.4 0.0 collective-permute-done.12.rest_3_
  36.4 1.9 %place_more.2._ = bf16[528,4096]{1,0:T(8,128)(2,1)S(1)} custom-call(bf16[528,4096]{1,0:T(8,128)(2,1)S(1)} %place_early.1._, bf16[544,128]{1,0:T(8,128)(2,1)S(1)} %get-tuple-element.45.rest_0_, bf16[544,128]{1,0:T(8,128)(2,1)S(1)} %collective-permute-done.7.rest_1_, ...), custom_call_target="tpu_custom_call", output_to_operand_aliasing={{}: (0, {})} | custom-call | bytes 4194304 | tf_op jit(solution)/shard_map/place_more/pallas_call | solution.py:276
  38.3 0.0 collective-permute-done.10.rest_4_
  38.3 0.0 collective-permute-done.8.rest_2_
  38.3 0.0 collective-permute-done.9.rest_3_
  38.3 0.4 collective-permute-done.13.rest_0_
  38.8 0.1 collective-permute-start.14
  38.9 1.9 %place_more.3._ = bf16[528,4096]{1,0:T(8,128)(2,1)S(1)} custom-call(bf16[528,4096]{1,0:T(8,128)(2,1)S(1)} %place_more.2._, bf16[2176,128]{1,0:T(8,128)(2,1)S(1)} %collective-permute-done.13.rest_0_, bf16[544,128]{1,0:T(8,128)(2,1)S(1)} %get-tuple-element.33.rest_1_, ...), custom_call_target="tpu_custom_call", output_to_operand_aliasing={{}: (0, {})} | custom-call | bytes 4194304 | tf_op jit(solution)/shard_map/place_more/pallas_call | solution.py:276
  40.8 0.0 collective-permute-done.14.rest_0_
  40.8 3.2 %place_and_multiply.1 = (bf16[528,4096]{1,0:T(8,128)(2,1)S(1)}, f32[256,1024]{1,0:T(8,128)S(1)}) custom-call(bf16[528,4096]{1,0:T(8,128)(2,1)S(1)} %place_more.3._, bf16[1024,4096]{1,0:T(8,128)(2,1)S(1)} %stage_integrals.1.cols, bf16[1088,128]{1,0:T(8,128)(2,1)S(1)} %collective-permute-done.14.rest_0_), custom_call_target="tpu_custom_call", output_to_operand_aliasing={{0}: (0, {})} | custom-call | flops 4294967296 | bytes 16777216 | tf_op jit(solution)/shard_map/place_and_multiply/pallas_call | solution.py:299
  44.0 0.5 collective-permute-start.15
  44.5 2.4 %multiply_kept.1.keep = f32[256,1024]{1,0:T(8,128)S(1)} custom-call(bf16[528,4096]{1,0:T(8,128)(2,1)S(1)} %get-tuple-element.38.lam, bf16[1024,4096]{1,0:T(8,128)(2,1)S(1)} %stage_integrals.1.cols), custom_call_target="tpu_custom_call" | custom-call | flops 2147483648 | bytes 10485760 | tf_op jit(solution)/shard_map/multiply_kept/pallas_call | solution.py:328
  46.9 0.0 collective-permute-done.15.got
  46.9 0.3 code_sums.3
  47.3 2.6 %collective-permute-start.16 = (s32[264,128]{1,0:T(8,128)S(1)}, s32[264,128]{1,0:T(8,128)S(1)}, u32[]{:S(2)}, u32[]{:S(2)}) collective-permute-start(s32[264,128]{1,0:T(8,128)S(1)} %code_sums.3), channel_id=1, source_target_pairs={{0,6},{1,7},{2,4},{3,5},{4,2},{5,3},{6,0},{7,1},{8,14},{9,15},{10,... | collective-permute-start | bytes 405512 | tf_op jit(solution)/shard_map/ppermute | solution.py:432
  49.8 0.6 %code_sums.2 = (f32[64,1024]{1,0:T(8,128)S(1)}, s32[264,128]{1,0:T(8,128)S(1)}, s32[264,128]{1,0:T(8,128)S(1)}) custom-call(f32[256,1024]{1,0:T(8,128)S(1)} %multiply_kept.1.keep, f32[256,1024]{1,0:T(8,128)S(1)} %collective-permute-done.15.got), custom_call_target="tpu_custom_call" | custom-call | bytes 4194304 | tf_op jit(solution)/shard_map/code_sums/pallas_call | solution.py:378
  50.5 0.6 %collective-permute-start.17 = (s32[264,128]{1,0:T(8,128)S(1)}, s32[264,128]{1,0:T(8,128)S(1)}, u32[]{:S(2)}, u32[]{:S(2)}) collective-permute-start(s32[264,128]{1,0:T(8,128)S(1)} %get-tuple-element.41), channel_id=1, source_target_pairs={{0,2},{1,3},{2,0},{3,1},{4,6},{5,7},{6,4},{7,5},{8,10},{9,11},{10,... | collective-permute-start | bytes 405512 | tf_op jit(solution)/shard_map/ppermute | solution.py:432
  51.1 0.4 collective-permute-start.18
  51.5 3.1 %collective-permute-done.16.rest_0_ = s32[264,128]{1,0:T(8,128)S(1)} collective-permute-done((s32[264,128]{1,0:T(8,128)S(1)}, s32[264,128]{1,0:T(8,128)S(1)}, u32[]{:S(2)}, u32[]{:S(2)}) %collective-permute-start.16) | collective-permute-done | bytes 135200 | tf_op jit(solution)/shard_map/ppermute | solution.py:432
  54.6 2.4 %collective-permute-done.17.rest_1_ = s32[264,128]{1,0:T(8,128)S(1)} collective-permute-done((s32[264,128]{1,0:T(8,128)S(1)}, s32[264,128]{1,0:T(8,128)S(1)}, u32[]{:S(2)}, u32[]{:S(2)}) %collective-permute-start.17) | collective-permute-done | bytes 135200 | tf_op jit(solution)/shard_map/ppermute | solution.py:432
  57.0 0.0 collective-permute-done.18.rest_2_
  57.0 1.1 %total_sums.1 = f32[64,1024]{1,0:T(8,128)} custom-call(f32[64,1024]{1,0:T(8,128)S(1)} %get-tuple-element.40.mine, s32[264,128]{1,0:T(8,128)S(1)} %collective-permute-done.16.rest_0_, s32[264,128]{1,0:T(8,128)S(1)} %collective-permute-done.17.rest_1_, s32[264,128]{1,0:T(8,128)S(1)} %collective-permute-done.18.rest_2_), custom_call_target="tpu_custom_call" | custom-call | bytes 4194304 | tf_op jit(solution)/shard_map/total_sums/pallas_call | solution.py:415
  (9 shorter events, 0.2 us)
Async XLA Ops:
  1.0 4.2 %collective-permute-start.1 = (bf16[1040,128]{1,0:T(8,128)(2,1)S(1)}, bf16[1040,128]{1,0:T(8,128)(2,1)S(1)}, u32[]{:S(2)}, u32[]{:S(2)}) collective-permute-start(bf16[1040,128]{1,0:T(8,128)(2,1)S(1)} %pack_tiles.1.rest_0_), channel_id=1, source_target_pairs={{0,1},{1,0},{2,3},{3,2},{4,5},{5,4},{6,7},{7,6},{8,9},{9,8},{10,11... | collective-permute-start | bytes 798728 | tf_op jit(solution)/shard_map/ppermute | solution.py:432
  1.5 16.4 %collective-permute-start = (bf16[1040,128]{1,0:T(8,128)(2,1)S(1)}, bf16[1040,128]{1,0:T(8,128)(2,1)S(1)}, u32[]{:S(2)}, u32[]{:S(2)}) collective-permute-start(bf16[1040,128]{1,0:T(8,128)(2,1)S(1)} %pack_tiles.1.rest_0_), channel_id=1, source_target_pairs={{0,16},{8,24},{16,0},{24,8},{1,17},{9,25},{17,1},{25,9},{2,18},{10... | collective-permute-start | bytes 798728 | tf_op jit(solution)/shard_map/ppermute | solution.py:432
  6.4 11.5 %collective-permute-start.2 = (bf16[544,128]{1,0:T(8,128)(2,1)S(1)}, bf16[544,128]{1,0:T(8,128)(2,1)S(1)}, u32[]{:S(2)}, u32[]{:S(2)}) collective-permute-start(bf16[544,128]{1,0:T(8,128)(2,1)S(1)} %get-tuple-element.53), channel_id=1, source_target_pairs={{0,2},{1,3},{2,0},{3,1},{4,6},{5,7},{6,4},{7,5},{8,10},{9,11},{10,... | collective-permute-start | bytes 417800 | tf_op jit(solution)/shard_map/ppermute | solution.py:432
  7.9 9.9 %collective-permute-start.3 = (bf16[544,128]{1,0:T(8,128)(2,1)S(1)}, bf16[544,128]{1,0:T(8,128)(2,1)S(1)}, u32[]{:S(2)}, u32[]{:S(2)}) collective-permute-start(bf16[544,128]{1,0:T(8,128)(2,1)S(1)} %get-tuple-element.52), channel_id=1, source_target_pairs={{0,4},{1,5},{2,6},{3,7},{4,0},{5,1},{6,2},{7,3},{8,12},{9,13},{10,... | collective-permute-start | bytes 417800 | tf_op jit(solution)/shard_map/ppermute | solution.py:432
  9.5 8.4 %collective-permute-start.4 = (bf16[544,128]{1,0:T(8,128)(2,1)S(1)}, bf16[544,128]{1,0:T(8,128)(2,1)S(1)}, u32[]{:S(2)}, u32[]{:S(2)}) collective-permute-start(bf16[544,128]{1,0:T(8,128)(2,1)S(1)} %get-tuple-element.51), channel_id=1, source_target_pairs={{0,6},{1,7},{2,4},{3,5},{4,2},{5,3},{6,0},{7,1},{8,14},{9,15},{10,... | collective-permute-start | bytes 417800 | tf_op jit(solution)/shard_map/ppermute | solution.py:432
  17.9 2.3 %collective-permute-start.6 = (bf16[1040,128]{1,0:T(8,128)(2,1)S(1)}, bf16[1040,128]{1,0:T(8,128)(2,1)S(1)}, u32[]{:S(2)}, u32[]{:S(2)}) collective-permute-start(bf16[1040,128]{1,0:T(8,128)(2,1)S(1)} %collective-permute-done.rest_0_), channel_id=1, source_target_pairs={{0,1},{1,0},{2,3},{3,2},{4,5},{5,4},{6,7},{7,6},{8,9},{9,8},{10,11... | collective-permute-start | bytes 798728 | tf_op jit(solution)/shard_map/ppermute | solution.py:432
  18.0 9.3 %collective-permute-start.5 = (bf16[1040,128]{1,0:T(8,128)(2,1)S(1)}, bf16[1040,128]{1,0:T(8,128)(2,1)S(1)}, u32[]{:S(2)}, u32[]{:S(2)}) collective-permute-start(bf16[1040,128]{1,0:T(8,128)(2,1)S(1)} %collective-permute-done.rest_0_), channel_id=1, source_target_pairs={{0,8},{8,0},{16,24},{24,16},{1,9},{9,1},{17,25},{25,17},{2,10},{10... | collective-permute-start | bytes 798728 | tf_op jit(solution)/shard_map/ppermute | solution.py:432
  18.8 19.9 %collective-permute-start.13 = (bf16[2176,128]{1,0:T(8,128)(2,1)S(1)}, bf16[2176,128]{1,0:T(8,128)(2,1)S(1)}, u32[]{:S(2)}, u32[]{:S(2)}) collective-permute-start(bf16[2176,128]{1,0:T(8,128)(2,1)S(1)} %pad_maximum_fusion), channel_id=1, source_target_pairs={{0,8},{8,0},{16,24},{24,16},{1,9},{9,1},{17,25},{25,17},{2,10},{10... | collective-permute-start | bytes 1671176 | tf_op jit(solution)/shard_map/ppermute | solution.py:432
  21.4 6.0 %collective-permute-start.7 = (bf16[544,128]{1,0:T(8,128)(2,1)S(1)}, bf16[544,128]{1,0:T(8,128)(2,1)S(1)}, u32[]{:S(2)}, u32[]{:S(2)}) collective-permute-start(bf16[544,128]{1,0:T(8,128)(2,1)S(1)} %get-tuple-element.46), channel_id=1, source_target_pairs={{0,2},{1,3},{2,0},{3,1},{4,6},{5,7},{6,4},{7,5},{8,10},{9,11},{10,... | collective-permute-start | bytes 417800 | tf_op jit(solution)/shard_map/ppermute | solution.py:432
  23.0 9.7 %collective-permute-start.11 = (bf16[544,128]{1,0:T(8,128)(2,1)S(1)}, bf16[544,128]{1,0:T(8,128)(2,1)S(1)}, u32[]{:S(2)}, u32[]{:S(2)}) collective-permute-start(bf16[544,128]{1,0:T(8,128)(2,1)S(1)} %get-tuple-element.44), channel_id=1, source_target_pairs={{0,4},{1,5},{2,6},{3,7},{4,0},{5,1},{6,2},{7,3},{8,12},{9,13},{10,... | collective-permute-start | bytes 417800 | tf_op jit(solution)/shard_map/ppermute | solution.py:432
  24.5 11.9 %collective-permute-start.12 = (bf16[544,128]{1,0:T(8,128)(2,1)S(1)}, bf16[544,128]{1,0:T(8,128)(2,1)S(1)}, u32[]{:S(2)}, u32[]{:S(2)}) collective-permute-start(bf16[544,128]{1,0:T(8,128)(2,1)S(1)} %get-tuple-element.43), channel_id=1, source_target_pairs={{0,6},{1,7},{2,4},{3,5},{4,2},{5,3},{6,0},{7,1},{8,14},{9,15},{10,... | collective-permute-start | bytes 417800 | tf_op jit(solution)/shard_map/ppermute | solution.py:432
  28.2 10.0 %collective-permute-start.10 = (bf16[544,128]{1,0:T(8,128)(2,1)S(1)}, bf16[544,128]{1,0:T(8,128)(2,1)S(1)}, u32[]{:S(2)}, u32[]{:S(2)}) collective-permute-start(bf16[544,128]{1,0:T(8,128)(2,1)S(1)} %get-tuple-element.47), channel_id=1, source_target_pairs={{0,6},{1,7},{2,4},{3,5},{4,2},{5,3},{6,0},{7,1},{8,14},{9,15},{10,... | collective-permute-start | bytes 417800 | tf_op jit(solution)/shard_map/ppermute | solution.py:432
  31.4 6.8 %collective-permute-start.8 = (bf16[544,128]{1,0:T(8,128)(2,1)S(1)}, bf16[544,128]{1,0:T(8,128)(2,1)S(1)}, u32[]{:S(2)}, u32[]{:S(2)}) collective-permute-start(bf16[544,128]{1,0:T(8,128)(2,1)S(1)} %get-tuple-element.49), channel_id=1, source_target_pairs={{0,2},{1,3},{2,0},{3,1},{4,6},{5,7},{6,4},{7,5},{8,10},{9,11},{10,... | collective-permute-start | bytes 417800 | tf_op jit(solution)/shard_map/ppermute | solution.py:432
  32.7 5.6 %collective-permute-start.9 = (bf16[544,128]{1,0:T(8,128)(2,1)S(1)}, bf16[544,128]{1,0:T(8,128)(2,1)S(1)}, u32[]{:S(2)}, u32[]{:S(2)}) collective-permute-start(bf16[544,128]{1,0:T(8,128)(2,1)S(1)} %get-tuple-element.48), channel_id=1, source_target_pairs={{0,4},{1,5},{2,6},{3,7},{4,0},{5,1},{6,2},{7,3},{8,12},{9,13},{10,... | collective-permute-start | bytes 417800 | tf_op jit(solution)/shard_map/ppermute | solution.py:432
  38.8 2.0 %collective-permute-start.14 = (bf16[1088,128]{1,0:T(8,128)(2,1)S(1)}, bf16[1088,128]{1,0:T(8,128)(2,1)S(1)}, u32[]{:S(2)}, u32[]{:S(2)}) collective-permute-start(bf16[1088,128]{1,0:T(8,128)(2,1)S(1)} %pad_maximum_fusion.1), channel_id=1, source_target_pairs={{0,1},{1,0},{2,3},{3,2},{4,5},{5,4},{6,7},{7,6},{8,9},{9,8},{10,11... | collective-permute-start | bytes 835592 | tf_op jit(solution)/shard_map/ppermute | solution.py:432
  44.0 2.9 %collective-permute-start.15 = (f32[256,1024]{1,0:T(8,128)S(1)}, f32[256,1024]{1,0:T(8,128)S(1)}, u32[]{:S(2)}, u32[]{:S(2)}) collective-permute-start(f32[256,1024]{1,0:T(8,128)S(1)} %get-tuple-element.39), channel_id=1, source_target_pairs={{0,1},{1,0},{2,3},{3,2},{4,5},{5,4},{6,7},{7,6},{8,9},{9,8},{10,11... | collective-permute-start | bytes 3145736 | tf_op jit(solution)/shard_map/ppermute | solution.py:432
  47.3 7.4 %collective-permute-start.16 = (s32[264,128]{1,0:T(8,128)S(1)}, s32[264,128]{1,0:T(8,128)S(1)}, u32[]{:S(2)}, u32[]{:S(2)}) collective-permute-start(s32[264,128]{1,0:T(8,128)S(1)} %code_sums.3), channel_id=1, source_target_pairs={{0,6},{1,7},{2,4},{3,5},{4,2},{5,3},{6,0},{7,1},{8,14},{9,15},{10,... | collective-permute-start | bytes 405512 | tf_op jit(solution)/shard_map/ppermute | solution.py:432
  50.5 6.6 %collective-permute-start.17 = (s32[264,128]{1,0:T(8,128)S(1)}, s32[264,128]{1,0:T(8,128)S(1)}, u32[]{:S(2)}, u32[]{:S(2)}) collective-permute-start(s32[264,128]{1,0:T(8,128)S(1)} %get-tuple-element.41), channel_id=1, source_target_pairs={{0,2},{1,3},{2,0},{3,1},{4,6},{5,7},{6,4},{7,5},{8,10},{9,11},{10,... | collective-permute-start | bytes 405512 | tf_op jit(solution)/shard_map/ppermute | solution.py:432
  51.1 5.9 %collective-permute-start.18 = (s32[264,128]{1,0:T(8,128)S(1)}, s32[264,128]{1,0:T(8,128)S(1)}, u32[]{:S(2)}, u32[]{:S(2)}) collective-permute-start(s32[264,128]{1,0:T(8,128)S(1)} %get-tuple-element.42), channel_id=1, source_target_pairs={{0,4},{1,5},{2,6},{3,7},{4,0},{5,1},{6,2},{7,3},{8,12},{9,13},{10,... | collective-permute-start | bytes 405512 | tf_op jit(solution)/shard_map/ppermute | solution.py:432

commit v8 on v7

--- a/solution.py
+++ b/solution.py
@@ -411,6 +411,32 @@
         copy.wait()
 
 
+def add_kernel(plan, mine, word, out, square):
+    rows, tile, chunks = plan.owned, plan.tile, chunks_of(plan)
+    square[...] = jnp.zeros(square.shape, jnp.float32)
+    square[:chunks, :] = word[chunks // 2 * rows :, :].astype(jnp.float32)
+    scale = jnp.exp2(square[...].T[:rows, :] - 15.0)
+    for j in range(chunks):
+        cell = slice(j * tile, (j + 1) * tile)
+        at = j % (chunks // 2) * rows
+        part = word[at : at + rows, :]
+        count = (part if j < chunks // 2 else part << 16) >> 16
+        out[:, cell] = mine[:, cell] + count.astype(jnp.float32) * scale[:, j : j + 1]
+
+
+def add_sums(plan, mine, word):
+    return pl.pallas_call(
+        functools.partial(add_kernel, plan),
+        out_shape=pltpu.VMEM(mine.shape, jnp.float32),
+        in_specs=[VMEM] * 2,
+        out_specs=VMEM,
+        scratch_shapes=[pltpu.VMEM((plan.tile, plan.tile), jnp.float32)],
+        compiler_params=pltpu.CompilerParams(vmem_limit_bytes=20 * 1024 * 1024),
+        cost_estimate=cost(plan, 4 * plan.owned * plan.ab * 4),
+        name="add_sums",
+    )(mine, word)
+
+
 def total_sums(plan, mine, words):
     return pl.pallas_call(
         functools.partial(total_kernel, plan),
@@ -469,7 +495,7 @@
     words = [swap(word, "col", 2 * far_part)]
     mine, *coded = code_sums(plan, [0] + near_parts, keep, got)
     words += [swap(word, "col", 2 * m) for m, word in zip(near_parts, coded, strict=True)]
-    return total_sums(plan, mine, words)
+    return total_sums(plan, add_sums(plan, mine, words[0]), words[1:])
 
 
 def solution(mesh):

time: 58.3 us -> 58.2 us (level)
  no operation moved by 1% of the time
where the time goes in v8:
time: 58.2 us; the launch traced here: 58.1 us
  starting transfers between devices  22.4 us (38%)
  Pallas kernels  21.4 us (37%)
  waiting for transfers between devices  13.8 us (24%)
    ppermute x19, starting transfers between devices, swap(): lax.ppermute(x, axis, [(i, i ^ m) for i in range(lax.axis_size(axis))])  22.4 us
    ppermute x19, waiting for transfers between devices, swap(): lax.ppermute(x, axis, [(i, i ^ m) for i in range(lax.axis_size(axis))])  13.8 us
    pallas_call x2, Pallas kernels, place_more(): pl.pallas_call(functools.partial(more_kernel, plan, planes), out_shape=la...  3.86 us
    pallas_call x1, Pallas kernels, stage(): pl.pallas_call(functools.partial(stage_kernel, plan, block), out_shape=pl...  3.5 us
    pallas_call x1, Pallas kernels, send_product(): pl.pallas_call(functools.partial(send_kernel, plan, planes, block), out_s...  3.18 us
    pallas_call x3, Pallas kernels, bucket(): pl.pallas_call(functools.partial(bucket_kernel, plan, count, both), out_s...  3.13 us
    pallas_call x1, Pallas kernels, keep_product(): pl.pallas_call(functools.partial(keep_kernel, plan, block), out_shape=plt...  2.35 us
    pallas_call x1, Pallas kernels, place_early(): pl.pallas_call(functools.partial(early_kernel, plan, planes), out_shape=l...  2.14 us
  transfers between devices with their start and end apart: 19, of which 7 were waited for; matrix products, arithmetic and copies ran while one was open for 0% of the time, Pallas kernels for 27%

profile of v8, /device:TPU:0, one launch (start us, length us, event | category | flops | bytes accessed | tf_op | source)
XLA Modules:
  0.0 58.1 jit_solution(1848991293155231286)
XLA Ops:
  0.0 1.0 %pack_tiles.1.rest_0_ = bf16[1040,128]{1,0:T(8,128)(2,1)S(1)} custom-call(s32[1,64]{1,0:T(1,128)} %ids.1, bf16[1024,128]{1,0:T(8,128)(2,1)} %bitcast.1), custom_call_target="tpu_custom_call" | custom-call | bytes 532480 | tf_op jit(solution)/shard_map/pack_tiles/pallas_call | solution.py:79
  1.0 0.5 collective-permute-start.1
  1.5 3.7 %collective-permute-start = (bf16[1040,128]{1,0:T(8,128)(2,1)S(1)}, bf16[1040,128]{1,0:T(8,128)(2,1)S(1)}, u32[]{:S(2)}, u32[]{:S(2)}) collective-permute-start(bf16[1040,128]{1,0:T(8,128)(2,1)S(1)} %pack_tiles.1.rest_0_), channel_id=1, source_target_pairs={{0,16},{8,24},{16,0},{24,8},{1,17},{9,25},{17,1},{25,9},{2,18},{10... | collective-permute-start | bytes 798728 | tf_op jit(solution)/shard_map/ppermute | solution.py:458
  5.2 0.0 collective-permute-done.1.rest_1_
  5.2 1.2 %bucket_tiles.3 = bf16[2192,128]{1,0:T(8,128)(2,1)S(1)} custom-call(bf16[1040,128]{1,0:T(8,128)(2,1)S(1)} %pack_tiles.1.rest_0_, bf16[1040,128]{1,0:T(8,128)(2,1)S(1)} %collective-permute-done.1.rest_1_), custom_call_target="tpu_custom_call" | custom-call | bytes 2228224 | tf_op jit(solution)/shard_map/bucket_tiles/pallas_call | solution.py:148
  6.4 1.6 %collective-permute-start.2 = (bf16[544,128]{1,0:T(8,128)(2,1)S(1)}, bf16[544,128]{1,0:T(8,128)(2,1)S(1)}, u32[]{:S(2)}, u32[]{:S(2)}) collective-permute-start(bf16[544,128]{1,0:T(8,128)(2,1)S(1)} %get-tuple-element.53), channel_id=1, source_target_pairs={{0,2},{1,3},{2,0},{3,1},{4,6},{5,7},{6,4},{7,5},{8,10},{9,11},{10,... | collective-permute-start | bytes 417800 | tf_op jit(solution)/shard_map/ppermute | solution.py:458
  7.9 1.5 %collective-permute-start.3 = (bf16[544,128]{1,0:T(8,128)(2,1)S(1)}, bf16[544,128]{1,0:T(8,128)(2,1)S(1)}, u32[]{:S(2)}, u32[]{:S(2)}) collective-permute-start(bf16[544,128]{1,0:T(8,128)(2,1)S(1)} %get-tuple-element.52), channel_id=1, source_target_pairs={{0,4},{1,5},{2,6},{3,7},{4,0},{5,1},{6,2},{7,3},{8,12},{9,13},{10,... | collective-permute-start | bytes 417800 | tf_op jit(solution)/shard_map/ppermute | solution.py:458
  9.5 0.5 collective-permute-start.4
  9.9 3.5 %stage_integrals.1.cols = bf16[1024,4096]{1,0:T(8,128)(2,1)S(1)} custom-call(bf16[1024,4096]{1,0:T(8,128)(2,1)} %integrals.1), custom_call_target="tpu_custom_call" | custom-call | bytes 16777216 | tf_op jit(solution)/shard_map/stage_integrals/pallas_call | solution.py:235
  13.4 4.4 %collective-permute-done.rest_0_ = bf16[1040,128]{1,0:T(8,128)(2,1)S(1)} collective-permute-done((bf16[1040,128]{1,0:T(8,128)(2,1)S(1)}, bf16[1040,128]{1,0:T(8,128)(2,1)S(1)}, u32[]{:S(2)}, u32[]{:S(2)}) %collective-permute-start) | collective-permute-done | bytes 266272 | tf_op jit(solution)/shard_map/ppermute | solution.py:458
  17.9 0.0 collective-permute-done.2.rest_1_
  17.9 0.0 collective-permute-done.3.rest_2_
  17.9 0.0 collective-permute-done.4.rest_3_
  17.9 0.1 collective-permute-start.6
  18.0 0.8 %collective-permute-start.5 = (bf16[1040,128]{1,0:T(8,128)(2,1)S(1)}, bf16[1040,128]{1,0:T(8,128)(2,1)S(1)}, u32[]{:S(2)}, u32[]{:S(2)}) collective-permute-start(bf16[1040,128]{1,0:T(8,128)(2,1)S(1)} %collective-permute-done.rest_0_), channel_id=1, source_target_pairs={{0,8},{8,0},{16,24},{24,16},{1,9},{9,1},{17,25},{25,17},{2,10},{10... | collective-permute-start | bytes 798728 | tf_op jit(solution)/shard_map/ppermute | solution.py:458
  18.8 1.3 %collective-permute-start.13 = (bf16[2176,128]{1,0:T(8,128)(2,1)S(1)}, bf16[2176,128]{1,0:T(8,128)(2,1)S(1)}, u32[]{:S(2)}, u32[]{:S(2)}) collective-permute-start(bf16[2176,128]{1,0:T(8,128)(2,1)S(1)} %pad_maximum_fusion), channel_id=1, source_target_pairs={{0,8},{8,0},{16,24},{24,16},{1,9},{9,1},{17,25},{25,17},{2,10},{10... | collective-permute-start | bytes 1671176 | tf_op jit(solution)/shard_map/ppermute | solution.py:458
  20.2 0.0 collective-permute-done.6.rest_1_
  20.2 1.2 %bucket_tiles.4 = bf16[2192,128]{1,0:T(8,128)(2,1)S(1)} custom-call(bf16[1040,128]{1,0:T(8,128)(2,1)S(1)} %collective-permute-done.rest_0_, bf16[1040,128]{1,0:T(8,128)(2,1)S(1)} %collective-permute-done.6.rest_1_), custom_call_target="tpu_custom_call" | custom-call | bytes 2228224 | tf_op jit(solution)/shard_map/bucket_tiles/pallas_call | solution.py:148
  21.4 1.6 %collective-permute-start.7 = (bf16[544,128]{1,0:T(8,128)(2,1)S(1)}, bf16[544,128]{1,0:T(8,128)(2,1)S(1)}, u32[]{:S(2)}, u32[]{:S(2)}) collective-permute-start(bf16[544,128]{1,0:T(8,128)(2,1)S(1)} %get-tuple-element.46), channel_id=1, source_target_pairs={{0,2},{1,3},{2,0},{3,1},{4,6},{5,7},{6,4},{7,5},{8,10},{9,11},{10,... | collective-permute-start | bytes 417800 | tf_op jit(solution)/shard_map/ppermute | solution.py:458
  23.0 1.5 %collective-permute-start.11 = (bf16[544,128]{1,0:T(8,128)(2,1)S(1)}, bf16[544,128]{1,0:T(8,128)(2,1)S(1)}, u32[]{:S(2)}, u32[]{:S(2)}) collective-permute-start(bf16[544,128]{1,0:T(8,128)(2,1)S(1)} %get-tuple-element.44), channel_id=1, source_target_pairs={{0,4},{1,5},{2,6},{3,7},{4,0},{5,1},{6,2},{7,3},{8,12},{9,13},{10,... | collective-permute-start | bytes 417800 | tf_op jit(solution)/shard_map/ppermute | solution.py:458
  24.5 0.4 collective-permute-start.12
  24.9 2.3 %collective-permute-done.5.rest_0_ = bf16[1040,128]{1,0:T(8,128)(2,1)S(1)} collective-permute-done((bf16[1040,128]{1,0:T(8,128)(2,1)S(1)}, bf16[1040,128]{1,0:T(8,128)(2,1)S(1)}, u32[]{:S(2)}, u32[]{:S(2)}) %collective-permute-start.5) | collective-permute-done | bytes 266272 | tf_op jit(solution)/shard_map/ppermute | solution.py:458
  27.2 0.1 collective-permute-done.7.rest_1_
  27.4 0.8 %bucket_tiles.5 = bf16[2192,128]{1,0:T(8,128)(2,1)S(1)} custom-call(bf16[1040,128]{1,0:T(8,128)(2,1)S(1)} %collective-permute-done.5.rest_0_), custom_call_target="tpu_custom_call" | custom-call | bytes 2228224 | tf_op jit(solution)/shard_map/bucket_tiles/pallas_call | solution.py:148
  28.2 3.2 %collective-permute-start.10 = (bf16[544,128]{1,0:T(8,128)(2,1)S(1)}, bf16[544,128]{1,0:T(8,128)(2,1)S(1)}, u32[]{:S(2)}, u32[]{:S(2)}) collective-permute-start(bf16[544,128]{1,0:T(8,128)(2,1)S(1)} %get-tuple-element.47), channel_id=1, source_target_pairs={{0,6},{1,7},{2,4},{3,5},{4,2},{5,3},{6,0},{7,1},{8,14},{9,15},{10,... | collective-permute-start | bytes 417800 | tf_op jit(solution)/shard_map/ppermute | solution.py:458
  31.4 0.0 collective-permute-start.8
  31.4 1.3 %collective-permute-done.11.rest_2_ = bf16[544,128]{1,0:T(8,128)(2,1)S(1)} collective-permute-done((bf16[544,128]{1,0:T(8,128)(2,1)S(1)}, bf16[544,128]{1,0:T(8,128)(2,1)S(1)}, u32[]{:S(2)}, u32[]{:S(2)}) %collective-permute-start.11) | collective-permute-done | bytes 139296 | tf_op jit(solution)/shard_map/ppermute | solution.py:458
  32.7 1.5 %collective-permute-start.9 = (bf16[544,128]{1,0:T(8,128)(2,1)S(1)}, bf16[544,128]{1,0:T(8,128)(2,1)S(1)}, u32[]{:S(2)}, u32[]{:S(2)}) collective-permute-start(bf16[544,128]{1,0:T(8,128)(2,1)S(1)} %get-tuple-element.48), channel_id=1, source_target_pairs={{0,4},{1,5},{2,6},{3,7},{4,0},{5,1},{6,2},{7,3},{8,12},{9,13},{10,... | collective-permute-start | bytes 417800 | tf_op jit(solution)/shard_map/ppermute | solution.py:458
  34.2 2.1 %place_early.1._ = bf16[528,4096]{1,0:T(8,128)(2,1)S(1)} custom-call(bf16[544,128]{1,0:T(8,128)(2,1)S(1)} %get-tuple-element.26.rest_0_, bf16[544,128]{1,0:T(8,128)(2,1)S(1)} %collective-permute-done.2.rest_1_, bf16[544,128]{1,0:T(8,128)(2,1)S(1)} %collective-permute-done.3.rest_2_, bf16[544,128]{1,0:T(8,128)(2,1)S(1)} %collective-permute-done.4.rest_3_), custom_call_target="tpu_custom_call" | custom-call | bytes 4194304 | tf_op jit(solution)/shard_map/place_early/pallas_call | solution.py:256
  36.4 0.0 collective-permute-done.12.rest_3_
  36.4 1.9 %place_more.2._ = bf16[528,4096]{1,0:T(8,128)(2,1)S(1)} custom-call(bf16[528,4096]{1,0:T(8,128)(2,1)S(1)} %place_early.1._, bf16[544,128]{1,0:T(8,128)(2,1)S(1)} %get-tuple-element.45.rest_0_, bf16[544,128]{1,0:T(8,128)(2,1)S(1)} %collective-permute-done.7.rest_1_, ...), custom_call_target="tpu_custom_call", output_to_operand_aliasing={{}: (0, {})} | custom-call | bytes 4194304 | tf_op jit(solution)/shard_map/place_more/pallas_call | solution.py:276
  38.3 0.0 collective-permute-done.10.rest_4_
  38.3 0.0 collective-permute-done.8.rest_2_
  38.3 0.0 collective-permute-done.9.rest_3_
  38.3 0.4 collective-permute-done.13.rest_0_
  38.8 0.1 collective-permute-start.14
  38.9 2.0 %place_more.3._ = bf16[528,4096]{1,0:T(8,128)(2,1)S(1)} custom-call(bf16[528,4096]{1,0:T(8,128)(2,1)S(1)} %place_more.2._, bf16[2176,128]{1,0:T(8,128)(2,1)S(1)} %collective-permute-done.13.rest_0_, bf16[544,128]{1,0:T(8,128)(2,1)S(1)} %get-tuple-element.33.rest_1_, ...), custom_call_target="tpu_custom_call", output_to_operand_aliasing={{}: (0, {})} | custom-call | bytes 4194304 | tf_op jit(solution)/shard_map/place_more/pallas_call | solution.py:276
  40.8 0.0 collective-permute-done.14.rest_0_
  40.8 3.2 %place_and_multiply.1 = (bf16[528,4096]{1,0:T(8,128)(2,1)S(1)}, f32[256,1024]{1,0:T(8,128)S(1)}) custom-call(bf16[528,4096]{1,0:T(8,128)(2,1)S(1)} %place_more.3._, bf16[1024,4096]{1,0:T(8,128)(2,1)S(1)} %stage_integrals.1.cols, bf16[1088,128]{1,0:T(8,128)(2,1)S(1)} %collective-permute-done.14.rest_0_), custom_call_target="tpu_custom_call", output_to_operand_aliasing={{0}: (0, {})} | custom-call | flops 4294967296 | bytes 16777216 | tf_op jit(solution)/shard_map/place_and_multiply/pallas_call | solution.py:299
  44.0 0.5 collective-permute-start.15
  44.5 2.4 %multiply_kept.1.keep = f32[256,1024]{1,0:T(8,128)S(1)} custom-call(bf16[528,4096]{1,0:T(8,128)(2,1)S(1)} %get-tuple-element.38.lam, bf16[1024,4096]{1,0:T(8,128)(2,1)S(1)} %stage_integrals.1.cols), custom_call_target="tpu_custom_call" | custom-call | flops 2147483648 | bytes 10485760 | tf_op jit(solution)/shard_map/multiply_kept/pallas_call | solution.py:328
  46.9 0.0 collective-permute-done.15.got
  46.9 0.3 code_sums.3
  47.3 2.6 %collective-permute-start.16 = (s32[264,128]{1,0:T(8,128)S(1)}, s32[264,128]{1,0:T(8,128)S(1)}, u32[]{:S(2)}, u32[]{:S(2)}) collective-permute-start(s32[264,128]{1,0:T(8,128)S(1)} %code_sums.3), channel_id=1, source_target_pairs={{0,6},{1,7},{2,4},{3,5},{4,2},{5,3},{6,0},{7,1},{8,14},{9,15},{10,... | collective-permute-start | bytes 405512 | tf_op jit(solution)/shard_map/ppermute | solution.py:458
  49.8 0.6 %code_sums.2 = (f32[64,1024]{1,0:T(8,128)S(1)}, s32[264,128]{1,0:T(8,128)S(1)}, s32[264,128]{1,0:T(8,128)S(1)}) custom-call(f32[256,1024]{1,0:T(8,128)S(1)} %multiply_kept.1.keep, f32[256,1024]{1,0:T(8,128)S(1)} %collective-permute-done.15.got), custom_call_target="tpu_custom_call" | custom-call | bytes 4194304 | tf_op jit(solution)/shard_map/code_sums/pallas_call | solution.py:378
  50.5 0.6 %collective-permute-start.17 = (s32[264,128]{1,0:T(8,128)S(1)}, s32[264,128]{1,0:T(8,128)S(1)}, u32[]{:S(2)}, u32[]{:S(2)}) collective-permute-start(s32[264,128]{1,0:T(8,128)S(1)} %get-tuple-element.41), channel_id=1, source_target_pairs={{0,2},{1,3},{2,0},{3,1},{4,6},{5,7},{6,4},{7,5},{8,10},{9,11},{10,... | collective-permute-start | bytes 405512 | tf_op jit(solution)/shard_map/ppermute | solution.py:458
  51.1 0.4 collective-permute-start.18
  51.5 3.1 %collective-permute-done.16.word = s32[264,128]{1,0:T(8,128)S(1)} collective-permute-done((s32[264,128]{1,0:T(8,128)S(1)}, s32[264,128]{1,0:T(8,128)S(1)}, u32[]{:S(2)}, u32[]{:S(2)}) %collective-permute-start.16) | collective-permute-done | bytes 135200 | tf_op jit(solution)/shard_map/ppermute | solution.py:458
  54.6 0.2 add_sums.1.mine
  54.9 2.2 %collective-permute-done.17.rest_0_ = s32[264,128]{1,0:T(8,128)S(1)} collective-permute-done((s32[264,128]{1,0:T(8,128)S(1)}, s32[264,128]{1,0:T(8,128)S(1)}, u32[]{:S(2)}, u32[]{:S(2)}) %collective-permute-start.17) | collective-permute-done | bytes 135200 | tf_op jit(solution)/shard_map/ppermute | solution.py:458
  57.0 0.0 collective-permute-done.18.rest_1_
  57.1 1.0 %total_sums.1 = f32[64,1024]{1,0:T(8,128)} custom-call(f32[64,1024]{1,0:T(8,128)S(1)} %add_sums.1.mine, s32[264,128]{1,0:T(8,128)S(1)} %collective-permute-done.17.rest_0_, s32[264,128]{1,0:T(8,128)S(1)} %collective-permute-done.18.rest_1_), custom_call_target="tpu_custom_call" | custom-call | bytes 4194304 | tf_op jit(solution)/shard_map/total_sums/pallas_call | solution.py:441
  (9 shorter events, 0.2 us)
Async XLA Ops:
  1.0 4.2 %collective-permute-start.1 = (bf16[1040,128]{1,0:T(8,128)(2,1)S(1)}, bf16[1040,128]{1,0:T(8,128)(2,1)S(1)}, u32[]{:S(2)}, u32[]{:S(2)}) collective-permute-start(bf16[1040,128]{1,0:T(8,128)(2,1)S(1)} %pack_tiles.1.rest_0_), channel_id=1, source_target_pairs={{0,1},{1,0},{2,3},{3,2},{4,5},{5,4},{6,7},{7,6},{8,9},{9,8},{10,11... | collective-permute-start | bytes 798728 | tf_op jit(solution)/shard_map/ppermute | solution.py:458
  1.5 16.4 %collective-permute-start = (bf16[1040,128]{1,0:T(8,128)(2,1)S(1)}, bf16[1040,128]{1,0:T(8,128)(2,1)S(1)}, u32[]{:S(2)}, u32[]{:S(2)}) collective-permute-start(bf16[1040,128]{1,0:T(8,128)(2,1)S(1)} %pack_tiles.1.rest_0_), channel_id=1, source_target_pairs={{0,16},{8,24},{16,0},{24,8},{1,17},{9,25},{17,1},{25,9},{2,18},{10... | collective-permute-start | bytes 798728 | tf_op jit(solution)/shard_map/ppermute | solution.py:458
  6.4 11.5 %collective-permute-start.2 = (bf16[544,128]{1,0:T(8,128)(2,1)S(1)}, bf16[544,128]{1,0:T(8,128)(2,1)S(1)}, u32[]{:S(2)}, u32[]{:S(2)}) collective-permute-start(bf16[544,128]{1,0:T(8,128)(2,1)S(1)} %get-tuple-element.53), channel_id=1, source_target_pairs={{0,2},{1,3},{2,0},{3,1},{4,6},{5,7},{6,4},{7,5},{8,10},{9,11},{10,... | collective-permute-start | bytes 417800 | tf_op jit(solution)/shard_map/ppermute | solution.py:458
  7.9 9.9 %collective-permute-start.3 = (bf16[544,128]{1,0:T(8,128)(2,1)S(1)}, bf16[544,128]{1,0:T(8,128)(2,1)S(1)}, u32[]{:S(2)}, u32[]{:S(2)}) collective-permute-start(bf16[544,128]{1,0:T(8,128)(2,1)S(1)} %get-tuple-element.52), channel_id=1, source_target_pairs={{0,4},{1,5},{2,6},{3,7},{4,0},{5,1},{6,2},{7,3},{8,12},{9,13},{10,... | collective-permute-start | bytes 417800 | tf_op jit(solution)/shard_map/ppermute | solution.py:458
  9.5 8.4 %collective-permute-start.4 = (bf16[544,128]{1,0:T(8,128)(2,1)S(1)}, bf16[544,128]{1,0:T(8,128)(2,1)S(1)}, u32[]{:S(2)}, u32[]{:S(2)}) collective-permute-start(bf16[544,128]{1,0:T(8,128)(2,1)S(1)} %get-tuple-element.51), channel_id=1, source_target_pairs={{0,6},{1,7},{2,4},{3,5},{4,2},{5,3},{6,0},{7,1},{8,14},{9,15},{10,... | collective-permute-start | bytes 417800 | tf_op jit(solution)/shard_map/ppermute | solution.py:458
  17.9 2.3 %collective-permute-start.6 = (bf16[1040,128]{1,0:T(8,128)(2,1)S(1)}, bf16[1040,128]{1,0:T(8,128)(2,1)S(1)}, u32[]{:S(2)}, u32[]{:S(2)}) collective-permute-start(bf16[1040,128]{1,0:T(8,128)(2,1)S(1)} %collective-permute-done.rest_0_), channel_id=1, source_target_pairs={{0,1},{1,0},{2,3},{3,2},{4,5},{5,4},{6,7},{7,6},{8,9},{9,8},{10,11... | collective-permute-start | bytes 798728 | tf_op jit(solution)/shard_map/ppermute | solution.py:458
  18.0 9.3 %collective-permute-start.5 = (bf16[1040,128]{1,0:T(8,128)(2,1)S(1)}, bf16[1040,128]{1,0:T(8,128)(2,1)S(1)}, u32[]{:S(2)}, u32[]{:S(2)}) collective-permute-start(bf16[1040,128]{1,0:T(8,128)(2,1)S(1)} %collective-permute-done.rest_0_), channel_id=1, source_target_pairs={{0,8},{8,0},{16,24},{24,16},{1,9},{9,1},{17,25},{25,17},{2,10},{10... | collective-permute-start | bytes 798728 | tf_op jit(solution)/shard_map/ppermute | solution.py:458
  18.8 19.9 %collective-permute-start.13 = (bf16[2176,128]{1,0:T(8,128)(2,1)S(1)}, bf16[2176,128]{1,0:T(8,128)(2,1)S(1)}, u32[]{:S(2)}, u32[]{:S(2)}) collective-permute-start(bf16[2176,128]{1,0:T(8,128)(2,1)S(1)} %pad_maximum_fusion), channel_id=1, source_target_pairs={{0,8},{8,0},{16,24},{24,16},{1,9},{9,1},{17,25},{25,17},{2,10},{10... | collective-permute-start | bytes 1671176 | tf_op jit(solution)/shard_map/ppermute | solution.py:458
  21.4 6.0 %collective-permute-start.7 = (bf16[544,128]{1,0:T(8,128)(2,1)S(1)}, bf16[544,128]{1,0:T(8,128)(2,1)S(1)}, u32[]{:S(2)}, u32[]{:S(2)}) collective-permute-start(bf16[544,128]{1,0:T(8,128)(2,1)S(1)} %get-tuple-element.46), channel_id=1, source_target_pairs={{0,2},{1,3},{2,0},{3,1},{4,6},{5,7},{6,4},{7,5},{8,10},{9,11},{10,... | collective-permute-start | bytes 417800 | tf_op jit(solution)/shard_map/ppermute | solution.py:458
  23.0 9.7 %collective-permute-start.11 = (bf16[544,128]{1,0:T(8,128)(2,1)S(1)}, bf16[544,128]{1,0:T(8,128)(2,1)S(1)}, u32[]{:S(2)}, u32[]{:S(2)}) collective-permute-start(bf16[544,128]{1,0:T(8,128)(2,1)S(1)} %get-tuple-element.44), channel_id=1, source_target_pairs={{0,4},{1,5},{2,6},{3,7},{4,0},{5,1},{6,2},{7,3},{8,12},{9,13},{10,... | collective-permute-start | bytes 417800 | tf_op jit(solution)/shard_map/ppermute | solution.py:458
  24.5 11.9 %collective-permute-start.12 = (bf16[544,128]{1,0:T(8,128)(2,1)S(1)}, bf16[544,128]{1,0:T(8,128)(2,1)S(1)}, u32[]{:S(2)}, u32[]{:S(2)}) collective-permute-start(bf16[544,128]{1,0:T(8,128)(2,1)S(1)} %get-tuple-element.43), channel_id=1, source_target_pairs={{0,6},{1,7},{2,4},{3,5},{4,2},{5,3},{6,0},{7,1},{8,14},{9,15},{10,... | collective-permute-start | bytes 417800 | tf_op jit(solution)/shard_map/ppermute | solution.py:458
  28.2 10.0 %collective-permute-start.10 = (bf16[544,128]{1,0:T(8,128)(2,1)S(1)}, bf16[544,128]{1,0:T(8,128)(2,1)S(1)}, u32[]{:S(2)}, u32[]{:S(2)}) collective-permute-start(bf16[544,128]{1,0:T(8,128)(2,1)S(1)} %get-tuple-element.47), channel_id=1, source_target_pairs={{0,6},{1,7},{2,4},{3,5},{4,2},{5,3},{6,0},{7,1},{8,14},{9,15},{10,... | collective-permute-start | bytes 417800 | tf_op jit(solution)/shard_map/ppermute | solution.py:458
  31.4 6.9 %collective-permute-start.8 = (bf16[544,128]{1,0:T(8,128)(2,1)S(1)}, bf16[544,128]{1,0:T(8,128)(2,1)S(1)}, u32[]{:S(2)}, u32[]{:S(2)}) collective-permute-start(bf16[544,128]{1,0:T(8,128)(2,1)S(1)} %get-tuple-element.49), channel_id=1, source_target_pairs={{0,2},{1,3},{2,0},{3,1},{4,6},{5,7},{6,4},{7,5},{8,10},{9,11},{10,... | collective-permute-start | bytes 417800 | tf_op jit(solution)/shard_map/ppermute | solution.py:458
  32.7 5.6 %collective-permute-start.9 = (bf16[544,128]{1,0:T(8,128)(2,1)S(1)}, bf16[544,128]{1,0:T(8,128)(2,1)S(1)}, u32[]{:S(2)}, u32[]{:S(2)}) collective-permute-start(bf16[544,128]{1,0:T(8,128)(2,1)S(1)} %get-tuple-element.48), channel_id=1, source_target_pairs={{0,4},{1,5},{2,6},{3,7},{4,0},{5,1},{6,2},{7,3},{8,12},{9,13},{10,... | collective-permute-start | bytes 417800 | tf_op jit(solution)/shard_map/ppermute | solution.py:458
  38.8 2.0 %collective-permute-start.14 = (bf16[1088,128]{1,0:T(8,128)(2,1)S(1)}, bf16[1088,128]{1,0:T(8,128)(2,1)S(1)}, u32[]{:S(2)}, u32[]{:S(2)}) collective-permute-start(bf16[1088,128]{1,0:T(8,128)(2,1)S(1)} %pad_maximum_fusion.1), channel_id=1, source_target_pairs={{0,1},{1,0},{2,3},{3,2},{4,5},{5,4},{6,7},{7,6},{8,9},{9,8},{10,11... | collective-permute-start | bytes 835592 | tf_op jit(solution)/shard_map/ppermute | solution.py:458
  44.0 2.9 %collective-permute-start.15 = (f32[256,1024]{1,0:T(8,128)S(1)}, f32[256,1024]{1,0:T(8,128)S(1)}, u32[]{:S(2)}, u32[]{:S(2)}) collective-permute-start(f32[256,1024]{1,0:T(8,128)S(1)} %get-tuple-element.39), channel_id=1, source_target_pairs={{0,1},{1,0},{2,3},{3,2},{4,5},{5,4},{6,7},{7,6},{8,9},{9,8},{10,11... | collective-permute-start | bytes 3145736 | tf_op jit(solution)/shard_map/ppermute | solution.py:458
  47.3 7.4 %collective-permute-start.16 = (s32[264,128]{1,0:T(8,128)S(1)}, s32[264,128]{1,0:T(8,128)S(1)}, u32[]{:S(2)}, u32[]{:S(2)}) collective-permute-start(s32[264,128]{1,0:T(8,128)S(1)} %code_sums.3), channel_id=1, source_target_pairs={{0,6},{1,7},{2,4},{3,5},{4,2},{5,3},{6,0},{7,1},{8,14},{9,15},{10,... | collective-permute-start | bytes 405512 | tf_op jit(solution)/shard_map/ppermute | solution.py:458
  50.5 6.6 %collective-permute-start.17 = (s32[264,128]{1,0:T(8,128)S(1)}, s32[264,128]{1,0:T(8,128)S(1)}, u32[]{:S(2)}, u32[]{:S(2)}) collective-permute-start(s32[264,128]{1,0:T(8,128)S(1)} %get-tuple-element.41), channel_id=1, source_target_pairs={{0,2},{1,3},{2,0},{3,1},{4,6},{5,7},{6,4},{7,5},{8,10},{9,11},{10,... | collective-permute-start | bytes 405512 | tf_op jit(solution)/shard_map/ppermute | solution.py:458
  51.1 5.9 %collective-permute-start.18 = (s32[264,128]{1,0:T(8,128)S(1)}, s32[264,128]{1,0:T(8,128)S(1)}, u32[]{:S(2)}, u32[]{:S(2)}) collective-permute-start(s32[264,128]{1,0:T(8,128)S(1)} %get-tuple-element.42), channel_id=1, source_target_pairs={{0,4},{1,5},{2,6},{3,7},{4,0},{5,1},{6,2},{7,3},{8,12},{9,13},{10,... | collective-permute-start | bytes 405512 | tf_op jit(solution)/shard_map/ppermute | solution.py:458
